TPU v7x, 32 devices: a whole 2x2x4 slice. The times are simulated.
32 devices in a mesh: dp: 4 (over z), fsdp: 8 (over y, x, core).
Axes of the slice: x: 2, y: 2, z: 4, core: 2. Of those that a mesh axis runs over, the one named last changes fastest.
Arguments:
- txt_tokens: bfloat16 [32, 8, 3072], P(('dp', 'fsdp')), may hold values from -6 to 6
- concept_table: bfloat16 [1024, 3072], P('dp'), may hold values from -6 to 6
- concept_ids: int32 [32], P(('dp', 'fsdp')), may hold values from 0 to 1023
- positions: int32 [32], P(('dp', 'fsdp')), may hold values from 0 to 7
- timesteps: int32 [32], P(('dp', 'fsdp')), may hold values from 0 to 63
- counts: int32 [1024], P('dp'), may hold values from 1 to 16
- mod_table: bfloat16 [64, 2, 3072], P(None, None, 'fsdp'), may hold values from -1.5 to 1.5
- kv_weight: bfloat16 [3072, 3072], P('fsdp'), may hold values from -0.109375 to 0.109375
- kv_bias: float32 [3072], replicated, may hold values from -3 to 3
- key_gain: float32 [128], replicated, may hold values from 0.5 to 1.5
- img_query: bfloat16 [32, 192, 1536], P(('dp', 'fsdp')), may hold values from -256 to 256
- img_key: bfloat16 [32, 192, 1536], P(('dp', 'fsdp')), may hold values from -6 to 6
- img_value: bfloat16 [32, 192, 1536], P(('dp', 'fsdp')), may hold values from -6 to 6
- out_grad: bfloat16 [32, 192, 1536], P(('dp', 'fsdp')), may hold values from -6 to 6
Outputs:
- table_grad: float32 [1024, 3072], P('dp', 'fsdp')
Inputs may be any that keep to these rules, and one draw needn't show every extreme that they name: `concept_ids`: concept of each sample, some concepts far more common than others.
All inputs are finite; a program needn't handle non-finite values.
Results may differ from a plain program's by a relative error of at most 0.0083.
Values may be sent and summed in bfloat16 or wider, within the bound.
No kernel may reach another device: no remote copies, remote signals or barrier semaphores. Data moves between devices by JAX's collectives and lax.ppermute only.
A program may use at most 64 MiB of HBM per device.

v0:
```python
import jax
import jax.numpy as jnp
from jax import lax
from jax.sharding import PartitionSpec as P

EPSILON = 1e-06


def layer_norm(values):
    centre = jnp.mean(values, -1, keepdims=True)
    spread = jnp.mean((values - centre) ** 2, -1, keepdims=True)
    inverse = lax.rsqrt(spread + EPSILON)
    return ((values - centre) * inverse, inverse[..., 0])


def shards(
    txt_tokens,
    concept_table,
    concept_ids,
    positions,
    timesteps,
    counts,
    mod_table,
    kv_weight,
    kv_bias,
    key_gain,
    img_query,
    img_key,
    img_value,
    out_grad,
):
    highest = lax.Precision.HIGHEST
    fsdp_size = lax.axis_size("fsdp")
    column = lax.axis_index("fsdp")
    tok_len = txt_tokens.shape[1]
    model_width = txt_tokens.shape[2]
    slice_width = kv_weight.shape[0]
    kv_width = kv_weight.shape[1]
    head_width = kv_width // 2
    head_dim = key_gain.shape[0]
    head_count = head_width // head_dim
    img_len = img_query.shape[1]
    conc_dev = concept_table.shape[0]
    bucket_count = mod_table.shape[0]
    root_dh = jnp.sqrt(jnp.float32(head_dim))
    table_hat, table_rstd = layer_norm(concept_table.astype(jnp.float32))
    table_part = lax.dynamic_slice_in_dim(
        table_hat.astype(jnp.bfloat16), column * slice_width, slice_width, 1
    )
    table_all = lax.all_gather(table_part, "dp", axis=0, tiled=True)
    own_hat = layer_norm(txt_tokens[0].astype(jnp.float32))[0].astype(jnp.bfloat16)
    labels = jnp.stack([concept_ids[0], positions[0], timesteps[0]])
    label_tile = jnp.tile(labels[None, :], (1, fsdp_size))
    token_cols, label_cols = (
        lax.all_to_all(own_hat, "fsdp", split_axis=1, concat_axis=0, tiled=True),
        lax.all_to_all(label_tile, "fsdp", split_axis=1, concat_axis=0, tiled=True),
    )
    group_ids = label_cols[:, 0]
    group_pos = label_cols[:, 1]
    group_time = label_cols[:, 2]
    concept_cols = jnp.take(table_all, group_ids, axis=0)
    token_cols = token_cols.reshape(fsdp_size, tok_len, slice_width)
    is_place = jnp.arange(tok_len, dtype=jnp.int32)[None, :] == group_pos[:, None]
    token_cols = jnp.where(is_place[:, :, None], concept_cols[:, None, :], token_cols)
    pick_time = (jnp.arange(bucket_count, dtype=jnp.int32)[None, :] == group_time[:, None]).astype(
        jnp.bfloat16
    )
    modulation = jnp.dot(
        pick_time,
        mod_table.reshape(bucket_count, 2 * slice_width),
        preferred_element_type=jnp.float32,
    )
    modulation = modulation.reshape(fsdp_size, 2, slice_width)
    shift_cols = modulation[:, 0]
    scale_cols = 1.0 + modulation[:, 1]
    modulated = (
        scale_cols[:, None, :] * token_cols.astype(jnp.float32) + shift_cols[:, None, :]
    ).astype(jnp.bfloat16)
    kv_terms = jnp.dot(
        modulated.reshape(fsdp_size * tok_len, slice_width),
        kv_weight,
        preferred_element_type=jnp.float32,
    )
    kv_terms = kv_terms.reshape(fsdp_size, tok_len, kv_width)
    weight_f = kv_weight.astype(jnp.float32)
    concept_f = concept_cols.astype(jnp.float32)
    side_rows = jnp.stack([scale_cols, scale_cols * concept_f], 1).reshape(
        fsdp_size * 2, slice_width
    )
    side_terms = jnp.dot(side_rows, weight_f, precision=highest).reshape(fsdp_size, 2, kv_width)
    all_terms = jnp.concatenate([kv_terms, side_terms], 1)
    row_block = all_terms.shape[1]
    all_terms = all_terms.reshape(fsdp_size * row_block, kv_width)
    own_rows = lax.psum_scatter(all_terms, "fsdp", scatter_dimension=0, tiled=True)
    kv_rows = own_rows[:tok_len] + kv_bias
    pos_pick = (jnp.arange(tok_len, dtype=jnp.int32) == positions[0]).astype(jnp.float32)
    key_raw = kv_rows[:, :head_width].reshape(tok_len, head_count, head_dim)
    key_inv = lax.rsqrt(jnp.mean(key_raw * key_raw, -1) + EPSILON)
    key_norm = (
        (key_raw * key_inv[..., None] * key_gain).astype(jnp.bfloat16).reshape(tok_len, head_width)
    )
    val_txt = kv_rows[:, head_width:].astype(jnp.bfloat16)
    keys_all = jnp.concatenate([key_norm, img_key[0]], 0).reshape(
        tok_len + img_len, head_count, head_dim
    )
    vals_all = jnp.concatenate([val_txt, img_value[0]], 0).reshape(
        tok_len + img_len, head_count, head_dim
    )
    queries = img_query[0].reshape(img_len, head_count, head_dim)
    scores = (
        jnp.einsum("qhd,khd->hqk", queries, keys_all, preferred_element_type=jnp.float32) / root_dh
    )
    row_top = jnp.max(scores, -1, keepdims=True)
    raised = jnp.exp(scores - row_top)
    prob_full = raised / jnp.sum(raised, -1, keepdims=True)
    prob_low = prob_full.astype(jnp.bfloat16)
    attended = jnp.einsum("hqk,khd->qhd", prob_low, vals_all, preferred_element_type=jnp.float32)
    grad_f = out_grad[0].reshape(img_len, head_count, head_dim).astype(jnp.float32)
    row_delta = jnp.einsum("qhd,qhd->hq", grad_f, attended)
    prob_pos = jnp.einsum("hqk,k->hq", prob_full[:, :, :tok_len], pos_pick, precision=highest)
    val_local = val_txt.reshape(tok_len, head_count, head_dim).astype(jnp.float32)
    val_pos = jnp.einsum("k,khd->hd", pos_pick, val_local, precision=highest)
    grad_prob = jnp.einsum("qhd,hd->hq", grad_f, val_pos, precision=highest)
    grad_score = prob_pos * (grad_prob - row_delta)
    grad_val = jnp.einsum("hq,qhd->hd", prob_pos, grad_f, precision=highest)
    grad_key = (
        jnp.einsum("hq,qhd->hd", grad_score, queries.astype(jnp.float32), precision=highest)
        / root_dh
    )
    raw_pos = jnp.einsum("k,khd->hd", pos_pick, key_raw, precision=highest)
    inv_pos = jnp.einsum("k,kh->h", pos_pick, key_inv, precision=highest)
    normed_key = raw_pos * inv_pos[:, None]
    grad_norm = grad_key * key_gain
    grad_raw = inv_pos[:, None] * (
        grad_norm - normed_key * jnp.mean(grad_norm * normed_key, -1, keepdims=True)
    )
    grad_kv = jnp.concatenate([grad_raw.reshape(head_width), grad_val.reshape(head_width)])[None, :]
    side_mean = (
        jnp.stack(
            [
                jnp.dot(grad_kv[0], own_rows[tok_len], precision=highest),
                jnp.dot(grad_kv[0], own_rows[tok_len + 1], precision=highest),
            ]
        )
        / model_width
    )
    grads_all, sides_all = (
        lax.all_gather(grad_kv, "fsdp", axis=0, tiled=True),
        lax.all_gather(side_mean[None, :], "fsdp", axis=0, tiled=True),
    )
    grad_cols = jnp.dot(grads_all, weight_f.T, precision=highest) * scale_cols
    row_grad = grad_cols - sides_all[:, 0:1] - concept_f * sides_all[:, 1:2]
    owner_scale = table_rstd / counts.astype(jnp.float32)
    rows_all, ids_all = (
        lax.all_gather(row_grad, "dp", axis=0, tiled=True),
        lax.all_gather(group_ids, "dp", axis=0, tiled=True),
    )
    first_row = lax.axis_index("dp") * conc_dev
    one_hot = (
        (first_row + jnp.arange(conc_dev, dtype=jnp.int32))[:, None] == ids_all[None, :]
    ).astype(jnp.float32)
    owned_rows = jnp.dot(one_hot, rows_all, precision=highest)
    return owned_rows * owner_scale[:, None]


def solution(mesh):
    placed = (
        P(("dp", "fsdp"), None, None),
        P("dp", None),
        P(("dp", "fsdp")),
        P(("dp", "fsdp")),
        P(("dp", "fsdp")),
        P("dp"),
        P(None, None, "fsdp"),
        P("fsdp", None),
        P(),
        P(),
        P(("dp", "fsdp"), None, None),
        P(("dp", "fsdp"), None, None),
        P(("dp", "fsdp"), None, None),
        P(("dp", "fsdp"), None, None),
    )
    return jax.shard_map(
        shards, mesh=mesh, in_specs=placed, out_specs=P("dp", "fsdp"), check_vma=False
    )
```

profile of v0, /device:TPU:0, one launch (start us, length us, event | category | flops | bytes accessed | tf_op | source)
XLA Modules:
  0.0 163.7 jit_solution(4914601136978119193)
XLA Ops:
  8.7 0.6 tile.2
  9.3 5.2 %all-to-all-start = ((s32[1,8,3]{2,0,1:T(1,128)}), s32[1,8,3]{2,0,1:T(1,128)S(1)}, u32[]{:S(2)}, u32[]{:S(2)}) async-start(s32[1,8,3]{2,0,1:T(1,128)} %tile.2), calls=%async_computation | async-start | bytes 8192 | tf_op jit(solution)/shard_map/all_to_all | solution.py:56
  14.5 1.8 %convert_reduce_fusion = f32[256]{0:T(256)S(1)} fusion(bf16[256,3072]{1,0:T(8,128)(2,1)} %param.15), kind=kLoop, calls=%fused_computation.3 | loop fusion | flops 1572608 | bytes 1573888 | tf_op jit(solution)/shard_map/reduce_sum | solution.py:10
  16.4 2.1 %multiply_reduce_fusion = (f32[256]{0:T(256)S(1)}, f32[256,3072]{1,0:T(8,128)}) fusion(f32[256]{0:T(256)S(1)} %broadcast_multiply_fusion, bf16[256,3072]{1,0:T(8,128)(2,1)S(1)} %copy-done.1), kind=kLoop, calls=%fused_computation.4 | loop fusion | flops 3145472 | bytes 4720640 | tf_op jit(solution)/shard_map/reduce_sum | solution.py:11
  18.5 1.1 fusion.30
  19.6 19.8 %all_gather.16 = bf16[1024,384]{1,0:T(8,128)(2,1)S(1)} all-gather(bf16[256,384]{1,0:T(8,128)(2,1)S(1)} %fusion.30), channel_id=1, replica_groups=mesh['dp'=4,'fsdp'=8] {'dp'}, dimensions={0}, use_global_device_ids=true | all-gather | bytes 983040 | tf_op jit(solution)/shard_map/all_gather | solution.py:50
  39.4 0.1 convert_reduce_fusion.1
  39.6 0.2 fusion.36
  39.8 0.7 multiply_convert_fusion
  40.5 4.2 %all-to-all-start.1 = ((bf16[8,8,384]{2,0,1:T(8,128)(2,1)}), bf16[8,8,384]{2,0,1:T(8,128)(2,1)S(1)}, u32[]{:S(2)}, u32[]{:S(2)}) async-start(bf16[8,8,384]{2,0,1:T(8,128)(2,1)} %multiply_convert_fusion), calls=%async_computation.1 | async-start | bytes 98304 | tf_op jit(solution)/shard_map/all_to_all | solution.py:55
  44.9 0.2 fusion.32
  45.1 0.6 gather_fusion
  45.8 1.0 fusion.3
  46.9 0.2 copy.34
  47.1 2.6 %all-to-all-done.1 = bf16[8,8,384]{2,0,1:T(8,128)(2,1)S(1)} async-done(((bf16[8,8,384]{2,0,1:T(8,128)(2,1)}), bf16[8,8,384]{2,0,1:T(8,128)(2,1)S(1)}, u32[]{:S(2)}, u32[]{:S(2)}) %all-to-all-start.1) | async-done | bytes 49184 | tf_op jit(solution)/shard_map/all_to_all | solution.py:55
  49.7 0.6 fusion.5
  50.2 1.3 pad_maximum_fusion
  51.5 2.5 %reshape.233 = f32[80,3072]{1,0:T(8,128)} reshape(f32[8,10,3072]{2,1,0:T(8,128)} %pad_maximum_fusion) | data formatting | bytes 1966080 | tf_op jit(solution)/shard_map/reshape | solution.py:93
  54.1 0.6 dynamic-slice.1
  55.3 1.5 reshape_squeeze.7
  56.8 2.3 %concatenate.29 = bf16[192,12,128]{2,1,0:T(8,128)(2,1)} reshape(bf16[1,192,1536]{2,1,0:T(8,128)(2,1)} %param.25) | data formatting | bytes 1179648 | tf_op jit(solution)/shard_map/concatenate | solution.py:103
  59.1 2.1 %copy.35 = bf16[192,12,128]{2,0,1:T(8,128)(2,1)} copy(bf16[192,12,128]{2,1,0:T(8,128)(2,1)} %concatenate.29) | data formatting | bytes 1179648 | tf_op jit(solution)/shard_map/concatenate | solution.py:103
  61.2 2.3 %reshape_squeeze.6 = bf16[192,12,128]{2,1,0:T(8,128)(2,1)} reshape(bf16[1,192,1536]{2,1,0:T(8,128)(2,1)} %param.24) | data formatting | bytes 1179648 | tf_op jit(solution)/shard_map/reshape;squeeze | solution.py:109
  63.5 2.3 %concatenate.31 = bf16[192,12,128]{2,1,0:T(8,128)(2,1)} reshape(bf16[1,192,1536]{2,1,0:T(8,128)(2,1)} %param.26) | data formatting | bytes 1179648 | tf_op jit(solution)/shard_map/concatenate | solution.py:106
  65.8 2.1 %copy.37 = bf16[192,12,128]{2,0,1:T(8,128)(2,1)} copy(bf16[192,12,128]{2,1,0:T(8,128)(2,1)} %concatenate.31) | data formatting | bytes 1179648 | tf_op jit(solution)/shard_map/concatenate | solution.py:106
  67.9 0.6 dynamic-slice
  69.2 6.7 %all-reduce = s32[32]{0:T(128)S(1)} all-reduce(s32[32]{0:T(128)S(1)} %bitcast_dynamic-update-slice_fusion), channel_id=2, replica_groups=mesh['dp'=4,'fsdp'=8] {'dp'}, use_global_device_ids=true, to_apply=%add | all-reduce | flops 32 | bytes 256
  75.9 32.3 %all-reduce.4.cloned.1.call-done = f32[80,3072]{1,0:T(8,128)} async-done(((f32[80,3072]{1,0:T(8,128)}), f32[80,3072]{1,0:T(8,128)}) %all-reduce.4.cloned.1.call-update) | async-done | bytes 983056
  108.2 0.9 dynamic-slice_add_fusion
  109.3 1.8 %fusion.16 = f32[12,200,192]{1,2,0:T(8,128)S(1)} fusion(bf16[192,12,128]{2,0,1:T(8,128)(2,1)} %copy.35, bf16[8,12,128]{2,0,1:T(8,128)(2,1)S(1)} %fusion.46, bf16[192,12,128]{2,1,0:T(8,128)(2,1)} %reshape_squeeze.6), kind=kOutput, calls=%fused_computation.29 | convolution fusion | flops 119193600 | bytes 3047424 | tf_op jit(solution)/shard_map/qhd,khd->hqk/dot_general | solution.py:111
  111.1 2.5 %fusion.79 = (f32[12,192]{1,0:T(8,128)S(1)}, f32[12,192,200]{2,1,0:T(8,128)S(1)}) fusion(f32[12,200,192]{1,2,0:T(8,128)S(1)} %fusion.16), kind=kOutput, calls=%fused_computation.140 | output fusion | flops 1843399 | bytes 3695616 | tf_op jit(solution)/shard_map/sub | solution.py:114
  113.7 0.4 broadcast_divide_fusion
  114.1 1.0 fusion.10
  115.1 0.6 fusion.23
  115.7 0.5 convolution_bitcast_fusion
  116.2 0.9 multiply_reduce_fusion.1
  117.3 1.0 fusion.25
  118.3 1.7 %fusion.27 = f32[12,1,128]{2,1,0:T(1,128)S(1)} fusion(bf16[192,12,128]{2,1,0:T(8,128)(2,1)} %reshape_squeeze.6, f32[12,192,1]{1,0,2:T(8,128)S(1)} %fusion.52), kind=kOutput, calls=%fused_computation.40 | convolution fusion | flops 3538944 | bytes 605184 | tf_op jit(solution)/shard_map/hq,qhd->hd/dot_general | solution.py:127
  120.0 0.2 convolution_reduce_fusion
  120.3 0.2 fusion.58
  120.6 1.0 constant_dynamic-slice_fusion.1
  121.6 0.7 multiply_reduce_fusion.3
  122.3 8.2 %all-gather.1 = f32[24576]{0:T(1024)S(1)} all-gather(f32[3072]{0:T(1024)S(1)} %get-tuple-element.7), channel_id=3, replica_groups=mesh['dp'=4,'fsdp'=8] {'fsdp'}, dimensions={0}, use_global_device_ids=true | all-gather | bytes 110592 | tf_op jit(solution)/shard_map/all_gather | solution.py:148
  130.5 1.4 fusion.68
  132.0 8.7 %all-gather.2 = f32[8,1,2]{2,1,0:T(1,128)S(1)} all-gather(f32[1,1,2]{2,1,0:T(1,128)S(1)} %fusion.68), channel_id=1, replica_groups=mesh['dp'=4,'fsdp'=8] {'fsdp'}, dimensions={0}, use_global_device_ids=true | all-gather | bytes 72 | tf_op jit(solution)/shard_map/all_gather | solution.py:149
  140.8 1.9 %fusion.15 = f32[8,384]{1,0:T(8,128)S(1)} fusion(f32[8,3072]{1,0:T(8,128)S(1)} %reshape.248, bf16[384,3072]{1,0:T(8,128)(2,1)S(1)} %copy-done, bf16[8,384]{1,0:T(8,128)(2,1)S(1)} %broadcast_select_fusion, f32[8]{0:T(128)S(1)} %get-tuple-element.22, f32[8]{0:T(128)S(1)} %get-tuple-element.21, f32[8,2,384]{2,0,1:T(8,128)S(1)} %fusion.32), kind=kOutput, calls=%fused_computation.25 | convolution fusion | flops 113264640 | bytes 2488384 | tf_op jit(solution)/shard_map/dot_general | solution.py:151
  142.7 13.1 %all_gather.19 = f32[32,384]{1,0:T(8,128)S(1)} all-gather(f32[8,384]{1,0:T(8,128)S(1)} %fusion.15), channel_id=1, replica_groups=mesh['dp'=4,'fsdp'=8] {'dp'}, dimensions={0}, use_global_device_ids=true | all-gather | bytes 61440 | tf_op jit(solution)/shard_map/all_gather | solution.py:155
  155.8 1.1 convolution_multiply_fusion
  (55 shorter events, 1.4 us)
Async XLA Ops:
  6.5 39.3 %copy-start = (bf16[384,3072]{1,0:T(8,128)(2,1)S(1)}, bf16[384,3072]{1,0:T(8,128)(2,1)}, u32[]{:S(2)}) copy-start(bf16[384,3072]{1,0:T(8,128)(2,1)} %param.21) | copy-start | bytes 7077892
  9.3 31.2 %all-to-all-start = ((s32[1,8,3]{2,0,1:T(1,128)}), s32[1,8,3]{2,0,1:T(1,128)S(1)}, u32[]{:S(2)}, u32[]{:S(2)}) async-start(s32[1,8,3]{2,0,1:T(1,128)} %tile.2), calls=%async_computation | async-start | bytes 8192 | tf_op jit(solution)/shard_map/all_to_all | solution.py:56
  14.5 1.9 %copy-start.1 = (bf16[256,3072]{1,0:T(8,128)(2,1)S(1)}, bf16[256,3072]{1,0:T(8,128)(2,1)}, u32[]{:S(2)}) copy-start(bf16[256,3072]{1,0:T(8,128)(2,1)} %param.15) | copy-start | bytes 4718596
  16.4 2.1 %copy-start.5 = (s32[256]{0:T(256)S(1)}, s32[256]{0:T(256)}, u32[]{:S(2)}) copy-start(s32[256]{0:T(256)} %param.19) | copy-start | bytes 3076
  16.4 23.0 %copy-start.3 = (bf16[1,8,3072]{2,1,0:T(8,128)(2,1)S(1)}, bf16[1,8,3072]{2,1,0:T(8,128)(2,1)}, u32[]{:S(2)}) copy-start(bf16[1,8,3072]{2,1,0:T(8,128)(2,1)} %param.14) | copy-start | bytes 147460
  16.4 23.4 %copy-start.6 = (f32[128]{0:T(128)S(1)}, f32[128]{0:T(128)}, u32[]{:S(2)}) copy-start(f32[128]{0:T(128)} %param.23) | copy-start | bytes 1540
  16.4 28.5 %copy-start.7 = (bf16[64,2,384]{2,1,0:T(2,128)(2,1)S(1)}, bf16[64,2,384]{2,1,0:T(2,128)(2,1)}, u32[]{:S(2)}) copy-start(bf16[64,2,384]{2,1,0:T(2,128)(2,1)} %param.20) | copy-start | bytes 294916
  40.5 9.2 %all-to-all-start.1 = ((bf16[8,8,384]{2,0,1:T(8,128)(2,1)}), bf16[8,8,384]{2,0,1:T(8,128)(2,1)S(1)}, u32[]{:S(2)}, u32[]{:S(2)}) async-start(bf16[8,8,384]{2,0,1:T(8,128)(2,1)} %multiply_convert_fusion), calls=%async_computation.1 | async-start | bytes 98304 | tf_op jit(solution)/shard_map/all_to_all | solution.py:55
  44.7 63.5 %all-reduce.4.cloned.1.call-start = ((), (), s32[]{:S(2)}) async-start(), calls=%async_computation.2 | async-start | bytes 1966080
  51.5 2.5 %copy-start.9 = (u32[32]{0:T(128)S(1)}, u32[32]{0:T(128)}, u32[]{:S(2)}) copy-start(u32[32]{0:T(128)} %constant.79) | copy-start | bytes 388
  61.2 6.6 %copy-start.8 = (u32[32]{0:T(128)S(1)}, u32[32]{0:T(128)}, u32[]{:S(2)}) copy-start(u32[32]{0:T(128)} %constant.70) | copy-start | bytes 388
  61.2 46.9 %copy-start.4 = (f32[3072]{0:T(1024)S(1)}, f32[3072]{0:T(1024)}, u32[]{:S(2)}) copy-start(f32[3072]{0:T(1024)} %param.22) | copy-start | bytes 36868
  113.7 2.0 %copy-start.2 = (bf16[192,12,128]{2,0,1:T(8,128)(2,1)S(1)}, bf16[192,12,128]{2,0,1:T(8,128)(2,1)}, u32[]{:S(2)}) copy-start(bf16[192,12,128]{2,0,1:T(8,128)(2,1)} %copy.37) | copy-start | bytes 1769476
Sparse Core Ops, SparseCore 0:
  54.2 53.9 all-reduce.3
where the time goes:
time: 164 us
  blocking collectives  56.5 us (34%)
  waiting for transfers between devices  34.9 us (21%)
  local copies, waits for them, and re-layouts  19 us (12%)
  between operations  17 us (10%)
  other arithmetic  15 us (9%)
  matrix products  11.9 us (7%)
  starting transfers between devices  9.43 us (6%)
    unnamed x2, waiting for transfers between devices  32.3 us
    all_gather x1, blocking collectives, shards(): table_all = lax.all_gather(table_part, 'dp', axis=0, tiled=True)  19.8 us
    all_gather x1, blocking collectives, shards(): lax.all_gather(row_grad, 'dp', axis=0, tiled=True)  13.1 us
    all_gather x1, blocking collectives, shards(): lax.all_gather(side_mean[None, :], 'fsdp', axis=0, tiled=True)  8.73 us
    all_gather x1, blocking collectives, shards(): lax.all_gather(grad_kv, 'fsdp', axis=0, tiled=True)  8.24 us
    unnamed x1, blocking collectives  6.68 us
    all_to_all x1, starting transfers between devices, shards(): lax.all_to_all(label_tile, 'fsdp', split_axis=1, concat_axis=0, tiled=True)  5.17 us
    concatenate x2, local copies, waits for them, and re-layouts, shards(): jnp.concatenate([key_norm, img_key[0]], 0)  4.4 us
  transfers between devices with their start and end apart: 3, of which 2 were waited for; matrix products, arithmetic and copies ran while one was open for 14% of the time, Pallas kernels for 0%

commit v1 on v0

v1 whole, which is shorter than its diff:
```python
import functools
import math

import jax
import jax.numpy as jnp
import numpy as np
from jax import lax
from jax.experimental import pallas as pl
from jax.experimental.pallas import tpu as pltpu
from jax.sharding import Mesh, PartitionSpec as P

EPSILON = 1e-06
BF16 = jnp.bfloat16
F32 = jnp.float32
VMEM_BYTES = 63 * 1024 * 1024 + 512 * 1024
NT = (((1,), (1,)), ((), ()))


def dot(a, b):
    return jnp.dot(a, b, preferred_element_type=F32)


def dot_nt(a, b):
    return lax.dot_general(a, b, NT, preferred_element_type=F32)


def split_bf16(x):
    high = x.astype(BF16)
    return high, (x - high.astype(F32)).astype(BF16)


def whole(*shape):
    return pl.BlockSpec(shape, lambda *_: (0,) * len(shape))


def params(**kw):
    return pltpu.CompilerParams(vmem_limit_bytes=VMEM_BYTES, **kw)


def token_norm_kernel(x_ref, out_ref):
    x = x_ref[...].astype(F32)
    d = x - jnp.mean(x, -1, keepdims=True)
    out_ref[...] = (d * lax.rsqrt(jnp.mean(d * d, -1, keepdims=True) + EPSILON)).astype(BF16)


def token_norm(tokens):
    return pl.pallas_call(
        token_norm_kernel, out_shape=jax.ShapeDtypeStruct(tokens.shape, BF16), compiler_params=params()
    )(tokens)


def table_norm_kernel(n_parts, x_ref, *refs):
    parts, hats, rstd_ref = refs[:n_parts], refs[n_parts : 2 * n_parts], refs[-1]
    x = x_ref[...].astype(F32)
    mean = jnp.mean(x, -1, keepdims=True)
    d = x - mean
    rstd = lax.rsqrt(jnp.mean(d * d, -1, keepdims=True) + EPSILON)
    rstd_ref[...] = rstd
    for part, hat in zip(parts, hats):
        hat[...] = ((part[...].astype(F32) - mean) * rstd).astype(BF16)


def table_norm(table, parts):
    rows, width = table.shape
    block = math.gcd(rows, 64)
    row_spec = lambda w: pl.BlockSpec((block, w), lambda i: (i, 0))
    widths = [p.shape[1] for p in parts]
    out = pl.pallas_call(
        functools.partial(table_norm_kernel, len(parts)),
        grid=(rows // block,),
        in_specs=[row_spec(width)] + [row_spec(w) for w in widths],
        out_specs=[row_spec(w) for w in widths] + [row_spec(1)],
        out_shape=[jax.ShapeDtypeStruct((rows, w), BF16) for w in widths]
        + [jax.ShapeDtypeStruct((rows, 1), F32)],
        compiler_params=params(),
    )(table, *parts)
    return out[:-1], out[-1]


def image_kernel(head_dim, q_ref, k_ref, v_ref, g_ref, out_ref):
    scale = 1.0 / math.sqrt(head_dim)
    for h in range(q_ref.shape[1] // head_dim):
        cols = slice(h * head_dim, (h + 1) * head_dim)
        s = dot_nt(k_ref[:, cols], q_ref[:, cols]) * scale
        gv = dot_nt(v_ref[:, cols], g_ref[:, cols])
        top = jnp.max(s, 0, keepdims=True)
        e = jnp.exp(s - top)
        out_ref[h, 0:1, :] = top
        out_ref[h, 1:2, :] = jnp.sum(e, 0, keepdims=True)
        out_ref[h, 2:3, :] = jnp.sum(e * gv, 0, keepdims=True)


def image_part(q, k, v, g, head_dim):
    rows, width = q.shape
    heads = width // head_dim
    per = math.gcd(heads, 3)
    spec = pl.BlockSpec((rows, per * head_dim), lambda i: (0, i))
    return pl.pallas_call(
        functools.partial(image_kernel, head_dim),
        grid=(heads // per,),
        in_specs=[spec] * 4,
        out_specs=pl.BlockSpec((per, 8, rows), lambda i: (i, 0, 0)),
        out_shape=jax.ShapeDtypeStruct((heads, 8, rows), F32),
        compiler_params=params(),
    )(q, k, v, g)


def project_kernel(dims, here_ref, labels_ref, *refs):
    n_dp, n_chip, n_core, tok_len, conc_dev, buckets, col_block, head_dim = dims
    mods, hats = refs[:n_core], refs[n_core : 2 * n_core]
    toks = refs[2 * n_core : 2 * n_core + n_chip]
    weights = refs[2 * n_core + n_chip : 3 * n_core + n_chip]
    rest = refs[3 * n_core + n_chip :]
    conc_out, tok_outs, lhs = rest[0], rest[1 : 1 + n_chip], rest[1 + n_chip]
    n_all = n_dp * n_chip
    n_tok = n_chip * tok_len

    @pl.when(pl.program_id(0) == 0)
    def _():
        my_dp, my_chip, my_core = here_ref[0], here_ref[1], here_ref[2]
        labels = labels_ref[:, 0, :].reshape(n_all, n_core, labels_ref.shape[2])
        mine = jnp.where(lax.broadcasted_iota(jnp.int32, labels.shape, 1) == my_core, labels, 0)
        mine = jnp.sum(mine, 1)
        ids, times = mine[:, 0:1], mine[:, 2:3]
        lanes = lambda r, n: lax.broadcasted_iota(jnp.int32, (r, n), 1)
        pick_time = (lanes(n_all, buckets) == times).astype(BF16)
        pick_row = (lanes(n_all, conc_dev) == ids - my_dp * conc_dev).astype(BF16)

        def owned_by(step):
            first = lax.rem(my_dp + n_dp - step, n_dp) * conc_dev
            return (ids >= first) & (ids < first + conc_dev)

        tok_times = jnp.concatenate(
            [
                jnp.broadcast_to(
                    labels_ref[(my_dp * n_chip + (my_chip ^ s)) * n_core + my_core][:, 2:3],
                    (tok_len, 1),
                )
                for s in range(n_chip)
            ],
            0,
        )
        pick_tok = (lanes(n_tok, buckets) == tok_times).astype(BF16)
        for p in range(n_core):
            shift, scale = mods[p][0], mods[p][1]
            scale_c, shift_c = 1.0 + dot(pick_time, scale), dot(pick_time, shift)
            conc = scale_c * dot(pick_row, hats[p][...]) + shift_c
            conc = conc.astype(BF16).astype(F32)
            rows = jnp.where(
                owned_by(0),
                conc,
                jnp.where(owned_by(1), scale_c, jnp.where(owned_by(2), shift_c, 0.0)),
            )
            high, low = split_bf16(rows)
            tok = jnp.concatenate([t[p].astype(F32) for t in toks], 0)
            tok = (1.0 + dot(pick_tok, scale)) * tok + dot(pick_tok, shift)
            lhs[p, 0:n_tok] = tok.astype(BF16)
            lhs[p, n_tok : n_tok + n_all] = high
            lhs[p, n_tok + n_all : n_tok + 2 * n_all] = low

    out = dot(lhs[0], weights[0][...])
    for p in range(1, n_core):
        out += dot(lhs[p], weights[p][...])
    conc = out[n_tok : n_tok + n_all] + out[n_tok + n_all :]
    for r in range(col_block // head_dim):
        conc_out[:, r, :] = conc[:, r * head_dim : (r + 1) * head_dim]
    for s in range(n_chip):
        tok_outs[s][...] = out[s * tok_len : (s + 1) * tok_len].astype(BF16)


def project(here, labels, mods, hats, toks, weights, sizes, head_dim):
    n_dp, n_chip, n_core = sizes
    tok_len = toks[0].shape[1]
    width, kv_width = weights[0].shape
    conc_dev, buckets = hats[0].shape[0], mods[0].shape[1]
    col_block = 8 * head_dim
    n_all, n_tok = n_dp * n_chip, n_chip * tok_len
    dims = (n_dp, n_chip, n_core, tok_len, conc_dev, buckets, col_block, head_dim)
    out = pl.pallas_call(
        functools.partial(project_kernel, dims),
        grid=(kv_width // col_block,),
        in_specs=[pl.BlockSpec(memory_space=pltpu.SMEM), whole(*labels.shape)]
        + [whole(*m.shape) for m in mods]
        + [whole(*h.shape) for h in hats]
        + [whole(*t.shape) for t in toks]
        + [pl.BlockSpec((width, col_block), lambda i: (0, i))] * n_core,
        out_specs=[pl.BlockSpec((n_all, 8, head_dim), lambda i: (0, i, 0))]
        + [pl.BlockSpec((tok_len, col_block), lambda i: (0, i))] * n_chip,
        out_shape=[jax.ShapeDtypeStruct((n_all, kv_width // head_dim, head_dim), F32)]
        + [jax.ShapeDtypeStruct((tok_len, kv_width), BF16)] * n_chip,
        scratch_shapes=[pltpu.VMEM((n_core, n_tok + 2 * n_all, width), BF16)],
        compiler_params=params(),
    )(here, labels, *mods, *hats, *toks, *weights)
    return out[0], out[1:]


def sample_kernel(dims, place_ref, conc_ref, bias_ref, gain_ref, stat_ref, q_ref, g_ref, *refs):
    n_chip, head_dim, model_width, n_dev = dims
    toks, out_ref = refs[:n_chip], refs[n_chip]
    heads = stat_ref.shape[0]
    scale = 1.0 / math.sqrt(head_dim)
    tok_len = toks[0].shape[0]
    kv = toks[0][...].astype(F32)
    for t in toks[1:]:
        kv += t[...].astype(F32)

    def gathered(i):
        total = conc_ref[place_ref[i] * n_chip]
        for s in range(1, n_chip):
            total += conc_ref[place_ref[i] * n_chip + s]
        return total

    conc, scale_sum, shift_sum = gathered(0), gathered(1), gathered(2)
    at_pos = lax.broadcasted_iota(jnp.int32, (tok_len, 1), 0) == place_ref[3]
    row = lax.broadcasted_iota(jnp.int32, (8, 1), 0)
    gain = gain_ref[...]
    rows = []
    for i in range(2 * heads):
        cols = slice(i * head_dim, (i + 1) * head_dim)
        rows.append(jnp.where(at_pos, conc[i : i + 1, :], kv[:, cols]) + bias_ref[:, cols])

    def pick(x):
        return jnp.sum(jnp.where(at_pos, x, 0.0), 0, keepdims=True)

    def contract(weights, cols, ref):
        high, low = split_bf16(weights)
        both = jnp.where(row == 0, high.astype(F32), jnp.where(row == 1, low.astype(F32), 0.0))
        return jnp.sum(dot(both.astype(BF16), ref[:, cols]), 0, keepdims=True)

    raw_rows, val_rows = [], []
    for h in range(heads):
        cols = slice(h * head_dim, (h + 1) * head_dim)
        raw = rows[h]
        inv = lax.rsqrt(jnp.mean(raw * raw, -1, keepdims=True) + EPSILON)
        key = (raw * inv * gain).astype(BF16)
        val = rows[heads + h].astype(BF16)
        s = dot_nt(key, q_ref[:, cols]) * scale
        gv = dot_nt(val, g_ref[:, cols])
        top, total, weighted = stat_ref[h, 0:1, :], stat_ref[h, 1:2, :], stat_ref[h, 2:3, :]
        new_top = jnp.maximum(top, jnp.max(s, 0, keepdims=True))
        e = jnp.exp(s - new_top)
        keep = jnp.exp(top - new_top)
        inv_total = 1.0 / (total * keep + jnp.sum(e, 0, keepdims=True))
        delta = (weighted * keep + jnp.sum(e * gv, 0, keepdims=True)) * inv_total
        p = pick(e) * inv_total
        dscore = p * (pick(gv) - delta)
        val_rows.append(contract(p, cols, g_ref))
        dkey = contract(dscore, cols, q_ref) * scale
        inv_pos = pick(inv)
        normed = pick(raw) * inv_pos
        dn = dkey * gain
        raw_rows.append(inv_pos * (dn - normed * jnp.mean(dn * normed, -1, keepdims=True)))
    dkv = jnp.concatenate(raw_rows + val_rows, 0)

    def total_of(x):
        return jnp.sum(jnp.sum(x, 0, keepdims=True), 1, keepdims=True) * (1.0 / model_width)

    mean_1 = split_bf16(total_of(dkv * scale_sum))
    mean_2 = split_bf16(total_of(dkv * (conc - shift_sum)))
    lane = lax.broadcasted_iota(jnp.int32, (8, head_dim), 1)
    side = jnp.zeros((8, head_dim), F32)
    for i, x in enumerate(mean_1 + mean_2):
        side = jnp.where(lane == i, x.astype(F32), side)
    packet = jnp.concatenate([dkv, side], 0).astype(BF16)
    out_ref[...] = jnp.broadcast_to(packet[None], out_ref.shape)


def sample_part(place, conc, bias, gain, stats, q, g, toks, n_dev, model_width):
    n_chip, head_dim = len(toks), gain.shape[1]
    rows = conc.shape[1] + 8
    vmem = pl.BlockSpec(memory_space=pltpu.VMEM)
    return pl.pallas_call(
        functools.partial(sample_kernel, (n_chip, head_dim, model_width, n_dev)),
        in_specs=[pl.BlockSpec(memory_space=pltpu.SMEM)] + [vmem] * (6 + n_chip),
        out_specs=vmem,
        out_shape=jax.ShapeDtypeStruct((n_dev, rows, head_dim), BF16),
        compiler_params=params(),
    )(place, conc, bias, gain, stats, q, g, *toks)


def owner_kernel(dims, here_ref, packet_ref, labels_ref, ids_ref, mod_ref, hat_ref, coef_ref, w_ref, out_ref, flat):
    conc_dev, buckets = dims
    n_dev, rows, head_dim = packet_ref.shape
    parts = w_ref.shape[1] // head_dim
    first = here_ref[0] * conc_dev
    flat[...] = packet_ref[...].reshape(n_dev * rows, head_dim).astype(F32)
    piece = lambda r: flat[pl.ds(r, n_dev, stride=rows), :]
    dkv = jnp.concatenate([piece(r).astype(BF16) for r in range(parts)], 1)
    side = piece(parts)
    mean_1 = side[:, 0:1] + side[:, 1:2]
    mean_2 = side[:, 2:3] + side[:, 3:4]
    labels = labels_ref[:, 0, :]
    ids, times = labels[:, 0:1], labels[:, 2:3]
    lanes = lambda n: lax.broadcasted_iota(jnp.int32, (n_dev, n), 1)
    scale = 1.0 + dot((lanes(buckets) == times).astype(BF16), mod_ref[1])
    conc = dot((lanes(conc_dev) == ids - first).astype(BF16), hat_ref[...])
    grad = dot_nt(dkv, w_ref[...]) * scale - mean_1 - conc * mean_2
    high, low = split_bf16(grad)
    one_hot = lax.broadcasted_iota(jnp.int32, (conc_dev, n_dev), 0) == ids_ref[...] - first
    one_hot = one_hot.astype(BF16)
    out_ref[...] = (dot(one_hot, high) + dot(one_hot, low)) * coef_ref[...]


def owner_part(here, packets, labels, ids, mod, hat, coef, weight):
    conc_dev, width = hat.shape
    n_dev, rows, head_dim = packets.shape
    vmem = pl.BlockSpec(memory_space=pltpu.VMEM)
    return pl.pallas_call(
        functools.partial(owner_kernel, (conc_dev, mod.shape[1])),
        in_specs=[pl.BlockSpec(memory_space=pltpu.SMEM)] + [vmem] * 7,
        out_specs=vmem,
        out_shape=jax.ShapeDtypeStruct((conc_dev, width), F32),
        scratch_shapes=[pltpu.VMEM((n_dev * rows, head_dim), F32)],
        compiler_params=params(),
    )(here, packets, labels, ids, mod, hat, coef, weight)


def shards(
    txt_tokens,
    concept_table,
    concept_ids,
    positions,
    timesteps,
    counts,
    mod_table,
    kv_weight,
    kv_bias,
    key_gain,
    img_query,
    img_key,
    img_value,
    out_grad,
):
    everyone = ("dp", "chip", "core")
    n_dp, n_chip, n_core = (lax.axis_size(a) for a in everyone)
    n_dev = n_dp * n_chip * n_core
    my_dp, my_chip, my_core = (lax.axis_index(a) for a in everyone)
    model_width = txt_tokens.shape[2]
    slice_width = kv_weight.shape[0]
    head_dim = key_gain.shape[0]
    conc_dev = concept_table.shape[0]
    here = jnp.stack([my_dp, my_chip, my_core]).astype(jnp.int32)

    labels = jnp.stack([concept_ids[0], positions[0], timesteps[0]])
    labels = jnp.pad(labels, (0, 125))
    labels = lax.all_to_all(
        jnp.broadcast_to(labels[None, None, :], (n_dev, 1, 128)), everyone, 0, 0, tiled=True
    )

    def from_core(x, s):
        return x if s == 0 else lax.ppermute(x, "core", [(i, i ^ s) for i in range(n_core)])

    def from_chip(x, s):
        return x if s == 0 else lax.ppermute(x, "chip", [(i, i ^ s) for i in range(n_chip)])

    def feature_slice(x, chip, s):
        part = chip * n_core + (my_core ^ s)
        return lax.dynamic_slice_in_dim(x, part * slice_width, slice_width, 1)

    own_hat = token_norm(txt_tokens[0])
    toks = [
        from_chip(
            jnp.stack([feature_slice(own_hat, my_chip ^ s, p) for p in range(n_core)]), s
        )
        for s in range(n_chip)
    ]
    weights = [from_core(kv_weight, s) for s in range(n_core)]
    mod_own = jnp.transpose(mod_table, (1, 0, 2))
    mods = [from_core(mod_own, s) for s in range(n_core)]
    hats, rstd = table_norm(
        concept_table, [feature_slice(concept_table, my_chip, s) for s in range(n_core)]
    )
    coef = rstd / counts.astype(F32)[:, None]
    stats = image_part(img_query[0], img_key[0], img_value[0], out_grad[0], head_dim)

    conc, tok_terms = project(
        here, labels, mods, hats, toks, weights, (n_dp, n_chip, n_core), head_dim
    )
    tok_rows = [from_chip(t, s) for s, t in enumerate(tok_terms)]
    conc = lax.all_to_all(conc, ("dp", "chip"), 0, 0, tiled=True)

    owner = concept_ids[0] // conc_dev
    place = jnp.stack([owner, (owner + 1) % n_dp, (owner + 2) % n_dp, positions[0]])
    packets = sample_part(
        place, conc, kv_bias[None], key_gain[None], stats, img_query[0], out_grad[0],
        tok_rows, n_dev, model_width,
    )
    packets = lax.all_to_all(packets, everyone, 0, 0, tiled=True)
    ids = labels[:, 0, 0][None, :]
    return owner_part(here, packets, labels, ids, mod_own, hats[0], coef, kv_weight)


def solution(mesh):
    n_dp, n_fsdp = mesh.shape["dp"], mesh.shape["fsdp"]
    n_core = 2 if n_fsdp % 2 == 0 else 1
    fine = Mesh(mesh.devices.reshape(n_dp, n_fsdp // n_core, n_core), ("dp", "chip", "core"))
    fsdp = ("chip", "core")
    every = ("dp",) + fsdp
    placed = (
        P(every, None, None),
        P("dp", None),
        P(every),
        P(every),
        P(every),
        P("dp"),
        P(None, None, fsdp),
        P(fsdp, None),
        P(),
        P(),
        P(every, None, None),
        P(every, None, None),
        P(every, None, None),
        P(every, None, None),
    )
    return jax.shard_map(
        shards, mesh=fine, in_specs=placed, out_specs=P("dp", fsdp), check_vma=False
    )
```

time: 164 us -> 73 us (0.45)
  blocking collectives: 56.5 us -> 0 us
  waiting for transfers between devices: 34.9 us -> 8.9 us
  Pallas kernels: 0 us -> 24 us
  starting transfers between devices: 9.43 us -> 27.1 us
  between operations: 17 us -> 2.19 us
  other arithmetic: 15 us -> 2.64 us
  matrix products: 11.9 us -> 0 us
  local copies, waits for them, and re-layouts: 19 us -> 7.48 us
    all_gather x4 -> x0, blocking collectives: 49.8 us -> none  [the longest x1 19.8 us: shards(): table_all = lax.all_gather(table_part, 'dp', axis=0, tiled=True)]
    unnamed x2 -> x0, waiting for transfers between devices: 32.3 us -> none
    pallas_call x0 -> x6, Pallas kernels: none -> 24 us  [the longest x1 5.04 us: sample_part(): pl.pallas_call(functools.partial(sample_kernel, (n_chip, head_dim, model_...]
    dot_general x12 -> x0, matrix products: 11.6 us -> none  [the longest x1 1.92 us: shards(): grad_cols = jnp.dot(grads_all, weight_f.T, precision=highest) * scale_cols]
    all_to_all x2 -> x3, starting transfers between devices: 9.4 us -> 19.2 us  [the longest x1 6.96 us: shards(): lax.all_to_all(jnp.broadcast_to(labels[None, None, :], (n_dev, 1, 128)),...]
    concatenate x4 -> x0, local copies, waits for them, and re-layouts: 8.75 us -> none  [the longest x2 4.4 us: shards(): jnp.concatenate([key_norm, img_key[0]], 0)]
    ppermute x0 -> x8, starting transfers between devices: none -> 7.88 us  [the longest x6 7.11 us: from_chip(): lax.ppermute(x, 'chip', [(i, i ^ s) for i in range(n_chip)])]
    unnamed x1 -> x0, blocking collectives: 6.68 us -> none
  transfers between devices with their start and end apart: 3 -> 11, of which waited for: 2 -> 2; matrix products, arithmetic and copies ran while one was open for 14% -> 11% of each run, Pallas kernels for 0% -> 14%
where the time goes in v1:
time: 73 us; the launch traced here: 72.3 us
  starting transfers between devices  27.1 us (37%)
  Pallas kernels  24 us (33%)
  waiting for transfers between devices  8.9 us (12%)
  local copies, waits for them, and re-layouts  7.48 us (10%)
  other arithmetic  2.64 us (4%)
  between operations  2.19 us (3%)
    all_to_all x1, waiting for transfers between devices, shards(): packets = lax.all_to_all(packets, everyone, 0, 0, tiled=True)  8.58 us
    ppermute x6, starting transfers between devices, from_chip(): lax.ppermute(x, 'chip', [(i, i ^ s) for i in range(n_chip)])  7.11 us
    all_to_all x1, starting transfers between devices, shards(): lax.all_to_all(jnp.broadcast_to(labels[None, None, :], (n_dev, 1, 128)),...  6.96 us
    all_to_all x1, starting transfers between devices, shards(): conc = lax.all_to_all(conc, ('dp', 'chip'), 0, 0, tiled=True)  6.76 us
    all_to_all x1, starting transfers between devices, shards(): packets = lax.all_to_all(packets, everyone, 0, 0, tiled=True)  5.5 us
    pallas_call x1, Pallas kernels, sample_part(): pl.pallas_call(functools.partial(sample_kernel, (n_chip, head_dim, model_...  5.04 us
    pallas_call x1, Pallas kernels, project(): pl.pallas_call(functools.partial(project_kernel, dims), grid=(kv_width //...  4.91 us
    pallas_call x1, Pallas kernels, image_part(): pl.pallas_call(functools.partial(image_kernel, head_dim), grid=(heads //...  4.4 us
  transfers between devices with their start and end apart: 11, of which 2 were waited for; matrix products, arithmetic and copies ran while one was open for 11% of the time, Pallas kernels for 14%

profile of v1, /device:TPU:0, one launch (start us, length us, event | category | flops | bytes accessed | tf_op | source)
XLA Modules:
  0.0 72.3 jit_solution(2412128369742245514)
XLA Ops:
  0.0 0.5 collective-permute-start.4
  2.4 0.1 pad_add_fusion.2
  2.5 0.6 broadcast_in_dim.15
  3.1 7.0 %all-to-all-start = ((s32[32,1,128]{2,1,0:T(1,128)}), s32[32,1,128]{2,1,0:T(1,128)S(1)}, u32[]{:S(2)}, u32[]{:S(2)}) async-start(s32[32,1,128]{2,1,0:T(1,128)} %broadcast_in_dim.15), calls=%async_computation | async-start | bytes 32768 | tf_op jit(solution)/shard_map/all_to_all | solution.py:346
  10.1 0.9 %copy.19 = bf16[64,2,384]{2,0,1:T(8,128)(2,1)S(1)} copy(bf16[64,2,384]{2,1,0:T(2,128)(2,1)} %param.20) | data formatting | bytes 196608 | tf_op args[6]
  11.0 0.3 collective-permute-start
  11.3 1.6 %shard_map.137 = bf16[8,3072]{1,0:T(8,128)(2,1)} custom-call(bf16[8,3072]{1,0:T(8,128)(2,1)} %bitcast.48), custom_call_target="tpu_custom_call" | custom-call | tf_op jit(solution)/shard_map/pallas_call | solution.py:47
  12.9 0.8 %dynamic-slice_bitcast_fusion.1 = (bf16[1,8,384]{2,1,0:T(8,128)(2,1)S(1)}, bf16[1,8,384]{2,1,0:T(8,128)(2,1)S(1)}, bf16[1,8,384]{2,1,0:T(8,128)(2,1)S(1)}, bf16[...) fusion(bf16[8,3072]{1,0:T(8,128)(2,1)} %shard_map.137, ...), kind=kLoop, calls=%fused_computation.7 | loop fusion | bytes 98336 | tf_op jit(solution)/shard_map/stack | solution.py:363
  13.8 1.7 %collective-permute-start.1 = (bf16[2,8,384]{2,1,0:T(8,128)(2,1)S(1)}, bf16[2,8,384]{2,1,0:T(8,128)(2,1)S(1)}, u32[]{:S(2)}, u32[]{:S(2)}) collective-permute-start(bf16[2,8,384]{2,1,0:T(8,128)(2,1)S(1)} %pad_maximum_fusion.1), channel_id=1, source_target_pairs={{0,2},{2,0},{4,6},{6,4},{1,3},{3,1},{5,7},{7,5},{8,10},{10,8},{12,... | collective-permute-start | bytes 36872 | tf_op jit(solution)/shard_map/ppermute | solution.py:354
  15.5 1.5 %collective-permute-start.2 = (bf16[2,8,384]{2,1,0:T(8,128)(2,1)S(1)}, bf16[2,8,384]{2,1,0:T(8,128)(2,1)S(1)}, u32[]{:S(2)}, u32[]{:S(2)}) collective-permute-start(bf16[2,8,384]{2,1,0:T(8,128)(2,1)S(1)} %pad_maximum_fusion.2), channel_id=1, source_target_pairs={{0,4},{2,6},{4,0},{6,2},{1,5},{3,7},{5,1},{7,3},{8,12},{10,14},{12... | collective-permute-start | bytes 36872 | tf_op jit(solution)/shard_map/ppermute | solution.py:354
  17.0 0.3 collective-permute-start.3
  17.3 0.6 pad_maximum_fusion.refs_4_
  17.9 1.8 %constant_dynamic-slice_fusion = (bf16[256,384]{1,0:T(8,128)(2,1)}, bf16[256,384]{1,0:T(8,128)(2,1)}) fusion(bf16[256,3072]{1,0:T(8,128)(2,1)} %x_ref.1, s32[]{:T(128)S(6)} %select_n.45, s32[]{:T(128)S(6)} %select_n.44), kind=kLoop, calls=%fused_computation.14 | loop fusion | bytes 786440 | tf_op jit(solution)/shard_map/dynamic_slice | solution.py:358
  19.7 0.7 pad_add_fusion.here_ref
  20.4 4.0 %shard_map.136 = (bf16[256,384]{1,0:T(8,128)(2,1)}, bf16[256,384]{1,0:T(8,128)(2,1)}, f32[256,1]{1,0:T(8,128)}) custom-call(bf16[256,3072]{1,0:T(8,128)(2,1)} %x_ref.1, bf16[256,384]{1,0:T(8,128)(2,1)} %get-tuple-element.22.refs_0_, bf16[256,384]{1,0:T(8,128)(2,1)} %get-tuple-element.21.refs_1_), custom_call_target="tpu_custom_call" | custom-call | tf_op jit(solution)/shard_map/pallas_call | solution.py:68
  24.4 0.0 collective-permute-done.1.refs_5_
  24.4 0.0 collective-permute-done.2.refs_6_
  24.4 0.0 collective-permute-done.3.refs_7_
  24.5 0.0 all-to-all-done.labels_ref
  24.5 0.0 collective-permute-done.refs_1_
  24.5 0.0 collective-permute-done.4.refs_9_
  24.5 0.5 copy-done.9
  25.0 0.0 copy-done.10
  25.0 0.0 copy-done.11
  25.0 0.0 copy-done.3
  25.1 0.1 copy-done.6
  25.1 4.9 %shard_map.138 = (f32[16,24,128]{2,1,0:T(8,128)}, bf16[8,3072]{1,0:T(8,128)(2,1)}, bf16[8,3072]{1,0:T(8,128)(2,1)}, bf16[8,3072]{1,0:T(8,128)(2,1)}, bf16[8,3072]{1,0:T(8,128)(2,1)}) custom-call(s32[3]{0:T(128)} %pad_add_fusion.here_ref, s32[32,1,128]{2,1,0:T(1,128)} %copy-done.3, bf16[2,64,384]{2,1,0:T(8,128)(2,1)} %bitcast.44, ...), custom_call_target="tpu_custom_call" | custom-call | tf_op jit(solution)/shard_map/pallas_call | solution.py:179
  30.0 6.8 %all-to-all-start.1 = ((f32[16,24,128]{2,1,0:T(8,128)}), f32[16,24,128]{2,1,0:T(8,128)S(1)}, u32[]{:S(2)}, u32[]{:S(2)}) async-start(f32[16,24,128]{2,1,0:T(8,128)} %get-tuple-element.15), calls=%async_computation.1 | async-start | bytes 393216 | tf_op jit(solution)/shard_map/all_to_all | solution.py:380
  36.9 1.9 %collective-permute-start.5 = (bf16[8,3072]{1,0:T(8,128)(2,1)}, bf16[8,3072]{1,0:T(8,128)(2,1)S(1)}, u32[]{:S(2)}, u32[]{:S(2)}) collective-permute-start(bf16[8,3072]{1,0:T(8,128)(2,1)} %get-tuple-element.17), channel_id=1, source_target_pairs={{0,2},{2,0},{4,6},{6,4},{1,3},{3,1},{5,7},{7,5},{8,10},{10,8},{12,... | collective-permute-start | bytes 147464 | tf_op jit(solution)/shard_map/ppermute | solution.py:354
  38.7 1.5 %collective-permute-start.6 = (bf16[8,3072]{1,0:T(8,128)(2,1)}, bf16[8,3072]{1,0:T(8,128)(2,1)S(1)}, u32[]{:S(2)}, u32[]{:S(2)}) collective-permute-start(bf16[8,3072]{1,0:T(8,128)(2,1)} %get-tuple-element.18), channel_id=1, source_target_pairs={{0,4},{2,6},{4,0},{6,2},{1,5},{3,7},{5,1},{7,3},{8,12},{10,14},{12... | collective-permute-start | bytes 147464 | tf_op jit(solution)/shard_map/ppermute | solution.py:354
  40.2 0.2 collective-permute-start.7
  40.4 0.6 pad_add_fusion.1.place_ref
  41.0 4.4 %shard_map.139.stat_ref = f32[12,8,192]{2,1,0:T(8,128)} custom-call(bf16[192,1536]{1,0:T(8,128)(2,1)} %bitcast.39, bf16[192,1536]{1,0:T(8,128)(2,1)} %bitcast.46, bf16[192,1536]{1,0:T(8,128)(2,1)} %bitcast.47, bf16[192,1536]{1,0:T(8,128)(2,1)} %bitcast.41), custom_call_target="tpu_custom_call" | custom-call | tf_op jit(solution)/shard_map/pallas_call | solution.py:98
  45.4 0.0 collective-permute-done.5.refs_1_
  45.4 0.0 collective-permute-done.6.refs_2_
  45.4 0.3 collective-permute-done.7.refs_3_
  45.7 0.0 all-to-all-done.1.conc_ref
  45.7 0.3 copy-done.7
  46.0 0.0 copy-done.8
  46.1 0.4 copy-done.2
  46.4 5.0 %shard_map.140 = bf16[32,32,128]{2,1,0:T(8,128)(2,1)} custom-call(s32[4]{0:T(128)} %pad_add_fusion.1.place_ref, f32[16,24,128]{2,1,0:T(8,128)} %copy-done.2, f32[1,3072]{1,0:T(1,128)} %bitcast.49, f32[1,128]{1,0:T(1,128)} %bitcast.52, f32[12,8,192]{2,1,0:T(8,128)} %shard_map.139.stat_ref, bf16[192,1536]{1,0:T(8,128)(2,1)} %bitcast.40, ...), custom_call_target="tpu_custom_call" | custom-call | tf_op jit(solution)/shard_map/pallas_call | solution.py:272
  51.5 5.5 %all-to-all-start.2 = ((bf16[32,32,128]{2,1,0:T(8,128)(2,1)}), bf16[32,32,128]{2,1,0:T(8,128)(2,1)S(1)}, u32[]{:S(2)}, u32[]{:S(2)}) async-start(bf16[32,32,128]{2,1,0:T(8,128)(2,1)} %shard_map.140), calls=%async_computation.2 | async-start | bytes 524288 | tf_op jit(solution)/shard_map/all_to_all | solution.py:388
  57.0 0.1 copy.17
  57.2 0.7 div.14.coef_ref
  57.8 1.2 %slice_reduce_fusion = s32[32]{0:T(128)} fusion(s32[32,1,128]{2,1,0:T(1,128)S(1)} %copy-done.4), kind=kLoop, calls=%fused_computation.1 | loop fusion | bytes 256 | tf_op jit(solution)/shard_map/slice | solution.py:389
  59.0 8.6 %all-to-all-done.2.packet_ref = bf16[32,32,128]{2,1,0:T(8,128)(2,1)S(1)} async-done(((bf16[32,32,128]{2,1,0:T(8,128)(2,1)}), bf16[32,32,128]{2,1,0:T(8,128)(2,1)S(1)}, u32[]{:S(2)}, u32[]{:S(2)}) %all-to-all-start.2) | async-done | bytes 262176 | tf_op jit(solution)/shard_map/all_to_all | solution.py:388
  67.6 0.7 copy-done
  68.3 4.0 %shard_map.141 = f32[256,384]{1,0:T(8,128)} custom-call(s32[3]{0:T(128)} %pad_add_fusion.here_ref, bf16[32,32,128]{2,1,0:T(8,128)(2,1)} %copy-done, s32[32,1,128]{2,1,0:T(1,128)} %copy-done.3, s32[1,32]{1,0:T(1,128)} %bitcast.51, bf16[2,64,384]{2,1,0:T(8,128)(2,1)} %bitcast.45, bf16[256,384]{1,0:T(8,128)(2,1)} %get-tuple-element.13.refs_2_.hat_ref, ...), custom_call_target="tpu_custom_call" | custom-call | tf_op jit(solution)/shard_map/pallas_call | solution.py:308
  (22 shorter events, 0.1 us)
Async XLA Ops:
  0.0 24.5 %collective-permute-start.4 = (bf16[384,3072]{1,0:T(8,128)(2,1)}, bf16[384,3072]{1,0:T(8,128)(2,1)}, u32[]{:S(2)}, u32[]{:S(2)}) collective-permute-start(bf16[384,3072]{1,0:T(8,128)(2,1)} %w_ref.1), channel_id=1, source_target_pairs={{0,1},{1,0},{2,3},{3,2},{4,5},{5,4},{6,7},{7,6},{8,9},{9,8},{10,11... | collective-permute-start | bytes 7077896 | tf_op jit(solution)/shard_map/ppermute | solution.py:351
  3.1 21.4 %all-to-all-start = ((s32[32,1,128]{2,1,0:T(1,128)}), s32[32,1,128]{2,1,0:T(1,128)S(1)}, u32[]{:S(2)}, u32[]{:S(2)}) async-start(s32[32,1,128]{2,1,0:T(1,128)} %broadcast_in_dim.15), calls=%async_computation | async-start | bytes 32768 | tf_op jit(solution)/shard_map/all_to_all | solution.py:346
  11.0 13.5 %copy-start.1 = (bf16[64,2,384]{2,0,1:T(8,128)(2,1)}, bf16[64,2,384]{2,0,1:T(8,128)(2,1)S(1)}, u32[]{:S(2)}) copy-start(bf16[64,2,384]{2,0,1:T(8,128)(2,1)S(1)} %copy.19) | copy-start | bytes 294916
  11.0 13.5 %collective-permute-start = (bf16[2,64,384]{2,1,0:T(8,128)(2,1)S(1)}, bf16[2,64,384]{2,1,0:T(8,128)(2,1)S(1)}, u32[]{:S(2)}, u32[]{:S(2)}) collective-permute-start(bf16[2,64,384]{2,1,0:T(8,128)(2,1)S(1)} %bitcast.43), channel_id=1, source_target_pairs={{0,1},{1,0},{2,3},{3,2},{4,5},{5,4},{6,7},{7,6},{8,9},{9,8},{10,11... | collective-permute-start | bytes 294920 | tf_op jit(solution)/shard_map/ppermute | solution.py:351
  13.8 10.6 %collective-permute-start.1 = (bf16[2,8,384]{2,1,0:T(8,128)(2,1)S(1)}, bf16[2,8,384]{2,1,0:T(8,128)(2,1)S(1)}, u32[]{:S(2)}, u32[]{:S(2)}) collective-permute-start(bf16[2,8,384]{2,1,0:T(8,128)(2,1)S(1)} %pad_maximum_fusion.1), channel_id=1, source_target_pairs={{0,2},{2,0},{4,6},{6,4},{1,3},{3,1},{5,7},{7,5},{8,10},{10,8},{12,... | collective-permute-start | bytes 36872 | tf_op jit(solution)/shard_map/ppermute | solution.py:354
  15.5 8.9 %collective-permute-start.2 = (bf16[2,8,384]{2,1,0:T(8,128)(2,1)S(1)}, bf16[2,8,384]{2,1,0:T(8,128)(2,1)S(1)}, u32[]{:S(2)}, u32[]{:S(2)}) collective-permute-start(bf16[2,8,384]{2,1,0:T(8,128)(2,1)S(1)} %pad_maximum_fusion.2), channel_id=1, source_target_pairs={{0,4},{2,6},{4,0},{6,2},{1,5},{3,7},{5,1},{7,3},{8,12},{10,14},{12... | collective-permute-start | bytes 36872 | tf_op jit(solution)/shard_map/ppermute | solution.py:354
  17.0 7.4 %collective-permute-start.3 = (bf16[2,8,384]{2,1,0:T(8,128)(2,1)S(1)}, bf16[2,8,384]{2,1,0:T(8,128)(2,1)S(1)}, u32[]{:S(2)}, u32[]{:S(2)}) collective-permute-start(bf16[2,8,384]{2,1,0:T(8,128)(2,1)S(1)} %pad_maximum_fusion.3), channel_id=1, source_target_pairs={{0,6},{2,4},{4,2},{6,0},{1,7},{3,5},{5,3},{7,1},{8,14},{10,12},{12... | collective-permute-start | bytes 36872 | tf_op jit(solution)/shard_map/ppermute | solution.py:354
  24.4 0.6 copy-start.9
  24.4 0.6 copy-start.10
  24.4 0.6 copy-start.11
  24.5 0.6 copy-start.3
  24.5 0.6 copy-start.6
  30.0 15.7 %all-to-all-start.1 = ((f32[16,24,128]{2,1,0:T(8,128)}), f32[16,24,128]{2,1,0:T(8,128)S(1)}, u32[]{:S(2)}, u32[]{:S(2)}) async-start(f32[16,24,128]{2,1,0:T(8,128)} %get-tuple-element.15), calls=%async_computation.1 | async-start | bytes 393216 | tf_op jit(solution)/shard_map/all_to_all | solution.py:380
  36.9 8.6 %collective-permute-start.5 = (bf16[8,3072]{1,0:T(8,128)(2,1)}, bf16[8,3072]{1,0:T(8,128)(2,1)S(1)}, u32[]{:S(2)}, u32[]{:S(2)}) collective-permute-start(bf16[8,3072]{1,0:T(8,128)(2,1)} %get-tuple-element.17), channel_id=1, source_target_pairs={{0,2},{2,0},{4,6},{6,4},{1,3},{3,1},{5,7},{7,5},{8,10},{10,8},{12,... | collective-permute-start | bytes 147464 | tf_op jit(solution)/shard_map/ppermute | solution.py:354
  38.7 6.7 %collective-permute-start.6 = (bf16[8,3072]{1,0:T(8,128)(2,1)}, bf16[8,3072]{1,0:T(8,128)(2,1)S(1)}, u32[]{:S(2)}, u32[]{:S(2)}) collective-permute-start(bf16[8,3072]{1,0:T(8,128)(2,1)} %get-tuple-element.18), channel_id=1, source_target_pairs={{0,4},{2,6},{4,0},{6,2},{1,5},{3,7},{5,1},{7,3},{8,12},{10,14},{12... | collective-permute-start | bytes 147464 | tf_op jit(solution)/shard_map/ppermute | solution.py:354
  40.2 5.5 %collective-permute-start.7 = (bf16[8,3072]{1,0:T(8,128)(2,1)}, bf16[8,3072]{1,0:T(8,128)(2,1)}, u32[]{:S(2)}, u32[]{:S(2)}) collective-permute-start(bf16[8,3072]{1,0:T(8,128)(2,1)} %get-tuple-element.19), channel_id=1, source_target_pairs={{0,6},{2,4},{4,2},{6,0},{1,7},{3,5},{5,3},{7,1},{8,14},{10,12},{12... | collective-permute-start | bytes 147464 | tf_op jit(solution)/shard_map/ppermute | solution.py:354
  41.0 16.0 %copy-start.12 = (s32[256]{0:T(256)S(1)}, s32[256]{0:T(256)}, u32[]{:S(2)}) copy-start(s32[256]{0:T(256)} %param.19) | copy-start | bytes 3076
  41.0 16.1 %copy-start.5 = (f32[256,1]{1,0:T(8,128)S(1)}, f32[256,1]{1,0:T(8,128)}, u32[]{:S(2)}) copy-start(f32[256,1]{1,0:T(8,128)} %get-tuple-element.20) | copy-start | bytes 3076
  41.0 16.8 %copy-start.4 = (s32[32,1,128]{2,1,0:T(1,128)S(1)}, s32[32,1,128]{2,1,0:T(1,128)}, u32[]{:S(2)}) copy-start(s32[32,1,128]{2,1,0:T(1,128)} %copy-done.3) | copy-start | bytes 49156
  45.4 0.6 copy-start.7
  45.4 0.6 copy-start.8
  45.7 0.7 copy-start.2
  51.5 16.1 %all-to-all-start.2 = ((bf16[32,32,128]{2,1,0:T(8,128)(2,1)}), bf16[32,32,128]{2,1,0:T(8,128)(2,1)S(1)}, u32[]{:S(2)}, u32[]{:S(2)}) async-start(bf16[32,32,128]{2,1,0:T(8,128)(2,1)} %shard_map.140), calls=%async_computation.2 | async-start | bytes 524288 | tf_op jit(solution)/shard_map/all_to_all | solution.py:388
  67.6 0.7 copy-start

commit v2 on v0

v2 whole, which is shorter than its diff:
```python
import functools
import math

import jax
import jax.numpy as jnp
from jax import lax
from jax.experimental import pallas as pl
from jax.experimental.pallas import tpu as pltpu
from jax.sharding import Mesh, PartitionSpec as P

EPSILON = 1e-06
BF16 = jnp.bfloat16
F32 = jnp.float32
I32 = jnp.int32
LANES = 128
MIB = 1024 * 1024
NT = (((1,), (1,)), ((), ()))
TN = (((0,), (0,)), ((), ()))
EVERYONE = ("dp", "chip", "core")
CLASS = ("dp", "chip")


def dot(a, b):
    return jnp.dot(a, b, preferred_element_type=F32)


def dot_nt(a, b):
    return lax.dot_general(a, b, NT, preferred_element_type=F32)


def dot_tn(a, b):
    return lax.dot_general(a, b, TN, preferred_element_type=F32)


def split_bf16(x):
    high = x.astype(BF16)
    return high, (x - high.astype(F32)).astype(BF16)


def iota(shape, axis):
    return lax.broadcasted_iota(I32, shape, axis)


def hold(x):
    return ("hold", x)


def late(x, chunks, axis=1):
    return ("late", x, chunks, axis)


def scalar(x):
    return ("scalar", x)


def call(body, operands, results, scratch=(), vmem=62, flops=2_000_000_000):
    arrays = [o[1] for o in operands]
    shapes = [jax.ShapeDtypeStruct(*r) for r in results]
    n_in, n_out = len(arrays), len(shapes)
    counts = [o[2] if o[0] == "late" else 1 for o in operands]
    offsets = [sum(counts[:i]) for i in range(n_in)]
    n_sems = sum(counts) + n_out

    def kernel(*refs):
        ins, outs = refs[:n_in], refs[n_in : n_in + n_out]
        held, made = refs[n_in + n_out : 2 * n_in + n_out], refs[2 * n_in + n_out : 2 * n_in + 2 * n_out]
        sems, extra = refs[2 * (n_in + n_out)], refs[2 * (n_in + n_out) + 1 :]

        def copies_of(i):
            o = operands[i]
            if o[0] != "late" or o[2] == 1:
                return [pltpu.make_async_copy(ins[i], held[i], sems.at[offsets[i]])]
            size = o[1].shape[o[3]] // o[2]
            cut = lambda k: tuple([slice(None)] * o[3] + [pl.ds(k * size, size)])
            return [
                pltpu.make_async_copy(ins[i].at[cut(k)], held[i].at[cut(k)], sems.at[offsets[i] + k])
                for k in range(o[2])
            ]

        copies = [copies_of(i) for i in range(n_in)]
        first = [c for i in range(n_in) if operands[i][0] != "late" for c in copies[i]]
        then = [i for i in range(n_in) if operands[i][0] == "late"]
        for c in first:
            c.start()
        for k in range(max([counts[i] for i in then], default=0)):
            for i in then:
                if k < counts[i]:
                    copies[i][k].start()
        for c in first:
            c.wait()
        given = [
            (held[i], lambda k, i=i: copies[i][k].wait()) if operands[i][0] == "late" else held[i]
            for i in range(n_in)
        ]
        body(given, made, extra)
        final = [
            pltpu.make_async_copy(m, out, sems.at[sum(counts) + k])
            for k, (m, out) in enumerate(zip(made, outs))
        ]
        for c in final:
            c.start()
        for c in final:
            c.wait()

    place = lambda o: pltpu.SMEM if o[0] == "scalar" else pltpu.VMEM
    return pl.pallas_call(
        kernel,
        in_specs=[pl.BlockSpec(memory_space=pltpu.HBM)] * n_in,
        out_specs=[pl.BlockSpec(memory_space=pltpu.HBM)] * n_out,
        out_shape=shapes,
        scratch_shapes=[place(o)(o[1].shape, o[1].dtype) for o in operands]
        + [pltpu.VMEM(s.shape, s.dtype) for s in shapes]
        + [pltpu.SemaphoreType.DMA((n_sems,))]
        + list(scratch),
        compiler_params=pltpu.CompilerParams(vmem_limit_bytes=vmem * MIB),
        cost_estimate=pl.CostEstimate(flops=flops, bytes_accessed=1024, transcendentals=0),
    )(*arrays)


def normalise(x):
    d = x - jnp.mean(x, -1, keepdims=True)
    rstd = lax.rsqrt(jnp.mean(d * d, -1, keepdims=True) + EPSILON)
    return d * rstd, rstd


def tokens_per_dp(sizes, tok_len):
    return -(-tok_len // sizes[0])


def packet_rows(per, n_core, width):
    need = -(-per * n_core * width // LANES) + 1
    return need, -(-need // 16) * 16


def pack_body(sizes, width, per, ins, outs, scratch):
    n_dp, n_chip, n_core = sizes
    ids, places, times, tokens = ins
    (out,), (held, flat) = outs, scratch
    tok_len = tokens.shape[0]
    need, rows = packet_rows(per, n_core, width)
    pieces = width // LANES
    held[...] = normalise(tokens[...].astype(F32))[0]
    flat[...] = jnp.zeros(flat.shape, F32)
    lane = iota((1, LANES), 1)
    values = (ids[0] // 64, lax.rem(ids[0], 64), places[0], times[0])
    label = jnp.zeros((1, LANES), F32)
    for i, x in enumerate(values):
        label = jnp.where(lane == i, x.astype(F32), label)
    core = lax.axis_index("core")
    for d in range(n_dp):
        for chip in range(n_chip):
            base = (d * n_chip + chip) * rows
            flat[base + need - 1 : base + need, :] = label
            for i in range(per):
                t = d * per + i
                for p in range(n_core if t < tok_len else 0):
                    at = (chip * n_core + (core ^ p)) * width
                    for k in range(pieces):
                        r = base + (i * n_core + p) * pieces + k
                        lanes = pl.ds(pl.multiple_of(at + k * LANES, LANES), LANES)
                        flat[r : r + 1, :] = held[t : t + 1, lanes]
    out[...] = flat[...].reshape(out.shape).astype(BF16)


def hat_body(ins, outs, scratch):
    outs[0][...] = normalise(ins[0][...].astype(F32))[0].astype(BF16)


def pack(ids, places, times, tokens, sizes, width):
    n_dp, n_chip, n_core = sizes
    n_all = n_dp * n_chip
    tok_len, model_width = tokens.shape
    per = tokens_per_dp(sizes, tok_len)
    need, rows = packet_rows(per, n_core, width)
    if width % LANES == 0:
        (out,) = call(
            functools.partial(pack_body, sizes, width, per),
            [scalar(ids), scalar(places), scalar(times), hold(tokens)],
            [((n_all, rows, LANES), BF16)],
            [pltpu.VMEM(tokens.shape, F32), pltpu.VMEM((n_all * rows, LANES), F32)],
        )
        return out
    (hat,) = call(hat_body, [hold(tokens)], [(tokens.shape, BF16)])
    hat = jnp.pad(hat, ((0, n_dp * per - tok_len), (0, 0)))
    hat = hat.reshape(n_dp, per, n_chip, n_core, width)
    core = lax.axis_index("core")
    own = [lax.dynamic_index_in_dim(hat, core ^ p, 3, keepdims=False) for p in range(n_core)]
    body = jnp.stack(own, 3).transpose(0, 2, 1, 3, 4).reshape(n_all, -1)
    body = jnp.pad(body, ((0, 0), (0, (need - 1) * LANES - body.shape[1])))
    label = jnp.stack([ids[0] // 64, ids[0] % 64, places[0], times[0]]).astype(BF16)
    label = jnp.broadcast_to(jnp.pad(label, (0, LANES - 4))[None], (n_all, LANES))
    out = jnp.concatenate([body, label], 1).reshape(n_all, need, LANES)
    return jnp.pad(out, ((0, 0), (0, rows - need), (0, 0)))


def table_body(width, n_core, ins, outs, scratch):
    (table, wait), mods, parts = ins[0], ins[1 : 1 + n_core], ins[1 + n_core :]
    hats, rstd_out, mod_outs = outs[:n_core], outs[n_core], outs[n_core + 1 :]
    chip, core = lax.axis_index("chip"), lax.axis_index("core")
    for mod, out in zip(mods, mod_outs):
        x = mod[...].astype(F32)
        out[0] = x[:, 0, :].astype(BF16)
        out[1] = x[:, 1, :].astype(BF16)
    rows = table.shape[0]
    block = rows // 4
    for i in range(4):
        wait(i)
        here = slice(i * block, (i + 1) * block)
        x = table[here, :].astype(F32)
        mean = jnp.mean(x, -1, keepdims=True)
        d = x - mean
        rstd = lax.rsqrt(jnp.mean(d * d, -1, keepdims=True) + EPSILON)
        rstd_out[here, :] = rstd
        for p in range(n_core):
            if parts:
                piece = parts[p][here, :]
            else:
                at = pl.multiple_of((chip * n_core + (core ^ p)) * width, LANES)
                piece = table[here, pl.ds(at, width)]
            hats[p][here, :] = ((piece.astype(F32) - mean) * rstd).astype(BF16)


def table_part(table, mods, width, n_core):
    rows = table.shape[0]
    buckets = mods[0].shape[0]
    parts = []
    if width % LANES:
        chip, core = lax.axis_index("chip"), lax.axis_index("core")
        cut = lambda p: lax.dynamic_slice_in_dim(table, (chip * n_core + (core ^ p)) * width, width, 1)
        parts = [hold(cut(p)) for p in range(n_core)]
    out = call(
        functools.partial(table_body, width, n_core),
        [late(table, 4, 0)] + [hold(m) for m in mods] + parts,
        [((rows, width), BF16)] * n_core + [((rows, 1), F32)] + [((2, buckets, width), BF16)] * n_core,
    )
    return out[:n_core], out[n_core], out[n_core + 1 :]


def image_body(head_dim, chunks, ins, outs, scratch):
    (q, _), (k, _), (v, _), (g, _) = ins
    (out,) = outs
    scale = 1.0 / math.sqrt(head_dim)
    heads = out.shape[0]
    for h in range(heads):
        if h % (heads // chunks) == 0:
            for _, wait in ins:
                wait(h // (heads // chunks))
        cols = slice(h * head_dim, (h + 1) * head_dim)
        s = dot_nt(k[:, cols], q[:, cols]) * scale
        gv = dot_nt(v[:, cols], g[:, cols])
        top = jnp.max(s, 0, keepdims=True)
        e = jnp.exp(s - top)
        out[h, 0:1, :] = top
        out[h, 1:2, :] = jnp.sum(e, 0, keepdims=True)
        out[h, 2:3, :] = jnp.sum(e * gv, 0, keepdims=True)


def image_part(q, k, v, g, head_dim):
    rows, width = q.shape
    heads = width // head_dim
    chunks = math.gcd(heads, 4)
    (out,) = call(
        functools.partial(image_body, head_dim, chunks),
        [late(x, chunks) for x in (q, k, v, g)],
        [((heads, 8, rows), F32)],
    )
    return out


def project_body(sizes, conc_dev, head_dim, per, chunks, ins, outs, scratch):
    n_dp, n_chip, n_core = sizes
    n_all = n_dp * n_chip
    mods, hats = ins[:n_core], ins[n_core : 2 * n_core]
    weights = ins[2 * n_core : 3 * n_core]
    given = ins[3 * n_core :]
    (out,), (lhs, flat, flat_in) = outs, scratch
    width, kv_width = weights[0][0].shape
    buckets = mods[0].shape[1]
    my_dp = lax.axis_index("dp")
    if len(given) == 1:
        need, rows = packet_rows(per, n_core, width)
        pieces = width // LANES
        flat_in[...] = given[0][...].reshape(n_all * rows, LANES).astype(F32)
        row = lambda r: flat_in[pl.ds(r, n_all, stride=rows), :]
        labels = row(need - 1)
        token = lambda i, p: jnp.concatenate(
            [row((i * n_core + p) * pieces + k) for k in range(pieces)], 1
        )
    else:
        labels = given[1][...].astype(F32)
        token = lambda i, p: given[0][i, p].astype(F32)
    label = lambda i: labels[:, i : i + 1].astype(I32)
    ids, times = label(0) * 64 + label(1), label(3)
    pick_time = (iota((n_all, buckets), 1) == times).astype(BF16)
    pick_row = (iota((n_all, conc_dev), 1) == ids - my_dp * conc_dev).astype(BF16)

    def owned_by(step):
        first = lax.rem(my_dp + n_dp - step, n_dp) * conc_dev
        return (ids >= first) & (ids < first + conc_dev)

    for p in range(n_core):
        shift, scale = dot(pick_time, mods[p][0]), 1.0 + dot(pick_time, mods[p][1])
        conc = scale * dot(pick_row, hats[p][...]) + shift
        first = jnp.where(
            owned_by(0), conc, jnp.where(owned_by(1), scale, jnp.where(owned_by(2), shift, 0.0))
        )
        lhs[p, 0:n_all] = first.astype(BF16)
        for i in range(per):
            rows_i = slice((1 + i) * n_all, (2 + i) * n_all)
            lhs[p, rows_i] = (scale * token(i, p) + shift).astype(BF16)
    slots = 1 + per
    kv_rows = kv_width // head_dim
    block = math.gcd(kv_width // chunks, 4 * head_dim)
    for at in range(0, kv_width, block):
        if at % (kv_width // chunks) == 0:
            for _, wait in weights:
                wait(at // (kv_width // chunks))
        cols = slice(at, at + block)
        terms = dot(lhs[0], weights[0][0][:, cols])
        for p in range(1, n_core):
            terms += dot(lhs[p], weights[p][0][:, cols])
        for s in range(slots):
            for r in range(block // head_dim):
                to = pl.ds(s * kv_rows + at // head_dim + r, n_all, stride=slots * kv_rows)
                flat[to, :] = terms[s * n_all : (s + 1) * n_all, r * head_dim : (r + 1) * head_dim]
    out[...] = flat[...].reshape(out.shape).astype(BF16)


def project(packets, mods, hats, weights, sizes, head_dim, tok_len):
    n_dp, n_chip, n_core = sizes
    width, kv_width = weights[0].shape
    per = tokens_per_dp(sizes, tok_len)
    need, rows = packet_rows(per, n_core, width)
    n_all = n_dp * n_chip
    slots, kv_rows = 1 + per, kv_width // head_dim
    chunks = 3
    given = [hold(packets)]
    if width % LANES:
        body = packets[:, : need - 1].reshape(n_all, -1)[:, : per * n_core * width]
        body = body.reshape(n_all, per, n_core, width).transpose(1, 2, 0, 3)
        given = [hold(body), hold(packets[:, need - 1])]
    (out,) = call(
        functools.partial(project_body, sizes, hats[0].shape[0], head_dim, per, chunks),
        [hold(x) for x in (*mods, *hats)] + [late(w, chunks) for w in weights] + given,
        [((n_all, slots * kv_rows, head_dim), BF16)],
        [
            pltpu.VMEM((n_core, slots * n_all, width), BF16),
            pltpu.VMEM((n_all * slots * kv_rows, head_dim), F32),
            pltpu.VMEM((n_all * rows, LANES), F32),
        ],
    )
    return out


def sample_body(sizes, tok_len, conc_dev, model_width, ins, outs, scratch):
    ids_ref, place_ref, time_ref, terms, bias, gain_ref, stat_ref = ins[:7]
    (q, q_wait), (g, g_wait) = ins[7:]
    (out,), (firsts, toks) = outs, scratch
    n_dp, n_chip, _ = sizes
    heads, _, img_len = stat_ref.shape
    kv_rows, head_dim = bias.shape
    per = tokens_per_dp(sizes, tok_len)
    scale = 1.0 / math.sqrt(head_dim)
    owner = jnp.int32(0)
    for d in range(1, n_dp):
        owner += (ids_ref[0] >= d * conc_dev).astype(I32)
    for d in range(n_dp):
        total = terms[d * n_chip].astype(F32)
        for s in range(1, n_chip):
            total += terms[d * n_chip + s].astype(F32)
        firsts[d * kv_rows : (d + 1) * kv_rows, :] = total[:kv_rows]
        for i in range(per):
            t = d * per + i
            if t < tok_len:
                toks[t * kv_rows : (t + 1) * kv_rows, :] = total[(1 + i) * kv_rows : (2 + i) * kv_rows]

    def gathered(step):
        at = lax.rem(owner + step, n_dp) * kv_rows
        return firsts[pl.ds(pl.multiple_of(at, 8), kv_rows), :]

    conc, scale_sum, shift_sum = gathered(0), gathered(1), gathered(2)
    full = conc + bias[...]
    raw_pos = full[:heads]
    inv_pos = lax.rsqrt(jnp.mean(raw_pos * raw_pos, -1, keepdims=True) + EPSILON)
    gain = gain_ref[...]
    at_pos = iota((tok_len, 1), 0) == place_ref[0]

    def text_rows(r):
        part = toks[pl.ds(r, tok_len, stride=kv_rows), :] + bias[r : r + 1, :]
        return jnp.where(at_pos, full[r : r + 1], part)

    keys, vals = [], []
    for h in range(heads):
        raw = text_rows(h)
        inv = lax.rsqrt(jnp.mean(raw * raw, -1, keepdims=True) + EPSILON)
        keys.append((raw * inv * gain).astype(BF16))
        vals.append(text_rows(heads + h).astype(BF16))
    q_wait(0)
    g_wait(0)
    cols = lambda h: slice(h * head_dim, (h + 1) * head_dim)
    shape = (heads, tok_len, img_len)
    s = jnp.concatenate([dot_nt(keys[h], q[:, cols(h)]) for h in range(heads)], 0)
    gv = jnp.concatenate([dot_nt(vals[h], g[:, cols(h)]) for h in range(heads)], 0)
    s, gv = s.reshape(shape) * scale, gv.reshape(shape)
    stats = stat_ref[...]
    top, total, weighted = stats[:, 0:1, :], stats[:, 1:2, :], stats[:, 2:3, :]
    new_top = jnp.maximum(top, jnp.max(s, 1, keepdims=True))
    e = jnp.exp(s - new_top)
    keep = jnp.exp(top - new_top)
    inv_total = 1.0 / (total * keep + jnp.sum(e, 1, keepdims=True))
    delta = (weighted * keep + jnp.sum(e * gv, 1, keepdims=True)) * inv_total
    here = iota((1, tok_len, 1), 1) == place_ref[0]
    p = jnp.sum(jnp.where(here, e, 0.0), 1, keepdims=True) * inv_total
    dscore = p * (jnp.sum(jnp.where(here, gv, 0.0), 1, keepdims=True) - delta)
    row = iota((1, 8, 1), 1)

    def two_rows(x):
        high = x.astype(BF16).astype(F32)
        return jnp.where(row == 0, high, jnp.where(row == 1, x - high, 0.0)).astype(BF16)

    p2, d2 = two_rows(p), two_rows(dscore)
    val_rows = [jnp.sum(dot(p2[h], g[:, cols(h)]), 0, keepdims=True) for h in range(heads)]
    key_rows = [jnp.sum(dot(d2[h], q[:, cols(h)]), 0, keepdims=True) for h in range(heads)]
    dn = jnp.concatenate(key_rows, 0) * scale * gain
    normed = raw_pos * inv_pos
    draw = inv_pos * (dn - normed * jnp.mean(dn * normed, -1, keepdims=True))
    dkv = jnp.concatenate([draw] + val_rows, 0)

    def total_of(x):
        return jnp.sum(jnp.sum(x, 0, keepdims=True), 1, keepdims=True) * (1.0 / model_width)

    means = split_bf16(total_of(dkv * scale_sum)) + split_bf16(total_of(dkv * (conc - shift_sum)))
    labels = (ids_ref[0] // 64, lax.rem(ids_ref[0], 64), time_ref[0])
    lane = iota((8, head_dim), 1)
    side = jnp.zeros((8, head_dim), F32)
    for i, x in enumerate(means + labels):
        side = jnp.where(lane == i, x.astype(F32), side)
    packet = jnp.concatenate([dkv, side], 0).astype(BF16)
    out[...] = jnp.broadcast_to(packet[None], out.shape)


def sample_part(ids, places, times, terms, bias, gain, stats, q, g, sizes, tok_len, conc_dev, model_width):
    kv_rows, head_dim = bias.shape
    per = tokens_per_dp(sizes, tok_len)
    (out,) = call(
        functools.partial(sample_body, sizes, tok_len, conc_dev, model_width),
        [scalar(ids), scalar(places), scalar(times), hold(terms), hold(bias), hold(gain), hold(stats)]
        + [late(q, 1), late(g, 1)],
        [((math.prod(sizes), kv_rows + 8, head_dim), BF16)],
        [
            pltpu.VMEM((sizes[0] * kv_rows, head_dim), F32),
            pltpu.VMEM((tok_len * kv_rows, head_dim), F32),
        ],
    )
    return out


def owner_body(chunks, ins, outs, scratch):
    packets, mod, hat, coef, (weight, wait) = ins
    (out,), (flat,) = outs, scratch
    n_dev, rows, head_dim = packets.shape
    conc_dev, buckets = hat.shape[0], mod.shape[1]
    parts = weight.shape[1] // head_dim
    first = lax.axis_index("dp") * conc_dev
    flat[...] = packets[...].reshape(n_dev * rows, head_dim).astype(F32)
    piece = lambda r: flat[pl.ds(r, n_dev, stride=rows), :]
    side = piece(parts)
    column = lambda i: side[:, i : i + 1]
    mean_1, mean_2 = column(0) + column(1), column(2) + column(3)
    mine = column(4).astype(I32) * 64 + column(5).astype(I32) - first
    times = column(6).astype(I32)
    scale = 1.0 + dot((iota((n_dev, buckets), 1) == times).astype(BF16), mod[1])
    one_hot = (iota((n_dev, conc_dev), 1) == mine).astype(BF16)
    conc = dot(one_hot, hat[...])
    size = parts // chunks
    grad = jnp.zeros(scale.shape, F32)
    for i in range(chunks):
        wait(i)
        dkv = jnp.concatenate([piece(r).astype(BF16) for r in range(i * size, (i + 1) * size)], 1)
        grad += dot_nt(dkv, weight[:, i * size * head_dim : (i + 1) * size * head_dim])
    grad = grad * scale - mean_1 - conc * mean_2
    high, low = split_bf16(grad)
    out[...] = (dot_tn(one_hot, high) + dot_tn(one_hot, low)) * coef[...]


def owner_part(packets, mod, hat, coef, weight):
    n_dev, rows, head_dim = packets.shape
    (out,) = call(
        functools.partial(owner_body, 3),
        [hold(x) for x in (packets, mod, hat, coef)] + [late(weight, 3)],
        [(hat.shape, F32)],
        [pltpu.VMEM((n_dev * rows, head_dim), F32)],
    )
    return out


def exchange(x, axes):
    return lax.all_to_all(x, axes, 0, 0, tiled=True)


def shards(
    txt_tokens,
    concept_table,
    concept_ids,
    positions,
    timesteps,
    counts,
    mod_table,
    kv_weight,
    kv_bias,
    key_gain,
    img_query,
    img_key,
    img_value,
    out_grad,
):
    sizes = tuple(lax.axis_size(a) for a in EVERYONE)
    n_dp, n_chip, n_core = sizes
    _, tok_len, model_width = txt_tokens.shape
    slice_width = kv_weight.shape[0]
    head_dim = key_gain.shape[0]
    conc_dev = concept_table.shape[0]

    def by_core(x):
        return [x] + [
            lax.ppermute(x, "core", [(i, i ^ s) for i in range(n_core)]) for s in range(1, n_core)
        ]

    packets = pack(concept_ids, positions, timesteps, txt_tokens[0], sizes, slice_width)
    packets = exchange(packets, CLASS)
    weights = by_core(kv_weight)
    hats, rstd, mods = table_part(concept_table, by_core(mod_table), slice_width, n_core)
    terms = project(packets, mods, hats, weights, sizes, head_dim, tok_len)
    terms = exchange(terms, CLASS)
    query, grad = img_query[0], out_grad[0]
    stats = image_part(query, img_key[0], img_value[0], grad, head_dim)
    packets = sample_part(
        concept_ids, positions, timesteps, terms, kv_bias.reshape(-1, head_dim), key_gain[None],
        stats, query, grad, sizes, tok_len, conc_dev, model_width,
    )
    packets = exchange(packets, EVERYONE)
    coef = rstd / counts.astype(F32)[:, None]
    return owner_part(packets, mods[0], hats[0], coef, kv_weight)


def solution(mesh):
    n_dp, n_fsdp = mesh.shape["dp"], mesh.shape["fsdp"]
    n_core = 2 if n_fsdp % 2 == 0 else 1
    fine = Mesh(mesh.devices.reshape(n_dp, n_fsdp // n_core, n_core), ("dp", "chip", "core"))
    fsdp = ("chip", "core")
    every = ("dp",) + fsdp
    placed = (
        P(every, None, None),
        P("dp", None),
        P(every),
        P(every),
        P(every),
        P("dp"),
        P(None, None, fsdp),
        P(fsdp, None),
        P(),
        P(),
        P(every, None, None),
        P(every, None, None),
        P(every, None, None),
        P(every, None, None),
    )
    return jax.shard_map(
        shards, mesh=fine, in_specs=placed, out_specs=P("dp", fsdp), check_vma=False
    )
```

time: 164 us -> 60.8 us (0.37)
  blocking collectives: 56.5 us -> 0 us
  Pallas kernels: 0 us -> 20.1 us
  local copies, waits for them, and re-layouts: 19 us -> 2.8 us
  waiting for transfers between devices: 34.9 us -> 19.6 us
  between operations: 17 us -> 2.06 us
  other arithmetic: 15 us -> 0.68 us
  matrix products: 11.9 us -> 0 us
  starting transfers between devices: 9.43 us -> 15 us
    all_gather x4 -> x0, blocking collectives: 49.8 us -> none  [the longest x1 19.8 us: shards(): table_all = lax.all_gather(table_part, 'dp', axis=0, tiled=True)]
    unnamed x2 -> x0, waiting for transfers between devices: 32.3 us -> none
    pallas_call x0 -> x6, Pallas kernels: none -> 20.1 us  [call(): pl.pallas_call(kernel, in_specs=[pl.BlockSpec(memory_space=pltpu.HBM)] *...]
    all_to_all x2 -> x3, waiting for transfers between devices: 2.58 us -> 19.6 us  [exchange(): return lax.all_to_all(x, axes, 0, 0, tiled=True)]
    dot_general x12 -> x0, matrix products: 11.6 us -> none  [the longest x1 1.92 us: shards(): grad_cols = jnp.dot(grads_all, weight_f.T, precision=highest) * scale_cols]
    concatenate x4 -> x0, local copies, waits for them, and re-layouts: 8.75 us -> none  [the longest x2 4.4 us: shards(): jnp.concatenate([key_norm, img_key[0]], 0)]
    unnamed x1 -> x0, blocking collectives: 6.68 us -> none
    all_to_all x2 -> x3, starting transfers between devices: 9.4 us -> 14.5 us  [exchange(): return lax.all_to_all(x, axes, 0, 0, tiled=True)]
  transfers between devices with their start and end apart: 3 -> 5, of which waited for: 2 -> 3; matrix products, arithmetic and copies ran while one was open for 14% -> 1% of each run, Pallas kernels for 0% -> 15%
where the time goes in v2:
time: 60.8 us; the launch traced here: 60.3 us
  Pallas kernels  20.1 us (33%)
  waiting for transfers between devices  19.6 us (32%)
  starting transfers between devices  15 us (25%)
  local copies, waits for them, and re-layouts  2.8 us (5%)
  between operations  2.06 us (3%)
  other arithmetic  0.68 us (1%)
    pallas_call x6, Pallas kernels, call(): pl.pallas_call(kernel, in_specs=[pl.BlockSpec(memory_space=pltpu.HBM)] *...  20.1 us
    all_to_all x3, waiting for transfers between devices, exchange(): return lax.all_to_all(x, axes, 0, 0, tiled=True)  19.6 us
    all_to_all x3, starting transfers between devices, exchange(): return lax.all_to_all(x, axes, 0, 0, tiled=True)  14.5 us
    unnamed x12, local copies, waits for them, and re-layouts  2.67 us
  transfers between devices with their start and end apart: 5, of which 3 were waited for; matrix products, arithmetic and copies ran while one was open for 1% of the time, Pallas kernels for 15%

profile of v2, /device:TPU:0, one launch (start us, length us, event | category | flops | bytes accessed | tf_op | source)
XLA Modules:
  0.0 60.3 jit_solution(8491314404475687534)
XLA Ops:
  0.0 0.5 collective-permute-start.1
  0.5 0.1 collective-permute-start
  2.5 1.8 %shard_map.137 = bf16[16,16,128]{2,1,0:T(8,128)(2,1)} custom-call(s32[1]{0:T(128)S(6)} %copy.16.refs_0_, s32[1]{0:T(128)S(6)} %copy.17.refs_1_, s32[1]{0:T(128)S(6)} %copy.18.refs_2_, bf16[8,3072]{1,0:T(8,128)(2,1)} %bitcast.15), custom_call_target="tpu_custom_call" | custom-call | flops 2000000000 | bytes 1024 | tf_op jit(solution)/shard_map/pallas_call | solution.py:106
  4.2 8.3 %all-to-all-start = ((bf16[16,16,128]{2,1,0:T(8,128)(2,1)}), bf16[16,16,128]{2,1,0:T(8,128)(2,1)S(1)}, u32[]{:S(2)}, u32[]{:S(2)}) async-start(bf16[16,16,128]{2,1,0:T(8,128)(2,1)} %shard_map.137), calls=%async_computation | async-start | bytes 131072 | tf_op jit(solution)/shard_map/all_to_all | solution.py:498
  12.5 0.0 collective-permute-done.refs_2_
  12.6 0.0 copy-start.5
  12.6 0.6 %copy-done.5 = bf16[64,2,384]{2,1,0:T(2,128)(2,1)} copy-done((bf16[64,2,384]{2,1,0:T(2,128)(2,1)}, bf16[64,2,384]{2,1,0:T(2,128)(2,1)S(1)}, u32[]{:S(2)}) %copy-start.5) | copy-done | bytes 98328
  13.2 3.5 %shard_map.136 = (bf16[256,384]{1,0:T(8,128)(2,1)}, bf16[256,384]{1,0:T(8,128)(2,1)}, f32[256,1]{1,0:T(8,128)}, bf16[2,64,384]{2,1,0:T(8,128)(2,1)}, bf16[2,64,384]{2,1,0:T(8,128)(2,1)}) custom-call(bf16[256,3072]{1,0:T(8,128)(2,1)} %refs_0_.3, bf16[64,2,384]{2,1,0:T(2,128)(2,1)} %refs_1_.3, bf16[64,2,384]{2,1,0:T(2,128)(2,1)} %copy-done.5), custom_call_target="tpu_custom_call" | custom-call | flops 2000000000 | bytes 1024 | tf_op jit(solution)/shard_map/pallas_call | solution.py:106
  16.8 3.3 %all-to-all-done.refs_6_ = bf16[16,16,128]{2,1,0:T(8,128)(2,1)S(1)} async-done(((bf16[16,16,128]{2,1,0:T(8,128)(2,1)}), bf16[16,16,128]{2,1,0:T(8,128)(2,1)S(1)}, u32[]{:S(2)}, u32[]{:S(2)}) %all-to-all-start) | async-done | bytes 65568 | tf_op jit(solution)/shard_map/all_to_all | solution.py:498
  20.1 0.0 copy-start.3
  20.1 0.0 collective-permute-done.1.refs_5_
  20.1 0.6 %copy-done.3 = bf16[16,16,128]{2,1,0:T(8,128)(2,1)} copy-done((bf16[16,16,128]{2,1,0:T(8,128)(2,1)}, bf16[16,16,128]{2,1,0:T(8,128)(2,1)S(1)}, u32[]{:S(2)}) %copy-start.3) | copy-done | bytes 65560
  20.7 3.9 %shard_map.138 = bf16[16,72,128]{2,1,0:T(8,128)(2,1)} custom-call(bf16[2,64,384]{2,1,0:T(8,128)(2,1)} %get-tuple-element.10.refs_0_.refs_1_, bf16[2,64,384]{2,1,0:T(8,128)(2,1)} %get-tuple-element.11.refs_1_, bf16[256,384]{1,0:T(8,128)(2,1)} %get-tuple-element.12.refs_2_, bf16[256,384]{1,0:T(8,128)(2,1)} %get-tuple-element.13.refs_3_, ...), custom_call_target="tpu_custom_call" | custom-call | flops 2000000000 | bytes 1024 | tf_op jit(solution)/shard_map/pallas_call | solution.py:106
  24.6 3.6 %all-to-all-start.1 = ((bf16[16,72,128]{2,1,0:T(8,128)(2,1)}), bf16[16,72,128]{2,1,0:T(8,128)(2,1)S(1)}, u32[]{:S(2)}, u32[]{:S(2)}) async-start(bf16[16,72,128]{2,1,0:T(8,128)(2,1)} %shard_map.138), calls=%async_computation.1 | async-start | bytes 589824 | tf_op jit(solution)/shard_map/all_to_all | solution.py:498
  28.2 3.8 %shard_map.139.refs_6_ = f32[12,8,192]{2,1,0:T(8,128)} custom-call(bf16[192,1536]{1,0:T(8,128)(2,1)} %bitcast.11, bf16[192,1536]{1,0:T(8,128)(2,1)} %bitcast.9, bf16[192,1536]{1,0:T(8,128)(2,1)} %bitcast.10, bf16[192,1536]{1,0:T(8,128)(2,1)} %bitcast.13), custom_call_target="tpu_custom_call" | custom-call | flops 2000000000 | bytes 1024 | tf_op jit(solution)/shard_map/pallas_call | solution.py:106
  32.0 6.5 %all-to-all-done.1.refs_3_ = bf16[16,72,128]{2,1,0:T(8,128)(2,1)S(1)} async-done(((bf16[16,72,128]{2,1,0:T(8,128)(2,1)}), bf16[16,72,128]{2,1,0:T(8,128)(2,1)S(1)}, u32[]{:S(2)}, u32[]{:S(2)}) %all-to-all-start.1) | async-done | bytes 294944 | tf_op jit(solution)/shard_map/all_to_all | solution.py:498
  38.5 0.0 copy-start
  38.5 0.7 %copy-done = bf16[16,72,128]{2,1,0:T(8,128)(2,1)} copy-done((bf16[16,72,128]{2,1,0:T(8,128)(2,1)}, bf16[16,72,128]{2,1,0:T(8,128)(2,1)S(1)}, u32[]{:S(2)}) %copy-start) | copy-done | bytes 294936
  39.2 0.0 copy-start.4
  39.2 0.0 copy-start.2
  39.2 3.5 %shard_map.140 = bf16[32,32,128]{2,1,0:T(8,128)(2,1)} custom-call(s32[1]{0:T(128)S(6)} %copy.16.refs_0_, s32[1]{0:T(128)S(6)} %copy.17.refs_1_, s32[1]{0:T(128)S(6)} %copy.18.refs_2_, bf16[16,72,128]{2,1,0:T(8,128)(2,1)} %copy-done, f32[24,128]{1,0:T(8,128)} %bitcast.16, f32[1,128]{1,0:T(1,128)} %bitcast.17, f32[12,8,192]{2,1,0:T(8,128)} %shard_map.139.refs_6_, ...), custom_call_target="tpu_custom_call" | custom-call | flops 2000000000 | bytes 1024 | tf_op jit(solution)/shard_map/pallas_call | solution.py:106
  42.7 2.6 %all-to-all-start.2 = ((bf16[32,32,128]{2,1,0:T(8,128)(2,1)}), bf16[32,32,128]{2,1,0:T(8,128)(2,1)S(1)}, u32[]{:S(2)}, u32[]{:S(2)}) async-start(bf16[32,32,128]{2,1,0:T(8,128)(2,1)} %shard_map.140), calls=%async_computation.2 | async-start | bytes 524288 | tf_op jit(solution)/shard_map/all_to_all | solution.py:498
  45.3 0.0 copy-done.4
  45.3 0.1 copy.15
  45.4 0.0 copy-done.2
  45.4 0.7 %div.3.refs_3_ = f32[256,1]{1,0:T(8,128)} divide(f32[256,1]{1,0:T(8,128)S(1)} %copy-done.2, f32[256,1]{1,0:T(8,128)S(1)} %copy.15) | non-fusion elementwise | flops 256 | bytes 3072 | tf_op jit(solution)/shard_map/div | solution.py:542
  46.1 9.7 %all-to-all-done.2.refs_0_ = bf16[32,32,128]{2,1,0:T(8,128)(2,1)S(1)} async-done(((bf16[32,32,128]{2,1,0:T(8,128)(2,1)}), bf16[32,32,128]{2,1,0:T(8,128)(2,1)S(1)}, u32[]{:S(2)}, u32[]{:S(2)}) %all-to-all-start.2) | async-done | bytes 262176 | tf_op jit(solution)/shard_map/all_to_all | solution.py:498
  55.9 0.0 copy-start.1
  55.9 0.7 %copy-done.1 = bf16[32,32,128]{2,1,0:T(8,128)(2,1)} copy-done((bf16[32,32,128]{2,1,0:T(8,128)(2,1)}, bf16[32,32,128]{2,1,0:T(8,128)(2,1)S(1)}, u32[]{:S(2)}) %copy-start.1) | copy-done | bytes 262168
  56.6 3.7 %shard_map.141 = f32[256,384]{1,0:T(8,128)} custom-call(bf16[32,32,128]{2,1,0:T(8,128)(2,1)} %copy-done.1, bf16[2,64,384]{2,1,0:T(8,128)(2,1)} %get-tuple-element.10.refs_0_.refs_1_, bf16[256,384]{1,0:T(8,128)(2,1)} %get-tuple-element.12.refs_2_, f32[256,1]{1,0:T(8,128)} %div.3.refs_3_, bf16[384,3072]{1,0:T(8,128)(2,1)} %refs_4_.3), custom_call_target="tpu_custom_call" | custom-call | flops 2000000000 | bytes 1024 | tf_op jit(solution)/shard_map/pallas_call | solution.py:106
  (1 shorter events, 0.0 us)
Async XLA Ops:
  0.0 20.1 %collective-permute-start.1 = (bf16[384,3072]{1,0:T(8,128)(2,1)}, bf16[384,3072]{1,0:T(8,128)(2,1)}, u32[]{:S(2)}, u32[]{:S(2)}) collective-permute-start(bf16[384,3072]{1,0:T(8,128)(2,1)} %refs_4_.3), channel_id=1, source_target_pairs={{0,1},{1,0},{2,3},{3,2},{4,5},{5,4},{6,7},{7,6},{8,9},{9,8},{10,11... | collective-permute-start | bytes 7077896 | tf_op jit(solution)/shard_map/ppermute | solution.py:526
  0.5 12.1 %collective-permute-start = (bf16[64,2,384]{2,1,0:T(2,128)(2,1)}, bf16[64,2,384]{2,1,0:T(2,128)(2,1)S(1)}, u32[]{:S(2)}, u32[]{:S(2)}) collective-permute-start(bf16[64,2,384]{2,1,0:T(2,128)(2,1)} %refs_1_.3), channel_id=1, source_target_pairs={{0,1},{1,0},{2,3},{3,2},{4,5},{5,4},{6,7},{7,6},{8,9},{9,8},{10,11... | collective-permute-start | bytes 294920 | tf_op jit(solution)/shard_map/ppermute | solution.py:526
  4.2 15.9 %all-to-all-start = ((bf16[16,16,128]{2,1,0:T(8,128)(2,1)}), bf16[16,16,128]{2,1,0:T(8,128)(2,1)S(1)}, u32[]{:S(2)}, u32[]{:S(2)}) async-start(bf16[16,16,128]{2,1,0:T(8,128)(2,1)} %shard_map.137), calls=%async_computation | async-start | bytes 131072 | tf_op jit(solution)/shard_map/all_to_all | solution.py:498
  12.6 0.6 %copy-start.5 = (bf16[64,2,384]{2,1,0:T(2,128)(2,1)}, bf16[64,2,384]{2,1,0:T(2,128)(2,1)S(1)}, u32[]{:S(2)}) copy-start(bf16[64,2,384]{2,1,0:T(2,128)(2,1)S(1)} %collective-permute-done.refs_2_) | copy-start | bytes 294916
  20.1 0.6 %copy-start.3 = (bf16[16,16,128]{2,1,0:T(8,128)(2,1)}, bf16[16,16,128]{2,1,0:T(8,128)(2,1)S(1)}, u32[]{:S(2)}) copy-start(bf16[16,16,128]{2,1,0:T(8,128)(2,1)S(1)} %all-to-all-done.refs_6_) | copy-start | bytes 196612
  24.6 13.9 %all-to-all-start.1 = ((bf16[16,72,128]{2,1,0:T(8,128)(2,1)}), bf16[16,72,128]{2,1,0:T(8,128)(2,1)S(1)}, u32[]{:S(2)}, u32[]{:S(2)}) async-start(bf16[16,72,128]{2,1,0:T(8,128)(2,1)} %shard_map.138), calls=%async_computation.1 | async-start | bytes 589824 | tf_op jit(solution)/shard_map/all_to_all | solution.py:498
  38.5 0.7 %copy-start = (bf16[16,72,128]{2,1,0:T(8,128)(2,1)}, bf16[16,72,128]{2,1,0:T(8,128)(2,1)S(1)}, u32[]{:S(2)}) copy-start(bf16[16,72,128]{2,1,0:T(8,128)(2,1)S(1)} %all-to-all-done.1.refs_3_) | copy-start | bytes 884740
  39.2 6.1 %copy-start.4 = (s32[256]{0:T(256)S(1)}, s32[256]{0:T(256)}, u32[]{:S(2)}) copy-start(s32[256]{0:T(256)} %param.19) | copy-start | bytes 3076
  39.2 6.2 %copy-start.2 = (f32[256,1]{1,0:T(8,128)S(1)}, f32[256,1]{1,0:T(8,128)}, u32[]{:S(2)}) copy-start(f32[256,1]{1,0:T(8,128)} %get-tuple-element.14) | copy-start | bytes 3076
  42.7 13.2 %all-to-all-start.2 = ((bf16[32,32,128]{2,1,0:T(8,128)(2,1)}), bf16[32,32,128]{2,1,0:T(8,128)(2,1)S(1)}, u32[]{:S(2)}, u32[]{:S(2)}) async-start(bf16[32,32,128]{2,1,0:T(8,128)(2,1)} %shard_map.140), calls=%async_computation.2 | async-start | bytes 524288 | tf_op jit(solution)/shard_map/all_to_all | solution.py:498
  55.9 0.7 %copy-start.1 = (bf16[32,32,128]{2,1,0:T(8,128)(2,1)}, bf16[32,32,128]{2,1,0:T(8,128)(2,1)S(1)}, u32[]{:S(2)}) copy-start(bf16[32,32,128]{2,1,0:T(8,128)(2,1)S(1)} %all-to-all-done.2.refs_0_) | copy-start | bytes 786436

commit v3 on v2

--- a/solution.py
+++ b/solution.py
@@ -14,6 +14,8 @@
 I32 = jnp.int32
 LANES = 128
 MIB = 1024 * 1024
+SPARE_ROWS = 128
+ROOM_FOR_ONE = 53.25
 NT = (((1,), (1,)), ((), ()))
 TN = (((0,), (0,)), ((), ()))
 EVERYONE = ("dp", "chip", "core")
@@ -45,6 +47,18 @@
     return ("hold", x)
 
 
+def part(x, *cut):
+    return ("part", x, cut)
+
+
+def cut_shape(shape, cut):
+    return tuple(c[1] for c in cut) + tuple(shape[len(cut) :])
+
+
+def cut_index(cut):
+    return tuple(pl.ds(*c) for c in cut)
+
+
 def late(x, chunks, axis=1):
     return ("late", x, chunks, axis)
 
@@ -53,9 +67,10 @@
     return ("scalar", x)
 
 
-def call(body, operands, results, scratch=(), vmem=62, flops=2_000_000_000):
+def call(body, operands, results, scratch=(), vmem=63, flops=2_000_000_000):
     arrays = [o[1] for o in operands]
-    shapes = [jax.ShapeDtypeStruct(*r) for r in results]
+    shapes = [jax.ShapeDtypeStruct(*r[:2]) for r in results]
+    cuts = [r[2] if len(r) > 2 else () for r in results]
     n_in, n_out = len(arrays), len(shapes)
     counts = [o[2] if o[0] == "late" else 1 for o in operands]
     offsets = [sum(counts[:i]) for i in range(n_in)]
@@ -68,6 +83,8 @@
 
         def copies_of(i):
             o = operands[i]
+            if o[0] == "part":
+                return [pltpu.make_async_copy(ins[i].at[cut_index(o[2])], held[i], sems.at[offsets[i]])]
             if o[0] != "late" or o[2] == 1:
                 return [pltpu.make_async_copy(ins[i], held[i], sems.at[offsets[i]])]
             size = o[1].shape[o[3]] // o[2]
@@ -94,25 +111,28 @@
         ]
         body(given, made, extra)
         final = [
-            pltpu.make_async_copy(m, out, sems.at[sum(counts) + k])
-            for k, (m, out) in enumerate(zip(made, outs))
+            pltpu.make_async_copy(m, out.at[cut_index(c)] if c else out, sems.at[sum(counts) + k])
+            for k, (m, out, c) in enumerate(zip(made, outs, cuts))
         ]
         for c in final:
             c.start()
         for c in final:
             c.wait()
 
-    place = lambda o: pltpu.SMEM if o[0] == "scalar" else pltpu.VMEM
+    def place(o):
+        shape = cut_shape(o[1].shape, o[2]) if o[0] == "part" else o[1].shape
+        return (pltpu.SMEM if o[0] == "scalar" else pltpu.VMEM)(shape, o[1].dtype)
+
     return pl.pallas_call(
         kernel,
         in_specs=[pl.BlockSpec(memory_space=pltpu.HBM)] * n_in,
         out_specs=[pl.BlockSpec(memory_space=pltpu.HBM)] * n_out,
         out_shape=shapes,
-        scratch_shapes=[place(o)(o[1].shape, o[1].dtype) for o in operands]
-        + [pltpu.VMEM(s.shape, s.dtype) for s in shapes]
+        scratch_shapes=[place(o) for o in operands]
+        + [pltpu.VMEM(cut_shape(s.shape, c), s.dtype) for s, c in zip(shapes, cuts)]
         + [pltpu.SemaphoreType.DMA((n_sems,))]
         + list(scratch),
-        compiler_params=pltpu.CompilerParams(vmem_limit_bytes=vmem * MIB),
+        compiler_params=pltpu.CompilerParams(vmem_limit_bytes=int(vmem * MIB)),
         cost_estimate=pl.CostEstimate(flops=flops, bytes_accessed=1024, transcendentals=0),
     )(*arrays)
 
@@ -134,7 +154,7 @@
 
 def pack_body(sizes, width, per, ins, outs, scratch):
     n_dp, n_chip, n_core = sizes
-    ids, places, times, tokens = ins
+    ids, times, tokens = ins
     (out,), (held, flat) = outs, scratch
     tok_len = tokens.shape[0]
     need, rows = packet_rows(per, n_core, width)
@@ -142,7 +162,7 @@
     held[...] = normalise(tokens[...].astype(F32))[0]
     flat[...] = jnp.zeros(flat.shape, F32)
     lane = iota((1, LANES), 1)
-    values = (ids[0] // 64, lax.rem(ids[0], 64), places[0], times[0])
+    values = (ids[0] // 64, lax.rem(ids[0], 64), times[0])
     label = jnp.zeros((1, LANES), F32)
     for i, x in enumerate(values):
         label = jnp.where(lane == i, x.astype(F32), label)
@@ -166,7 +186,7 @@
     outs[0][...] = normalise(ins[0][...].astype(F32))[0].astype(BF16)
 
 
-def pack(ids, places, times, tokens, sizes, width):
+def pack(ids, times, tokens, sizes, width):
     n_dp, n_chip, n_core = sizes
     n_all = n_dp * n_chip
     tok_len, model_width = tokens.shape
@@ -175,7 +195,7 @@
     if width % LANES == 0:
         (out,) = call(
             functools.partial(pack_body, sizes, width, per),
-            [scalar(ids), scalar(places), scalar(times), hold(tokens)],
+            [scalar(ids), scalar(times), hold(tokens)],
             [((n_all, rows, LANES), BF16)],
             [pltpu.VMEM(tokens.shape, F32), pltpu.VMEM((n_all * rows, LANES), F32)],
         )
@@ -187,21 +207,27 @@
     own = [lax.dynamic_index_in_dim(hat, core ^ p, 3, keepdims=False) for p in range(n_core)]
     body = jnp.stack(own, 3).transpose(0, 2, 1, 3, 4).reshape(n_all, -1)
     body = jnp.pad(body, ((0, 0), (0, (need - 1) * LANES - body.shape[1])))
-    label = jnp.stack([ids[0] // 64, ids[0] % 64, places[0], times[0]]).astype(BF16)
-    label = jnp.broadcast_to(jnp.pad(label, (0, LANES - 4))[None], (n_all, LANES))
+    label = jnp.stack([ids[0] // 64, ids[0] % 64, times[0]]).astype(BF16)
+    label = jnp.broadcast_to(jnp.pad(label, (0, LANES - 3))[None], (n_all, LANES))
     out = jnp.concatenate([body, label], 1).reshape(n_all, need, LANES)
     return jnp.pad(out, ((0, 0), (0, rows - need), (0, 0)))
 
 
+def bank_rows(conc_dev, buckets):
+    return conc_dev + 2 * buckets
+
+
 def table_body(width, n_core, ins, outs, scratch):
     (table, wait), mods, parts = ins[0], ins[1 : 1 + n_core], ins[1 + n_core :]
-    hats, rstd_out, mod_outs = outs[:n_core], outs[n_core], outs[n_core + 1 :]
+    bank, rstd_out = outs
     chip, core = lax.axis_index("chip"), lax.axis_index("core")
-    for mod, out in zip(mods, mod_outs):
+    rows, buckets = table.shape[0], mods[0].shape[0]
+    each = bank_rows(rows, buckets)
+    for p, mod in enumerate(mods):
         x = mod[...].astype(F32)
-        out[0] = x[:, 0, :].astype(BF16)
-        out[1] = x[:, 1, :].astype(BF16)
-    rows = table.shape[0]
+        for i in range(2):
+            at = p * each + rows + i * buckets
+            bank[at : at + buckets, :] = x[:, i, :].astype(BF16)
     block = rows // 4
     for i in range(4):
         wait(i)
@@ -217,7 +243,8 @@
             else:
                 at = pl.multiple_of((chip * n_core + (core ^ p)) * width, LANES)
                 piece = table[here, pl.ds(at, width)]
-            hats[p][here, :] = ((piece.astype(F32) - mean) * rstd).astype(BF16)
+            to = slice(p * each + i * block, p * each + (i + 1) * block)
+            bank[to, :] = ((piece.astype(F32) - mean) * rstd).astype(BF16)
 
 
 def table_part(table, mods, width, n_core):
@@ -228,12 +255,12 @@
         chip, core = lax.axis_index("chip"), lax.axis_index("core")
         cut = lambda p: lax.dynamic_slice_in_dim(table, (chip * n_core + (core ^ p)) * width, width, 1)
         parts = [hold(cut(p)) for p in range(n_core)]
-    out = call(
+    used = n_core * bank_rows(rows, buckets)
+    return call(
         functools.partial(table_body, width, n_core),
         [late(table, 4, 0)] + [hold(m) for m in mods] + parts,
-        [((rows, width), BF16)] * n_core + [((rows, 1), F32)] + [((2, buckets, width), BF16)] * n_core,
-    )
-    return out[:n_core], out[n_core], out[n_core + 1 :]
+        [((used + SPARE_ROWS, width), BF16, ((0, used),)), ((rows, 1), F32)],
+    )
 
 
 def image_body(head_dim, chunks, ins, outs, scratch):
@@ -262,7 +289,7 @@
     (out,) = call(
         functools.partial(image_body, head_dim, chunks),
         [late(x, chunks) for x in (q, k, v, g)],
-        [((heads, 8, rows), F32)],
+        [((heads, 8 + SPARE_ROWS // 2, rows), F32, ((0, heads), (0, 8)))],
     )
     return out
 
@@ -270,12 +297,11 @@
 def project_body(sizes, conc_dev, head_dim, per, chunks, ins, outs, scratch):
     n_dp, n_chip, n_core = sizes
     n_all = n_dp * n_chip
-    mods, hats = ins[:n_core], ins[n_core : 2 * n_core]
-    weights = ins[2 * n_core : 3 * n_core]
-    given = ins[3 * n_core :]
+    bank, weights, given = ins[0], ins[1 : 1 + n_core], ins[1 + n_core :]
     (out,), (lhs, flat, flat_in) = outs, scratch
     width, kv_width = weights[0][0].shape
-    buckets = mods[0].shape[1]
+    each = bank.shape[0] // n_core
+    buckets = (each - conc_dev) // 2
     my_dp = lax.axis_index("dp")
     if len(given) == 1:
         need, rows = packet_rows(per, n_core, width)
@@ -290,7 +316,7 @@
         labels = given[1][...].astype(F32)
         token = lambda i, p: given[0][i, p].astype(F32)
     label = lambda i: labels[:, i : i + 1].astype(I32)
-    ids, times = label(0) * 64 + label(1), label(3)
+    ids, times = label(0) * 64 + label(1), label(2)
     pick_time = (iota((n_all, buckets), 1) == times).astype(BF16)
     pick_row = (iota((n_all, conc_dev), 1) == ids - my_dp * conc_dev).astype(BF16)
 
@@ -299,8 +325,10 @@
         return (ids >= first) & (ids < first + conc_dev)
 
     for p in range(n_core):
-        shift, scale = dot(pick_time, mods[p][0]), 1.0 + dot(pick_time, mods[p][1])
-        conc = scale * dot(pick_row, hats[p][...]) + shift
+        at = p * each + conc_dev
+        shift = dot(pick_time, bank[at : at + buckets, :])
+        scale = 1.0 + dot(pick_time, bank[at + buckets : at + 2 * buckets, :])
+        conc = scale * dot(pick_row, bank[p * each : p * each + conc_dev, :]) + shift
         first = jnp.where(
             owned_by(0), conc, jnp.where(owned_by(1), scale, jnp.where(owned_by(2), shift, 0.0))
         )
@@ -326,7 +354,7 @@
     out[...] = flat[...].reshape(out.shape).astype(BF16)
 
 
-def project(packets, mods, hats, weights, sizes, head_dim, tok_len):
+def project(packets, bank, conc_dev, weights, sizes, head_dim, tok_len):
     n_dp, n_chip, n_core = sizes
     width, kv_width = weights[0].shape
     per = tokens_per_dp(sizes, tok_len)
@@ -340,14 +368,15 @@
         body = body.reshape(n_all, per, n_core, width).transpose(1, 2, 0, 3)
         given = [hold(body), hold(packets[:, need - 1])]
     (out,) = call(
-        functools.partial(project_body, sizes, hats[0].shape[0], head_dim, per, chunks),
-        [hold(x) for x in (*mods, *hats)] + [late(w, chunks) for w in weights] + given,
+        functools.partial(project_body, sizes, conc_dev, head_dim, per, chunks),
+        [part(bank, (0, bank.shape[0] - SPARE_ROWS))] + [late(w, chunks) for w in weights] + given,
         [((n_all, slots * kv_rows, head_dim), BF16)],
         [
             pltpu.VMEM((n_core, slots * n_all, width), BF16),
             pltpu.VMEM((n_all * slots * kv_rows, head_dim), F32),
             pltpu.VMEM((n_all * rows, LANES), F32),
         ],
+        vmem=ROOM_FOR_ONE,
     )
     return out
 
@@ -444,34 +473,41 @@
     per = tokens_per_dp(sizes, tok_len)
     (out,) = call(
         functools.partial(sample_body, sizes, tok_len, conc_dev, model_width),
-        [scalar(ids), scalar(places), scalar(times), hold(terms), hold(bias), hold(gain), hold(stats)]
+        [scalar(ids), scalar(places), scalar(times), hold(terms), hold(bias), hold(gain)]
+        + [part(stats, (0, stats.shape[0]), (0, 8))]
         + [late(q, 1), late(g, 1)],
-        [((math.prod(sizes), kv_rows + 8, head_dim), BF16)],
+        [((sizes[0] * sizes[1], kv_rows + 8, head_dim), BF16)],
         [
             pltpu.VMEM((sizes[0] * kv_rows, head_dim), F32),
             pltpu.VMEM((tok_len * kv_rows, head_dim), F32),
         ],
+        vmem=ROOM_FOR_ONE,
     )
     return out
 
 
 def owner_body(chunks, ins, outs, scratch):
-    packets, mod, hat, coef, (weight, wait) = ins
+    bank, coef, (weight, wait), packets = *ins[:3], ins[3:]
     (out,), (flat,) = outs, scratch
-    n_dev, rows, head_dim = packets.shape
-    conc_dev, buckets = hat.shape[0], mod.shape[1]
+    n_each, rows, head_dim = packets[0].shape
+    n_dev = n_each * len(packets)
+    conc_dev = coef.shape[0]
+    buckets = (bank.shape[0] - conc_dev) // 2
     parts = weight.shape[1] // head_dim
     first = lax.axis_index("dp") * conc_dev
-    flat[...] = packets[...].reshape(n_dev * rows, head_dim).astype(F32)
+    for i, x in enumerate(packets):
+        flat[i * n_each * rows : (i + 1) * n_each * rows, :] = (
+            x[...].reshape(n_each * rows, head_dim).astype(F32)
+        )
     piece = lambda r: flat[pl.ds(r, n_dev, stride=rows), :]
     side = piece(parts)
     column = lambda i: side[:, i : i + 1]
     mean_1, mean_2 = column(0) + column(1), column(2) + column(3)
     mine = column(4).astype(I32) * 64 + column(5).astype(I32) - first
     times = column(6).astype(I32)
-    scale = 1.0 + dot((iota((n_dev, buckets), 1) == times).astype(BF16), mod[1])
+    scale = 1.0 + dot((iota((n_dev, buckets), 1) == times).astype(BF16), bank[conc_dev + buckets :, :])
     one_hot = (iota((n_dev, conc_dev), 1) == mine).astype(BF16)
-    conc = dot(one_hot, hat[...])
+    conc = dot(one_hot, bank[0:conc_dev, :])
     size = parts // chunks
     grad = jnp.zeros(scale.shape, F32)
     for i in range(chunks):
@@ -483,13 +519,16 @@
     out[...] = (dot_tn(one_hot, high) + dot_tn(one_hot, low)) * coef[...]
 
 
-def owner_part(packets, mod, hat, coef, weight):
-    n_dev, rows, head_dim = packets.shape
+def owner_part(packets, bank, n_core, coef, weight):
+    each = (bank.shape[0] - SPARE_ROWS) // n_core
+    n_each, rows, head_dim = packets[0].shape
+    n_dev = n_each * len(packets)
     (out,) = call(
         functools.partial(owner_body, 3),
-        [hold(x) for x in (packets, mod, hat, coef)] + [late(weight, 3)],
-        [(hat.shape, F32)],
+        [part(bank, (0, each)), hold(coef), late(weight, 3)] + [hold(x) for x in packets],
+        [((coef.shape[0], weight.shape[0]), F32)],
         [pltpu.VMEM((n_dev * rows, head_dim), F32)],
+        vmem=ROOM_FOR_ONE,
     )
     return out
 
@@ -526,11 +565,11 @@
             lax.ppermute(x, "core", [(i, i ^ s) for i in range(n_core)]) for s in range(1, n_core)
         ]
 
-    packets = pack(concept_ids, positions, timesteps, txt_tokens[0], sizes, slice_width)
+    packets = pack(concept_ids, timesteps, txt_tokens[0], sizes, slice_width)
     packets = exchange(packets, CLASS)
     weights = by_core(kv_weight)
-    hats, rstd, mods = table_part(concept_table, by_core(mod_table), slice_width, n_core)
-    terms = project(packets, mods, hats, weights, sizes, head_dim, tok_len)
+    bank, rstd = table_part(concept_table, by_core(mod_table), slice_width, n_core)
+    terms = project(packets, bank, conc_dev, weights, sizes, head_dim, tok_len)
     terms = exchange(terms, CLASS)
     query, grad = img_query[0], out_grad[0]
     stats = image_part(query, img_key[0], img_value[0], grad, head_dim)
@@ -538,9 +577,9 @@
         concept_ids, positions, timesteps, terms, kv_bias.reshape(-1, head_dim), key_gain[None],
         stats, query, grad, sizes, tok_len, conc_dev, model_width,
     )
-    packets = exchange(packets, EVERYONE)
+    packets = by_core(exchange(packets, CLASS))
     coef = rstd / counts.astype(F32)[:, None]
-    return owner_part(packets, mods[0], hats[0], coef, kv_weight)
+    return owner_part(packets, bank, n_core, coef, kv_weight)
 
 
 def solution(mesh):

time: 60.8 us -> 56.7 us (0.933)
  blocking collectives: 0 us -> 11 us
  waiting for transfers between devices: 19.6 us -> 10.3 us
  starting transfers between devices: 15 us -> 12.4 us
  local copies, waits for them, and re-layouts: 2.8 us -> 0.79 us
  other arithmetic: 0.68 us -> 0.03 us
    all_to_all x0 -> x1, blocking collectives: none -> 11 us  [exchange(): return lax.all_to_all(x, axes, 0, 0, tiled=True)]
    all_to_all x3 -> x2, waiting for transfers between devices: 19.6 us -> 9.16 us  [exchange(): return lax.all_to_all(x, axes, 0, 0, tiled=True)]
    all_to_all x3 -> x2, starting transfers between devices: 14.5 us -> 11.9 us  [exchange(): return lax.all_to_all(x, axes, 0, 0, tiled=True)]
    unnamed x12 -> x10, local copies, waits for them, and re-layouts: 2.67 us -> 0.66 us
    ppermute x2 -> x3, waiting for transfers between devices: 0.01 us -> 1.16 us  [by_core(): lax.ppermute(x, 'core', [(i, i ^ s) for i in range(n_core)])]
    div x1, other arithmetic: 0.68 us -> 0.03 us  [shards(): coef = rstd / counts.astype(F32)[:, None]]
  transfers between devices with their start and end apart: 5 -> 5, of which waited for: 3 -> 3; matrix products, arithmetic and copies ran while one was open for 1% -> 0% of each run, Pallas kernels for 15% -> 16%
where the time goes in v3:
time: 56.7 us; the launch traced here: 56.2 us
  Pallas kernels  19.6 us (35%)
  starting transfers between devices  12.4 us (22%)
  blocking collectives  11 us (19%)
  waiting for transfers between devices  10.3 us (18%)
  between operations  2.07 us (4%)
  local copies, waits for them, and re-layouts  0.79 us (1%)
    pallas_call x6, Pallas kernels, call(): pl.pallas_call(kernel, in_specs=[pl.BlockSpec(memory_space=pltpu.HBM)] *...  19.6 us
    all_to_all x2, starting transfers between devices, exchange(): return lax.all_to_all(x, axes, 0, 0, tiled=True)  11.9 us
    all_to_all x1, blocking collectives, exchange(): return lax.all_to_all(x, axes, 0, 0, tiled=True)  11 us
    all_to_all x2, waiting for transfers between devices, exchange(): return lax.all_to_all(x, axes, 0, 0, tiled=True)  9.16 us
    ppermute x3, waiting for transfers between devices, by_core(): lax.ppermute(x, 'core', [(i, i ^ s) for i in range(n_core)])  1.16 us
  transfers between devices with their start and end apart: 5, of which 3 were waited for; matrix products, arithmetic and copies ran while one was open for 0% of the time, Pallas kernels for 16%

profile of v3, /device:TPU:0, one launch (start us, length us, event | category | flops | bytes accessed | tf_op | source)
XLA Modules:
  0.0 56.2 jit_solution(17770385854230000758)
XLA Ops:
  0.0 0.5 collective-permute-start.1
  0.5 0.1 collective-permute-start
  1.8 1.8 %shard_map.137 = bf16[16,16,128]{2,1,0:T(8,128)(2,1)} custom-call(s32[1]{0:T(128)S(6)} %copy.16.refs_0_, s32[1]{0:T(128)S(6)} %copy.18.refs_1_.refs_2_, bf16[8,3072]{1,0:T(8,128)(2,1)} %bitcast.17), custom_call_target="tpu_custom_call" | custom-call | flops 2000000000 | bytes 1024 | tf_op jit(solution)/shard_map/pallas_call | solution.py:126
  3.6 8.3 %all-to-all-start = ((bf16[16,16,128]{2,1,0:T(8,128)(2,1)}), bf16[16,16,128]{2,1,0:T(8,128)(2,1)S(1)}, u32[]{:S(2)}, u32[]{:S(2)}) async-start(bf16[16,16,128]{2,1,0:T(8,128)(2,1)} %shard_map.137), calls=%async_computation | async-start | bytes 131072 | tf_op jit(solution)/shard_map/all_to_all | solution.py:537
  11.9 0.0 collective-permute-done.refs_2_
  11.9 0.0 copy-start.4
  11.9 0.6 %copy-done.4 = bf16[64,2,384]{2,1,0:T(2,128)(2,1)} copy-done((bf16[64,2,384]{2,1,0:T(2,128)(2,1)}, bf16[64,2,384]{2,1,0:T(2,128)(2,1)S(1)}, u32[]{:S(2)}) %copy-start.4) | copy-done | bytes 98328
  12.6 3.5 %shard_map.136 = (bf16[896,384]{1,0:T(8,128)(2,1)}, f32[256,1]{1,0:T(8,128)}) custom-call(bf16[256,3072]{1,0:T(8,128)(2,1)} %refs_0_.3, bf16[64,2,384]{2,1,0:T(2,128)(2,1)} %refs_1_.4, bf16[64,2,384]{2,1,0:T(2,128)(2,1)} %copy-done.4), custom_call_target="tpu_custom_call" | custom-call | flops 2000000000 | bytes 1024 | tf_op jit(solution)/shard_map/pallas_call | solution.py:126
  16.1 3.4 %all-to-all-done.refs_3_ = bf16[16,16,128]{2,1,0:T(8,128)(2,1)S(1)} async-done(((bf16[16,16,128]{2,1,0:T(8,128)(2,1)}), bf16[16,16,128]{2,1,0:T(8,128)(2,1)S(1)}, u32[]{:S(2)}, u32[]{:S(2)}) %all-to-all-start) | async-done | bytes 65568 | tf_op jit(solution)/shard_map/all_to_all | solution.py:537
  19.4 0.0 collective-permute-done.1.refs_2_
  19.4 3.7 %shard_map.138 = bf16[16,72,128]{2,1,0:T(8,128)(2,1)} custom-call(bf16[896,384]{1,0:T(8,128)(2,1)} %get-tuple-element.7.refs_0_, bf16[384,3072]{1,0:T(8,128)(2,1)} %refs_2_.2, bf16[384,3072]{1,0:T(8,128)(2,1)} %collective-permute-done.1.refs_2_, bf16[16,16,128]{2,1,0:T(8,128)(2,1)S(1)} %all-to-all-done.refs_3_), custom_call_target="tpu_custom_call" | custom-call | flops 2000000000 | bytes 1024 | tf_op jit(solution)/shard_map/pallas_call | solution.py:126
  23.2 3.6 %all-to-all-start.1 = ((bf16[16,72,128]{2,1,0:T(8,128)(2,1)}), bf16[16,72,128]{2,1,0:T(8,128)(2,1)S(1)}, u32[]{:S(2)}, u32[]{:S(2)}) async-start(bf16[16,72,128]{2,1,0:T(8,128)(2,1)} %shard_map.138), calls=%async_computation.1 | async-start | bytes 589824 | tf_op jit(solution)/shard_map/all_to_all | solution.py:537
  27.4 0.0 copy-start
  27.4 0.0 copy-start.1
  27.4 3.8 %shard_map.139.refs_6_ = f32[12,72,192]{2,1,0:T(8,128)} custom-call(bf16[192,1536]{1,0:T(8,128)(2,1)} %bitcast.13, bf16[192,1536]{1,0:T(8,128)(2,1)} %bitcast.11, bf16[192,1536]{1,0:T(8,128)(2,1)} %bitcast.12, bf16[192,1536]{1,0:T(8,128)(2,1)} %bitcast.15), custom_call_target="tpu_custom_call" | custom-call | flops 2000000000 | bytes 1024 | tf_op jit(solution)/shard_map/pallas_call | solution.py:126
  31.3 5.8 %all-to-all-done.1.refs_3_ = bf16[16,72,128]{2,1,0:T(8,128)(2,1)S(1)} async-done(((bf16[16,72,128]{2,1,0:T(8,128)(2,1)}), bf16[16,72,128]{2,1,0:T(8,128)(2,1)S(1)}, u32[]{:S(2)}, u32[]{:S(2)}) %all-to-all-start.1) | async-done | bytes 294944 | tf_op jit(solution)/shard_map/all_to_all | solution.py:537
  37.1 0.0 copy-done
  37.1 0.0 copy-done.1
  37.1 0.0 copy-start.3
  37.1 0.0 copy-start.2
  37.1 2.9 %shard_map.140 = bf16[16,32,128]{2,1,0:T(8,128)(2,1)S(1)} custom-call(s32[1]{0:T(128)S(6)} %copy.16.refs_0_, s32[1]{0:T(128)S(6)} %copy.17.refs_1_, s32[1]{0:T(128)S(6)} %copy.18.refs_1_.refs_2_, bf16[16,72,128]{2,1,0:T(8,128)(2,1)S(1)} %all-to-all-done.1.refs_3_, f32[24,128]{1,0:T(8,128)S(1)} %bitcast.8, f32[1,128]{1,0:T(1,128)S(1)} %bitcast.9, ...), custom_call_target="tpu_custom_call" | custom-call | flops 2000000000 | bytes 1024 | tf_op jit(solution)/shard_map/pallas_call | solution.py:126
  39.9 11.0 %all_to_all.15.refs_3_ = bf16[16,32,128]{2,1,0:T(8,128)(2,1)S(1)} all-to-all(bf16[16,32,128]{2,1,0:T(8,128)(2,1)S(1)} %shard_map.140), channel_id=1, replica_groups=mesh['dp'=4,'chip'=4,'core'=2] {'dp','chip'}, dimensions={0} | all-to-all | bytes 262144 | tf_op jit(solution)/shard_map/all_to_all | solution.py:537
  51.0 0.0 collective-permute-start.2
  51.0 0.0 copy-done.3
  51.0 0.1 copy.15
  51.1 0.0 copy-done.2
  51.2 1.2 %collective-permute-done.2.refs_4_ = bf16[16,32,128]{2,1,0:T(8,128)(2,1)S(1)} collective-permute-done((bf16[16,32,128]{2,1,0:T(8,128)(2,1)S(1)}, bf16[16,32,128]{2,1,0:T(8,128)(2,1)S(1)}, u32[]{:S(2)}, u32[]{:S(2)}) %collective-permute-start.2) | collective-permute-done | bytes 131104 | tf_op jit(solution)/shard_map/ppermute | solution.py:565
  52.3 3.9 %shard_map.141 = f32[256,384]{1,0:T(8,128)} custom-call(bf16[896,384]{1,0:T(8,128)(2,1)} %get-tuple-element.7.refs_0_, f32[256,1]{1,0:T(8,128)S(1)} %div.3.refs_1_, bf16[384,3072]{1,0:T(8,128)(2,1)} %refs_2_.2, bf16[16,32,128]{2,1,0:T(8,128)(2,1)S(1)} %all_to_all.15.refs_3_, bf16[16,32,128]{2,1,0:T(8,128)(2,1)S(1)} %collective-permute-done.2.refs_4_), custom_call_target="tpu_custom_call" | custom-call | flops 2000000000 | bytes 1024 | tf_op jit(solution)/shard_map/pallas_call | solution.py:126
  (2 shorter events, 0.0 us)
Async XLA Ops:
  0.0 19.4 %collective-permute-start.1 = (bf16[384,3072]{1,0:T(8,128)(2,1)}, bf16[384,3072]{1,0:T(8,128)(2,1)}, u32[]{:S(2)}, u32[]{:S(2)}) collective-permute-start(bf16[384,3072]{1,0:T(8,128)(2,1)} %refs_2_.2), channel_id=1, source_target_pairs={{0,1},{1,0},{2,3},{3,2},{4,5},{5,4},{6,7},{7,6},{8,9},{9,8},{10,11... | collective-permute-start | bytes 7077896 | tf_op jit(solution)/shard_map/ppermute | solution.py:565
  0.5 11.4 %collective-permute-start = (bf16[64,2,384]{2,1,0:T(2,128)(2,1)}, bf16[64,2,384]{2,1,0:T(2,128)(2,1)S(1)}, u32[]{:S(2)}, u32[]{:S(2)}) collective-permute-start(bf16[64,2,384]{2,1,0:T(2,128)(2,1)} %refs_1_.4), channel_id=1, source_target_pairs={{0,1},{1,0},{2,3},{3,2},{4,5},{5,4},{6,7},{7,6},{8,9},{9,8},{10,11... | collective-permute-start | bytes 294920 | tf_op jit(solution)/shard_map/ppermute | solution.py:565
  3.6 15.9 %all-to-all-start = ((bf16[16,16,128]{2,1,0:T(8,128)(2,1)}), bf16[16,16,128]{2,1,0:T(8,128)(2,1)S(1)}, u32[]{:S(2)}, u32[]{:S(2)}) async-start(bf16[16,16,128]{2,1,0:T(8,128)(2,1)} %shard_map.137), calls=%async_computation | async-start | bytes 131072 | tf_op jit(solution)/shard_map/all_to_all | solution.py:537
  11.9 0.6 %copy-start.4 = (bf16[64,2,384]{2,1,0:T(2,128)(2,1)}, bf16[64,2,384]{2,1,0:T(2,128)(2,1)S(1)}, u32[]{:S(2)}) copy-start(bf16[64,2,384]{2,1,0:T(2,128)(2,1)S(1)} %collective-permute-done.refs_2_) | copy-start | bytes 294916
  23.2 13.9 %all-to-all-start.1 = ((bf16[16,72,128]{2,1,0:T(8,128)(2,1)}), bf16[16,72,128]{2,1,0:T(8,128)(2,1)S(1)}, u32[]{:S(2)}, u32[]{:S(2)}) async-start(bf16[16,72,128]{2,1,0:T(8,128)(2,1)} %shard_map.138), calls=%async_computation.1 | async-start | bytes 589824 | tf_op jit(solution)/shard_map/all_to_all | solution.py:537
  27.4 9.6 %copy-start = (f32[3072]{0:T(1024)S(1)}, f32[3072]{0:T(1024)}, u32[]{:S(2)}) copy-start(f32[3072]{0:T(1024)} %param.22) | copy-start | bytes 36868
  27.4 9.6 %copy-start.1 = (f32[128]{0:T(128)S(1)}, f32[128]{0:T(128)}, u32[]{:S(2)}) copy-start(f32[128]{0:T(128)} %param.23) | copy-start | bytes 1540
  37.1 13.9 %copy-start.3 = (s32[256]{0:T(256)S(1)}, s32[256]{0:T(256)}, u32[]{:S(2)}) copy-start(s32[256]{0:T(256)} %param.19) | copy-start | bytes 3076
  37.1 14.1 %copy-start.2 = (f32[256,1]{1,0:T(8,128)S(1)}, f32[256,1]{1,0:T(8,128)}, u32[]{:S(2)}) copy-start(f32[256,1]{1,0:T(8,128)} %get-tuple-element.8) | copy-start | bytes 3076
  51.0 1.3 %collective-permute-start.2 = (bf16[16,32,128]{2,1,0:T(8,128)(2,1)S(1)}, bf16[16,32,128]{2,1,0:T(8,128)(2,1)S(1)}, u32[]{:S(2)}, u32[]{:S(2)}) collective-permute-start(bf16[16,32,128]{2,1,0:T(8,128)(2,1)S(1)} %all_to_all.15.refs_3_), channel_id=1, source_target_pairs={{0,1},{1,0},{2,3},{3,2},{4,5},{5,4},{6,7},{7,6},{8,9},{9,8},{10,11... | collective-permute-start | bytes 393224 | tf_op jit(solution)/shard_map/ppermute | solution.py:565

commit v4 on v3

--- a/solution.py
+++ b/solution.py
@@ -15,7 +15,7 @@
 LANES = 128
 MIB = 1024 * 1024
 SPARE_ROWS = 128
-ROOM_FOR_ONE = 53.25
+GRANT = dict(table=51.6, image=51.8, project=52.7, sample=51.8, owner=53.25)
 NT = (((1,), (1,)), ((), ()))
 TN = (((0,), (0,)), ((), ()))
 EVERYONE = ("dp", "chip", "core")
@@ -65,6 +65,10 @@
 
 def scalar(x):
     return ("scalar", x)
+
+
+def direct(x):
+    return ("direct", x)
 
 
 def call(body, operands, results, scratch=(), vmem=63, flops=2_000_000_000):
@@ -78,11 +82,14 @@
 
     def kernel(*refs):
         ins, outs = refs[:n_in], refs[n_in : n_in + n_out]
-        held, made = refs[n_in + n_out : 2 * n_in + n_out], refs[2 * n_in + n_out : 2 * n_in + 2 * n_out]
+        spare, made = refs[n_in + n_out : 2 * n_in + n_out], refs[2 * n_in + n_out : 2 * n_in + 2 * n_out]
+        held = [r if o[0] == "direct" else h for o, r, h in zip(operands, ins, spare)]
         sems, extra = refs[2 * (n_in + n_out)], refs[2 * (n_in + n_out) + 1 :]
 
         def copies_of(i):
             o = operands[i]
+            if o[0] == "direct":
+                return []
             if o[0] == "part":
                 return [pltpu.make_async_copy(ins[i].at[cut_index(o[2])], held[i], sems.at[offsets[i]])]
             if o[0] != "late" or o[2] == 1:
@@ -121,11 +128,14 @@
 
     def place(o):
         shape = cut_shape(o[1].shape, o[2]) if o[0] == "part" else o[1].shape
+        shape = (8, LANES) if o[0] == "direct" else shape
         return (pltpu.SMEM if o[0] == "scalar" else pltpu.VMEM)(shape, o[1].dtype)
 
     return pl.pallas_call(
         kernel,
-        in_specs=[pl.BlockSpec(memory_space=pltpu.HBM)] * n_in,
+        in_specs=[
+            pl.BlockSpec(memory_space=pltpu.VMEM if o[0] == "direct" else pltpu.HBM) for o in operands
+        ],
         out_specs=[pl.BlockSpec(memory_space=pltpu.HBM)] * n_out,
         out_shape=shapes,
         scratch_shapes=[place(o) for o in operands]
@@ -228,8 +238,8 @@
         for i in range(2):
             at = p * each + rows + i * buckets
             bank[at : at + buckets, :] = x[:, i, :].astype(BF16)
-    block = rows // 4
-    for i in range(4):
+    block = rows // 2
+    for i in range(2):
         wait(i)
         here = slice(i * block, (i + 1) * block)
         x = table[here, :].astype(F32)
@@ -258,8 +268,9 @@
     used = n_core * bank_rows(rows, buckets)
     return call(
         functools.partial(table_body, width, n_core),
-        [late(table, 4, 0)] + [hold(m) for m in mods] + parts,
+        [late(table, 2, 0)] + [hold(m) for m in mods] + parts,
         [((used + SPARE_ROWS, width), BF16, ((0, used),)), ((rows, 1), F32)],
+        vmem=GRANT["table"],
     )
 
 
@@ -285,11 +296,12 @@
 def image_part(q, k, v, g, head_dim):
     rows, width = q.shape
     heads = width // head_dim
-    chunks = math.gcd(heads, 4)
+    chunks = math.gcd(heads, 2)
     (out,) = call(
         functools.partial(image_body, head_dim, chunks),
         [late(x, chunks) for x in (q, k, v, g)],
-        [((heads, 8 + SPARE_ROWS // 2, rows), F32, ((0, heads), (0, 8)))],
+        [((heads, 8 + SPARE_ROWS, rows), F32, ((0, heads), (0, 8)))],
+        vmem=GRANT["image"],
     )
     return out
 
@@ -376,14 +388,14 @@
             pltpu.VMEM((n_all * slots * kv_rows, head_dim), F32),
             pltpu.VMEM((n_all * rows, LANES), F32),
         ],
-        vmem=ROOM_FOR_ONE,
+        vmem=GRANT["project"],
     )
     return out
 
 
 def sample_body(sizes, tok_len, conc_dev, model_width, ins, outs, scratch):
     ids_ref, place_ref, time_ref, terms, bias, gain_ref, stat_ref = ins[:7]
-    (q, q_wait), (g, g_wait) = ins[7:]
+    q, g = ins[7:]
     (out,), (firsts, toks) = outs, scratch
     n_dp, n_chip, _ = sizes
     heads, _, img_len = stat_ref.shape
@@ -424,8 +436,6 @@
         inv = lax.rsqrt(jnp.mean(raw * raw, -1, keepdims=True) + EPSILON)
         keys.append((raw * inv * gain).astype(BF16))
         vals.append(text_rows(heads + h).astype(BF16))
-    q_wait(0)
-    g_wait(0)
     cols = lambda h: slice(h * head_dim, (h + 1) * head_dim)
     shape = (heads, tok_len, img_len)
     s = jnp.concatenate([dot_nt(keys[h], q[:, cols(h)]) for h in range(heads)], 0)
@@ -475,13 +485,13 @@
         functools.partial(sample_body, sizes, tok_len, conc_dev, model_width),
         [scalar(ids), scalar(places), scalar(times), hold(terms), hold(bias), hold(gain)]
         + [part(stats, (0, stats.shape[0]), (0, 8))]
-        + [late(q, 1), late(g, 1)],
+        + [direct(q), direct(g)],
         [((sizes[0] * sizes[1], kv_rows + 8, head_dim), BF16)],
         [
             pltpu.VMEM((sizes[0] * kv_rows, head_dim), F32),
             pltpu.VMEM((tok_len * kv_rows, head_dim), F32),
         ],
-        vmem=ROOM_FOR_ONE,
+        vmem=GRANT["sample"],
     )
     return out
 
@@ -528,7 +538,7 @@
         [part(bank, (0, each)), hold(coef), late(weight, 3)] + [hold(x) for x in packets],
         [((coef.shape[0], weight.shape[0]), F32)],
         [pltpu.VMEM((n_dev * rows, head_dim), F32)],
-        vmem=ROOM_FOR_ONE,
+        vmem=GRANT["owner"],
     )
     return out
 

time: 56.7 us -> 55.8 us (0.984)
  Pallas kernels: 19.6 us -> 17.8 us
  waiting for transfers between devices: 10.3 us -> 11.8 us
  local copies, waits for them, and re-layouts: 0.79 us -> 0.18 us
    pallas_call x6, Pallas kernels: 19.6 us -> 17.8 us  [call(): pl.pallas_call(kernel, in_specs=[pl.BlockSpec(memory_space=pltpu.VMEM if...]
    all_to_all x2, waiting for transfers between devices: 9.16 us -> 10.7 us  [exchange(): return lax.all_to_all(x, axes, 0, 0, tiled=True)]
    unnamed x10 -> x18, local copies, waits for them, and re-layouts: 0.66 us -> 0.04 us
  transfers between devices with their start and end apart: 5 -> 5, of which waited for: 3 -> 3; matrix products, arithmetic and copies ran while one was open for 0% -> 0% of each run, Pallas kernels for 16% -> 14%
where the time goes in v4:
time: 55.8 us; the launch traced here: 55.4 us
  Pallas kernels  17.8 us (32%)
  starting transfers between devices  12.4 us (22%)
  waiting for transfers between devices  11.8 us (21%)
  blocking collectives  11 us (20%)
  between operations  2.13 us (4%)
    pallas_call x6, Pallas kernels, call(): pl.pallas_call(kernel, in_specs=[pl.BlockSpec(memory_space=pltpu.VMEM if...  17.8 us
    all_to_all x2, starting transfers between devices, exchange(): return lax.all_to_all(x, axes, 0, 0, tiled=True)  11.9 us
    all_to_all x1, blocking collectives, exchange(): return lax.all_to_all(x, axes, 0, 0, tiled=True)  11 us
    all_to_all x2, waiting for transfers between devices, exchange(): return lax.all_to_all(x, axes, 0, 0, tiled=True)  10.7 us
    ppermute x3, waiting for transfers between devices, by_core(): lax.ppermute(x, 'core', [(i, i ^ s) for i in range(n_core)])  1.17 us
  transfers between devices with their start and end apart: 5, of which 3 were waited for; matrix products, arithmetic and copies ran while one was open for 0% of the time, Pallas kernels for 14%

profile of v4, /device:TPU:0, one launch (start us, length us, event | category | flops | bytes accessed | tf_op | source)
XLA Modules:
  0.0 55.4 jit_solution(7196463092527783425)
XLA Ops:
  0.0 0.5 collective-permute-start.1
  0.5 0.1 collective-permute-start
  1.8 0.0 copy-start.4
  1.8 1.8 %shard_map.137 = bf16[16,16,128]{2,1,0:T(8,128)(2,1)} custom-call(s32[1]{0:T(128)S(6)} %copy.16.refs_0_, s32[1]{0:T(128)S(6)} %copy.18.refs_1_.refs_2_, bf16[8,3072]{1,0:T(8,128)(2,1)} %bitcast.17), custom_call_target="tpu_custom_call" | custom-call | flops 2000000000 | bytes 1024 | tf_op jit(solution)/shard_map/pallas_call | solution.py:134
  3.6 8.3 %all-to-all-start = ((bf16[16,16,128]{2,1,0:T(8,128)(2,1)}), bf16[16,16,128]{2,1,0:T(8,128)(2,1)S(1)}, u32[]{:S(2)}, u32[]{:S(2)}) async-start(bf16[16,16,128]{2,1,0:T(8,128)(2,1)} %shard_map.137), calls=%async_computation | async-start | bytes 131072 | tf_op jit(solution)/shard_map/all_to_all | solution.py:547
  12.0 0.0 collective-permute-done.refs_2_
  12.0 0.0 copy-done.4
  12.0 2.6 %shard_map.136 = (bf16[896,384]{1,0:T(8,128)(2,1)S(1)}, f32[256,1]{1,0:T(8,128)S(1)}) custom-call(bf16[256,3072]{1,0:T(8,128)(2,1)} %refs_0_.3, bf16[64,2,384]{2,1,0:T(2,128)(2,1)S(1)} %copy-done.4, bf16[64,2,384]{2,1,0:T(2,128)(2,1)S(1)} %collective-permute-done.refs_2_), custom_call_target="tpu_custom_call" | custom-call | flops 2000000000 | bytes 1024 | tf_op jit(solution)/shard_map/pallas_call | solution.py:134
  14.5 0.0 copy-start.7
  14.6 4.9 %all-to-all-done.refs_3_ = bf16[16,16,128]{2,1,0:T(8,128)(2,1)S(1)} async-done(((bf16[16,16,128]{2,1,0:T(8,128)(2,1)}), bf16[16,16,128]{2,1,0:T(8,128)(2,1)S(1)}, u32[]{:S(2)}, u32[]{:S(2)}) %all-to-all-start) | async-done | bytes 65568 | tf_op jit(solution)/shard_map/all_to_all | solution.py:547
  19.5 0.0 collective-permute-done.1.refs_2_
  19.5 0.0 copy-start
  19.5 0.0 copy-start.1
  19.5 0.0 copy-start.2
  19.5 3.8 %shard_map.138 = bf16[16,72,128]{2,1,0:T(8,128)(2,1)} custom-call(bf16[896,384]{1,0:T(8,128)(2,1)S(1)} %get-tuple-element.7.refs_0_, bf16[384,3072]{1,0:T(8,128)(2,1)} %refs_2_.2, bf16[384,3072]{1,0:T(8,128)(2,1)} %collective-permute-done.1.refs_2_, bf16[16,16,128]{2,1,0:T(8,128)(2,1)S(1)} %all-to-all-done.refs_3_), custom_call_target="tpu_custom_call" | custom-call | flops 2000000000 | bytes 1024 | tf_op jit(solution)/shard_map/pallas_call | solution.py:134
  23.4 0.0 copy-done.7
  23.4 3.5 %all-to-all-start.1 = ((bf16[16,72,128]{2,1,0:T(8,128)(2,1)}), bf16[16,72,128]{2,1,0:T(8,128)(2,1)S(1)}, u32[]{:S(2)}, u32[]{:S(2)}) async-start(bf16[16,72,128]{2,1,0:T(8,128)(2,1)} %shard_map.138), calls=%async_computation.1 | async-start | bytes 589824 | tf_op jit(solution)/shard_map/all_to_all | solution.py:547
  27.6 0.0 copy-done
  27.6 0.0 copy-done.1
  27.6 0.0 copy-done.2
  27.6 0.0 copy-start.3
  27.6 0.0 copy-start.5
  27.6 0.0 copy-start.6
  27.6 3.2 %shard_map.139.refs_6_ = f32[12,136,192]{2,1,0:T(8,128)} custom-call(bf16[192,1536]{1,0:T(8,128)(2,1)S(1)} %bitcast.10, bf16[192,1536]{1,0:T(8,128)(2,1)S(1)} %bitcast.8, bf16[192,1536]{1,0:T(8,128)(2,1)S(1)} %bitcast.9, bf16[192,1536]{1,0:T(8,128)(2,1)} %bitcast.12), custom_call_target="tpu_custom_call" | custom-call | flops 2000000000 | bytes 1024 | tf_op jit(solution)/shard_map/pallas_call | solution.py:134
  30.8 5.8 %all-to-all-done.1.refs_3_ = bf16[16,72,128]{2,1,0:T(8,128)(2,1)S(1)} async-done(((bf16[16,72,128]{2,1,0:T(8,128)(2,1)}), bf16[16,72,128]{2,1,0:T(8,128)(2,1)S(1)}, u32[]{:S(2)}, u32[]{:S(2)}) %all-to-all-start.1) | async-done | bytes 294944 | tf_op jit(solution)/shard_map/all_to_all | solution.py:547
  36.6 0.0 copy-done.3
  36.6 0.0 copy-done.5
  36.6 0.0 copy-done.6
  36.6 0.0 copy-start.8
  36.6 2.5 %shard_map.140 = bf16[16,32,128]{2,1,0:T(8,128)(2,1)S(1)} custom-call(s32[1]{0:T(128)S(6)} %copy.16.refs_0_, s32[1]{0:T(128)S(6)} %copy.17.refs_1_, s32[1]{0:T(128)S(6)} %copy.18.refs_1_.refs_2_, bf16[16,72,128]{2,1,0:T(8,128)(2,1)S(1)} %all-to-all-done.1.refs_3_, f32[24,128]{1,0:T(8,128)S(1)} %bitcast.14, f32[1,128]{1,0:T(1,128)S(1)} %bitcast.15, ...), custom_call_target="tpu_custom_call" | custom-call | flops 2000000000 | bytes 1024 | tf_op jit(solution)/shard_map/pallas_call | solution.py:134
  39.1 11.0 %all_to_all.15.refs_3_ = bf16[16,32,128]{2,1,0:T(8,128)(2,1)S(1)} all-to-all(bf16[16,32,128]{2,1,0:T(8,128)(2,1)S(1)} %shard_map.140), channel_id=1, replica_groups=mesh['dp'=4,'chip'=4,'core'=2] {'dp','chip'}, dimensions={0} | all-to-all | bytes 262144 | tf_op jit(solution)/shard_map/all_to_all | solution.py:547
  50.1 0.0 collective-permute-start.2
  50.1 0.0 copy-done.8
  50.1 0.1 copy.15
  50.3 1.2 %collective-permute-done.2.refs_4_ = bf16[16,32,128]{2,1,0:T(8,128)(2,1)S(1)} collective-permute-done((bf16[16,32,128]{2,1,0:T(8,128)(2,1)S(1)}, bf16[16,32,128]{2,1,0:T(8,128)(2,1)S(1)}, u32[]{:S(2)}, u32[]{:S(2)}) %collective-permute-start.2) | collective-permute-done | bytes 131104 | tf_op jit(solution)/shard_map/ppermute | solution.py:575
  51.5 3.9 %shard_map.141 = f32[256,384]{1,0:T(8,128)} custom-call(bf16[896,384]{1,0:T(8,128)(2,1)} %copy-done.7, f32[256,1]{1,0:T(8,128)S(1)} %div.3.refs_1_, bf16[384,3072]{1,0:T(8,128)(2,1)} %refs_2_.2, bf16[16,32,128]{2,1,0:T(8,128)(2,1)S(1)} %all_to_all.15.refs_3_, bf16[16,32,128]{2,1,0:T(8,128)(2,1)S(1)} %collective-permute-done.2.refs_4_), custom_call_target="tpu_custom_call" | custom-call | flops 2000000000 | bytes 1024 | tf_op jit(solution)/shard_map/pallas_call | solution.py:134
  (2 shorter events, 0.0 us)
Async XLA Ops:
  0.0 19.5 %collective-permute-start.1 = (bf16[384,3072]{1,0:T(8,128)(2,1)}, bf16[384,3072]{1,0:T(8,128)(2,1)}, u32[]{:S(2)}, u32[]{:S(2)}) collective-permute-start(bf16[384,3072]{1,0:T(8,128)(2,1)} %refs_2_.2), channel_id=1, source_target_pairs={{0,1},{1,0},{2,3},{3,2},{4,5},{5,4},{6,7},{7,6},{8,9},{9,8},{10,11... | collective-permute-start | bytes 7077896 | tf_op jit(solution)/shard_map/ppermute | solution.py:575
  0.5 11.5 %collective-permute-start = (bf16[64,2,384]{2,1,0:T(2,128)(2,1)}, bf16[64,2,384]{2,1,0:T(2,128)(2,1)S(1)}, u32[]{:S(2)}, u32[]{:S(2)}) collective-permute-start(bf16[64,2,384]{2,1,0:T(2,128)(2,1)} %refs_1_.4), channel_id=1, source_target_pairs={{0,1},{1,0},{2,3},{3,2},{4,5},{5,4},{6,7},{7,6},{8,9},{9,8},{10,11... | collective-permute-start | bytes 294920 | tf_op jit(solution)/shard_map/ppermute | solution.py:575
  1.8 10.2 %copy-start.4 = (bf16[64,2,384]{2,1,0:T(2,128)(2,1)S(1)}, bf16[64,2,384]{2,1,0:T(2,128)(2,1)}, u32[]{:S(2)}) copy-start(bf16[64,2,384]{2,1,0:T(2,128)(2,1)} %refs_1_.4) | copy-start | bytes 294916
  3.6 15.9 %all-to-all-start = ((bf16[16,16,128]{2,1,0:T(8,128)(2,1)}), bf16[16,16,128]{2,1,0:T(8,128)(2,1)S(1)}, u32[]{:S(2)}, u32[]{:S(2)}) async-start(bf16[16,16,128]{2,1,0:T(8,128)(2,1)} %shard_map.137), calls=%async_computation | async-start | bytes 131072 | tf_op jit(solution)/shard_map/all_to_all | solution.py:547
  14.5 8.8 %copy-start.7 = (bf16[896,384]{1,0:T(8,128)(2,1)}, bf16[896,384]{1,0:T(8,128)(2,1)S(1)}, u32[]{:S(2)}) copy-start(bf16[896,384]{1,0:T(8,128)(2,1)S(1)} %get-tuple-element.7.refs_0_) | copy-start | bytes 2064388
  19.5 8.1 %copy-start = (bf16[1,192,1536]{2,1,0:T(8,128)(2,1)S(1)}, bf16[1,192,1536]{2,1,0:T(8,128)(2,1)}, u32[]{:S(2)}) copy-start(bf16[1,192,1536]{2,1,0:T(8,128)(2,1)} %param.25) | copy-start | bytes 1769476
  19.5 8.1 %copy-start.1 = (bf16[1,192,1536]{2,1,0:T(8,128)(2,1)S(1)}, bf16[1,192,1536]{2,1,0:T(8,128)(2,1)}, u32[]{:S(2)}) copy-start(bf16[1,192,1536]{2,1,0:T(8,128)(2,1)} %param.26) | copy-start | bytes 1769476
  19.5 8.1 %copy-start.2 = (bf16[1,192,1536]{2,1,0:T(8,128)(2,1)S(1)}, bf16[1,192,1536]{2,1,0:T(8,128)(2,1)}, u32[]{:S(2)}) copy-start(bf16[1,192,1536]{2,1,0:T(8,128)(2,1)} %param.24) | copy-start | bytes 1769476
  23.4 13.2 %all-to-all-start.1 = ((bf16[16,72,128]{2,1,0:T(8,128)(2,1)}), bf16[16,72,128]{2,1,0:T(8,128)(2,1)S(1)}, u32[]{:S(2)}, u32[]{:S(2)}) async-start(bf16[16,72,128]{2,1,0:T(8,128)(2,1)} %shard_map.138), calls=%async_computation.1 | async-start | bytes 589824 | tf_op jit(solution)/shard_map/all_to_all | solution.py:547
  27.6 9.0 %copy-start.3 = (bf16[1,192,1536]{2,1,0:T(8,128)(2,1)S(1)}, bf16[1,192,1536]{2,1,0:T(8,128)(2,1)}, u32[]{:S(2)}) copy-start(bf16[1,192,1536]{2,1,0:T(8,128)(2,1)} %param.27) | copy-start | bytes 1769476
  27.6 9.0 %copy-start.5 = (f32[3072]{0:T(1024)S(1)}, f32[3072]{0:T(1024)}, u32[]{:S(2)}) copy-start(f32[3072]{0:T(1024)} %param.22) | copy-start | bytes 36868
  27.6 8.9 %copy-start.6 = (f32[128]{0:T(128)S(1)}, f32[128]{0:T(128)}, u32[]{:S(2)}) copy-start(f32[128]{0:T(128)} %param.23) | copy-start | bytes 1540
  36.6 13.5 %copy-start.8 = (s32[256]{0:T(256)S(1)}, s32[256]{0:T(256)}, u32[]{:S(2)}) copy-start(s32[256]{0:T(256)} %param.19) | copy-start | bytes 3076
  50.1 1.3 %collective-permute-start.2 = (bf16[16,32,128]{2,1,0:T(8,128)(2,1)S(1)}, bf16[16,32,128]{2,1,0:T(8,128)(2,1)S(1)}, u32[]{:S(2)}, u32[]{:S(2)}) collective-permute-start(bf16[16,32,128]{2,1,0:T(8,128)(2,1)S(1)} %all_to_all.15.refs_3_), channel_id=1, source_target_pairs={{0,1},{1,0},{2,3},{3,2},{4,5},{5,4},{6,7},{7,6},{8,9},{9,8},{10,11... | collective-permute-start | bytes 393224 | tf_op jit(solution)/shard_map/ppermute | solution.py:575

commit v5 on v4

--- a/solution.py
+++ b/solution.py
@@ -51,6 +51,10 @@
     return ("part", x, cut)
 
 
+def late_part(x, *cut):
+    return ("late_part", x, cut)
+
+
 def cut_shape(shape, cut):
     return tuple(c[1] for c in cut) + tuple(shape[len(cut) :])
 
@@ -83,14 +87,14 @@
     def kernel(*refs):
         ins, outs = refs[:n_in], refs[n_in : n_in + n_out]
         spare, made = refs[n_in + n_out : 2 * n_in + n_out], refs[2 * n_in + n_out : 2 * n_in + 2 * n_out]
-        held = [r if o[0] == "direct" else h for o, r, h in zip(operands, ins, spare)]
+        held = [r if o[0] in ("direct", "scalar") else h for o, r, h in zip(operands, ins, spare)]
         sems, extra = refs[2 * (n_in + n_out)], refs[2 * (n_in + n_out) + 1 :]
 
         def copies_of(i):
             o = operands[i]
-            if o[0] == "direct":
+            if o[0] in ("direct", "scalar"):
                 return []
-            if o[0] == "part":
+            if o[0] in ("part", "late_part"):
                 return [pltpu.make_async_copy(ins[i].at[cut_index(o[2])], held[i], sems.at[offsets[i]])]
             if o[0] != "late" or o[2] == 1:
                 return [pltpu.make_async_copy(ins[i], held[i], sems.at[offsets[i]])]
@@ -102,8 +106,9 @@
             ]
 
         copies = [copies_of(i) for i in range(n_in)]
-        first = [c for i in range(n_in) if operands[i][0] != "late" for c in copies[i]]
-        then = [i for i in range(n_in) if operands[i][0] == "late"]
+        is_late = [o[0] in ("late", "late_part") for o in operands]
+        first = [c for i in range(n_in) if not is_late[i] for c in copies[i]]
+        then = [i for i in range(n_in) if is_late[i]]
         for c in first:
             c.start()
         for k in range(max([counts[i] for i in then], default=0)):
@@ -113,7 +118,7 @@
         for c in first:
             c.wait()
         given = [
-            (held[i], lambda k, i=i: copies[i][k].wait()) if operands[i][0] == "late" else held[i]
+            (held[i], lambda k, i=i: copies[i][k].wait()) if is_late[i] else held[i]
             for i in range(n_in)
         ]
         body(given, made, extra)
@@ -126,19 +131,19 @@
         for c in final:
             c.wait()
 
-    def place(o):
-        shape = cut_shape(o[1].shape, o[2]) if o[0] == "part" else o[1].shape
-        shape = (8, LANES) if o[0] == "direct" else shape
-        return (pltpu.SMEM if o[0] == "scalar" else pltpu.VMEM)(shape, o[1].dtype)
-
+    def spare_of(o):
+        shape = cut_shape(o[1].shape, o[2]) if o[0] in ("part", "late_part") else o[1].shape
+        return pltpu.VMEM((8, LANES) if o[0] in ("direct", "scalar") else shape, o[1].dtype)
+
+    spaces = {"direct": pltpu.VMEM, "scalar": pltpu.SMEM}
     return pl.pallas_call(
         kernel,
         in_specs=[
-            pl.BlockSpec(memory_space=pltpu.VMEM if o[0] == "direct" else pltpu.HBM) for o in operands
+            pl.BlockSpec(memory_space=spaces.get(o[0], pltpu.HBM)) for o in operands
         ],
         out_specs=[pl.BlockSpec(memory_space=pltpu.HBM)] * n_out,
         out_shape=shapes,
-        scratch_shapes=[place(o) for o in operands]
+        scratch_shapes=[spare_of(o) for o in operands]
         + [pltpu.VMEM(cut_shape(s.shape, c), s.dtype) for s, c in zip(shapes, cuts)]
         + [pltpu.SemaphoreType.DMA((n_sems,))]
         + list(scratch),
@@ -312,7 +317,7 @@
     bank, weights, given = ins[0], ins[1 : 1 + n_core], ins[1 + n_core :]
     (out,), (lhs, flat, flat_in) = outs, scratch
     width, kv_width = weights[0][0].shape
-    each = bank.shape[0] // n_core
+    each = (bank.shape[0] - SPARE_ROWS) // n_core
     buckets = (each - conc_dev) // 2
     my_dp = lax.axis_index("dp")
     if len(given) == 1:
@@ -374,14 +379,14 @@
     n_all = n_dp * n_chip
     slots, kv_rows = 1 + per, kv_width // head_dim
     chunks = 3
-    given = [hold(packets)]
+    given = [direct(packets)]
     if width % LANES:
         body = packets[:, : need - 1].reshape(n_all, -1)[:, : per * n_core * width]
         body = body.reshape(n_all, per, n_core, width).transpose(1, 2, 0, 3)
         given = [hold(body), hold(packets[:, need - 1])]
     (out,) = call(
         functools.partial(project_body, sizes, conc_dev, head_dim, per, chunks),
-        [part(bank, (0, bank.shape[0] - SPARE_ROWS))] + [late(w, chunks) for w in weights] + given,
+        [direct(bank)] + [late(w, chunks) for w in weights] + given,
         [((n_all, slots * kv_rows, head_dim), BF16)],
         [
             pltpu.VMEM((n_core, slots * n_all, width), BF16),
@@ -394,7 +399,7 @@
 
 
 def sample_body(sizes, tok_len, conc_dev, model_width, ins, outs, scratch):
-    ids_ref, place_ref, time_ref, terms, bias, gain_ref, stat_ref = ins[:7]
+    ids_ref, place_ref, time_ref, terms, bias, gain_ref, (stat_ref, stat_wait) = ins[:7]
     q, g = ins[7:]
     (out,), (firsts, toks) = outs, scratch
     n_dp, n_chip, _ = sizes
@@ -441,6 +446,7 @@
     s = jnp.concatenate([dot_nt(keys[h], q[:, cols(h)]) for h in range(heads)], 0)
     gv = jnp.concatenate([dot_nt(vals[h], g[:, cols(h)]) for h in range(heads)], 0)
     s, gv = s.reshape(shape) * scale, gv.reshape(shape)
+    stat_wait(0)
     stats = stat_ref[...]
     top, total, weighted = stats[:, 0:1, :], stats[:, 1:2, :], stats[:, 2:3, :]
     new_top = jnp.maximum(top, jnp.max(s, 1, keepdims=True))
@@ -483,8 +489,8 @@
     per = tokens_per_dp(sizes, tok_len)
     (out,) = call(
         functools.partial(sample_body, sizes, tok_len, conc_dev, model_width),
-        [scalar(ids), scalar(places), scalar(times), hold(terms), hold(bias), hold(gain)]
-        + [part(stats, (0, stats.shape[0]), (0, 8))]
+        [scalar(ids), scalar(places), scalar(times), direct(terms), direct(bias), direct(gain)]
+        + [late_part(stats, (0, stats.shape[0]), (0, 8))]
         + [direct(q), direct(g)],
         [((sizes[0] * sizes[1], kv_rows + 8, head_dim), BF16)],
         [
@@ -497,7 +503,7 @@
 
 
 def owner_body(chunks, ins, outs, scratch):
-    bank, coef, (weight, wait), packets = *ins[:3], ins[3:]
+    (bank, bank_wait), (coef, coef_wait), (weight, wait), packets = *ins[:3], ins[3:]
     (out,), (flat,) = outs, scratch
     n_each, rows, head_dim = packets[0].shape
     n_dev = n_each * len(packets)
@@ -513,20 +519,27 @@
     side = piece(parts)
     column = lambda i: side[:, i : i + 1]
     mean_1, mean_2 = column(0) + column(1), column(2) + column(3)
+    side_rows = side.T
+    row = lambda i: side_rows[i : i + 1, :].astype(I32)
+    ids_row = row(4) * 64 + row(5) - first
+    owned = (iota((conc_dev, n_dev), 0) == ids_row).astype(BF16)
+    owned = jnp.concatenate([owned, owned], 1)
     mine = column(4).astype(I32) * 64 + column(5).astype(I32) - first
     times = column(6).astype(I32)
+    bank_wait(0)
     scale = 1.0 + dot((iota((n_dev, buckets), 1) == times).astype(BF16), bank[conc_dev + buckets :, :])
     one_hot = (iota((n_dev, conc_dev), 1) == mine).astype(BF16)
-    conc = dot(one_hot, bank[0:conc_dev, :])
+    offset = mean_1 + dot(one_hot, bank[0:conc_dev, :]) * mean_2
+    coef_wait(0)
+    factor = jnp.broadcast_to(coef[...], out.shape)
     size = parts // chunks
-    grad = jnp.zeros(scale.shape, F32)
+    grad = jnp.zeros((n_dev, weight.shape[0]), F32)
     for i in range(chunks):
+        dkv = jnp.concatenate([piece(r).astype(BF16) for r in range(i * size, (i + 1) * size)], 1)
         wait(i)
-        dkv = jnp.concatenate([piece(r).astype(BF16) for r in range(i * size, (i + 1) * size)], 1)
         grad += dot_nt(dkv, weight[:, i * size * head_dim : (i + 1) * size * head_dim])
-    grad = grad * scale - mean_1 - conc * mean_2
-    high, low = split_bf16(grad)
-    out[...] = (dot_tn(one_hot, high) + dot_tn(one_hot, low)) * coef[...]
+    high, low = split_bf16(grad * scale - offset)
+    out[...] = dot(owned, jnp.concatenate([high, low], 0)) * factor
 
 
 def owner_part(packets, bank, n_core, coef, weight):
@@ -535,7 +548,7 @@
     n_dev = n_each * len(packets)
     (out,) = call(
         functools.partial(owner_body, 3),
-        [part(bank, (0, each)), hold(coef), late(weight, 3)] + [hold(x) for x in packets],
+        [late_part(bank, (0, each)), late(coef, 1), late(weight, 3)] + [direct(x) for x in packets],
         [((coef.shape[0], weight.shape[0]), F32)],
         [pltpu.VMEM((n_dev * rows, head_dim), F32)],
         vmem=GRANT["owner"],

time: 55.8 us -> 55.4 us (level)
  no operation moved by 1% of the time
where the time goes in v5:
time: 55.4 us; the launch traced here: 54.9 us
  Pallas kernels  17.4 us (31%)
  starting transfers between devices  12.4 us (22%)
  waiting for transfers between devices  11.8 us (21%)
  blocking collectives  11 us (20%)
  between operations  2.13 us (4%)
    pallas_call x6, Pallas kernels, call(): pl.pallas_call(kernel, in_specs=[pl.BlockSpec(memory_space=spaces.get(o[0...  17.4 us
    all_to_all x2, starting transfers between devices, exchange(): return lax.all_to_all(x, axes, 0, 0, tiled=True)  11.9 us
    all_to_all x1, blocking collectives, exchange(): return lax.all_to_all(x, axes, 0, 0, tiled=True)  11 us
    all_to_all x2, waiting for transfers between devices, exchange(): return lax.all_to_all(x, axes, 0, 0, tiled=True)  10.7 us
    ppermute x3, waiting for transfers between devices, by_core(): lax.ppermute(x, 'core', [(i, i ^ s) for i in range(n_core)])  1.17 us
  transfers between devices with their start and end apart: 5, of which 3 were waited for; matrix products, arithmetic and copies ran while one was open for 0% of the time, Pallas kernels for 14%

profile of v5, /device:TPU:0, one launch (start us, length us, event | category | flops | bytes accessed | tf_op | source)
XLA Modules:
  0.0 54.9 jit_solution(8188787464420231008)
XLA Ops:
  0.0 0.5 collective-permute-start.1
  0.5 0.1 collective-permute-start
  1.8 0.0 copy-start.4
  1.8 1.8 %shard_map.137 = bf16[16,16,128]{2,1,0:T(8,128)(2,1)} custom-call(s32[1]{0:T(128)S(6)} %copy.16.refs_0_, s32[1]{0:T(128)S(6)} %copy.18.refs_1_.refs_2_, bf16[8,3072]{1,0:T(8,128)(2,1)} %bitcast.17), custom_call_target="tpu_custom_call" | custom-call | flops 2000000000 | bytes 1024 | tf_op jit(solution)/shard_map/pallas_call | solution.py:139
  3.6 8.3 %all-to-all-start = ((bf16[16,16,128]{2,1,0:T(8,128)(2,1)}), bf16[16,16,128]{2,1,0:T(8,128)(2,1)S(1)}, u32[]{:S(2)}, u32[]{:S(2)}) async-start(bf16[16,16,128]{2,1,0:T(8,128)(2,1)} %shard_map.137), calls=%async_computation | async-start | bytes 131072 | tf_op jit(solution)/shard_map/all_to_all | solution.py:560
  11.9 0.0 collective-permute-done.refs_2_
  12.0 0.0 copy-done.4
  12.0 2.6 %shard_map.136 = (bf16[896,384]{1,0:T(8,128)(2,1)S(1)}, f32[256,1]{1,0:T(8,128)S(1)}) custom-call(bf16[256,3072]{1,0:T(8,128)(2,1)} %refs_0_.3, bf16[64,2,384]{2,1,0:T(2,128)(2,1)S(1)} %copy-done.4, bf16[64,2,384]{2,1,0:T(2,128)(2,1)S(1)} %collective-permute-done.refs_2_), custom_call_target="tpu_custom_call" | custom-call | flops 2000000000 | bytes 1024 | tf_op jit(solution)/shard_map/pallas_call | solution.py:139
  14.5 0.0 copy-start.7
  14.6 4.9 %all-to-all-done.refs_3_ = bf16[16,16,128]{2,1,0:T(8,128)(2,1)S(1)} async-done(((bf16[16,16,128]{2,1,0:T(8,128)(2,1)}), bf16[16,16,128]{2,1,0:T(8,128)(2,1)S(1)}, u32[]{:S(2)}, u32[]{:S(2)}) %all-to-all-start) | async-done | bytes 65568 | tf_op jit(solution)/shard_map/all_to_all | solution.py:560
  19.5 0.0 collective-permute-done.1.refs_2_
  19.5 0.0 copy-start
  19.5 0.0 copy-start.1
  19.5 0.0 copy-start.2
  19.5 3.8 %shard_map.138 = bf16[16,72,128]{2,1,0:T(8,128)(2,1)} custom-call(bf16[896,384]{1,0:T(8,128)(2,1)S(1)} %get-tuple-element.7.refs_0_, bf16[384,3072]{1,0:T(8,128)(2,1)} %refs_2_.2, bf16[384,3072]{1,0:T(8,128)(2,1)} %collective-permute-done.1.refs_2_, bf16[16,16,128]{2,1,0:T(8,128)(2,1)S(1)} %all-to-all-done.refs_3_), custom_call_target="tpu_custom_call" | custom-call | flops 2000000000 | bytes 1024 | tf_op jit(solution)/shard_map/pallas_call | solution.py:139
  23.3 0.0 copy-done.7
  23.3 3.5 %all-to-all-start.1 = ((bf16[16,72,128]{2,1,0:T(8,128)(2,1)}), bf16[16,72,128]{2,1,0:T(8,128)(2,1)S(1)}, u32[]{:S(2)}, u32[]{:S(2)}) async-start(bf16[16,72,128]{2,1,0:T(8,128)(2,1)} %shard_map.138), calls=%async_computation.1 | async-start | bytes 589824 | tf_op jit(solution)/shard_map/all_to_all | solution.py:560
  27.6 0.0 copy-done
  27.6 0.0 copy-done.1
  27.6 0.0 copy-done.2
  27.6 0.0 copy-start.3
  27.6 0.0 copy-start.5
  27.6 0.0 copy-start.6
  27.6 3.2 %shard_map.139.refs_6_ = f32[12,136,192]{2,1,0:T(8,128)} custom-call(bf16[192,1536]{1,0:T(8,128)(2,1)S(1)} %bitcast.10, bf16[192,1536]{1,0:T(8,128)(2,1)S(1)} %bitcast.8, bf16[192,1536]{1,0:T(8,128)(2,1)S(1)} %bitcast.9, bf16[192,1536]{1,0:T(8,128)(2,1)} %bitcast.12), custom_call_target="tpu_custom_call" | custom-call | flops 2000000000 | bytes 1024 | tf_op jit(solution)/shard_map/pallas_call | solution.py:139
  30.8 5.7 %all-to-all-done.1.refs_3_ = bf16[16,72,128]{2,1,0:T(8,128)(2,1)S(1)} async-done(((bf16[16,72,128]{2,1,0:T(8,128)(2,1)}), bf16[16,72,128]{2,1,0:T(8,128)(2,1)S(1)}, u32[]{:S(2)}, u32[]{:S(2)}) %all-to-all-start.1) | async-done | bytes 294944 | tf_op jit(solution)/shard_map/all_to_all | solution.py:560
  36.5 0.0 copy-done.3
  36.5 0.0 copy-done.5
  36.6 0.0 copy-done.6
  36.6 0.0 copy-start.8
  36.6 2.5 %shard_map.140 = bf16[16,32,128]{2,1,0:T(8,128)(2,1)S(1)} custom-call(s32[1]{0:T(128)S(6)} %copy.16.refs_0_, s32[1]{0:T(128)S(6)} %copy.17.refs_1_, s32[1]{0:T(128)S(6)} %copy.18.refs_1_.refs_2_, bf16[16,72,128]{2,1,0:T(8,128)(2,1)S(1)} %all-to-all-done.1.refs_3_, f32[24,128]{1,0:T(8,128)S(1)} %bitcast.14, f32[1,128]{1,0:T(1,128)S(1)} %bitcast.15, ...), custom_call_target="tpu_custom_call" | custom-call | flops 2000000000 | bytes 1024 | tf_op jit(solution)/shard_map/pallas_call | solution.py:139
  39.0 11.0 %all_to_all.15.refs_3_ = bf16[16,32,128]{2,1,0:T(8,128)(2,1)S(1)} all-to-all(bf16[16,32,128]{2,1,0:T(8,128)(2,1)S(1)} %shard_map.140), channel_id=1, replica_groups=mesh['dp'=4,'chip'=4,'core'=2] {'dp','chip'}, dimensions={0} | all-to-all | bytes 262144 | tf_op jit(solution)/shard_map/all_to_all | solution.py:560
  50.0 0.0 collective-permute-start.2
  50.0 0.0 copy-done.8
  50.0 0.1 copy.15
  50.2 1.2 %collective-permute-done.2.refs_4_ = bf16[16,32,128]{2,1,0:T(8,128)(2,1)S(1)} collective-permute-done((bf16[16,32,128]{2,1,0:T(8,128)(2,1)S(1)}, bf16[16,32,128]{2,1,0:T(8,128)(2,1)S(1)}, u32[]{:S(2)}, u32[]{:S(2)}) %collective-permute-start.2) | collective-permute-done | bytes 131104 | tf_op jit(solution)/shard_map/ppermute | solution.py:588
  51.4 3.5 %shard_map.141 = f32[256,384]{1,0:T(8,128)} custom-call(bf16[896,384]{1,0:T(8,128)(2,1)} %copy-done.7, f32[256,1]{1,0:T(8,128)S(1)} %div.3.refs_1_, bf16[384,3072]{1,0:T(8,128)(2,1)} %refs_2_.2, bf16[16,32,128]{2,1,0:T(8,128)(2,1)S(1)} %all_to_all.15.refs_3_, bf16[16,32,128]{2,1,0:T(8,128)(2,1)S(1)} %collective-permute-done.2.refs_4_), custom_call_target="tpu_custom_call" | custom-call | flops 2000000000 | bytes 1024 | tf_op jit(solution)/shard_map/pallas_call | solution.py:139
  (2 shorter events, 0.0 us)
Async XLA Ops:
  0.0 19.5 %collective-permute-start.1 = (bf16[384,3072]{1,0:T(8,128)(2,1)}, bf16[384,3072]{1,0:T(8,128)(2,1)}, u32[]{:S(2)}, u32[]{:S(2)}) collective-permute-start(bf16[384,3072]{1,0:T(8,128)(2,1)} %refs_2_.2), channel_id=1, source_target_pairs={{0,1},{1,0},{2,3},{3,2},{4,5},{5,4},{6,7},{7,6},{8,9},{9,8},{10,11... | collective-permute-start | bytes 7077896 | tf_op jit(solution)/shard_map/ppermute | solution.py:588
  0.5 11.5 %collective-permute-start = (bf16[64,2,384]{2,1,0:T(2,128)(2,1)}, bf16[64,2,384]{2,1,0:T(2,128)(2,1)S(1)}, u32[]{:S(2)}, u32[]{:S(2)}) collective-permute-start(bf16[64,2,384]{2,1,0:T(2,128)(2,1)} %refs_1_.4), channel_id=1, source_target_pairs={{0,1},{1,0},{2,3},{3,2},{4,5},{5,4},{6,7},{7,6},{8,9},{9,8},{10,11... | collective-permute-start | bytes 294920 | tf_op jit(solution)/shard_map/ppermute | solution.py:588
  1.8 10.2 %copy-start.4 = (bf16[64,2,384]{2,1,0:T(2,128)(2,1)S(1)}, bf16[64,2,384]{2,1,0:T(2,128)(2,1)}, u32[]{:S(2)}) copy-start(bf16[64,2,384]{2,1,0:T(2,128)(2,1)} %refs_1_.4) | copy-start | bytes 294916
  3.6 15.9 %all-to-all-start = ((bf16[16,16,128]{2,1,0:T(8,128)(2,1)}), bf16[16,16,128]{2,1,0:T(8,128)(2,1)S(1)}, u32[]{:S(2)}, u32[]{:S(2)}) async-start(bf16[16,16,128]{2,1,0:T(8,128)(2,1)} %shard_map.137), calls=%async_computation | async-start | bytes 131072 | tf_op jit(solution)/shard_map/all_to_all | solution.py:560
  14.5 8.8 %copy-start.7 = (bf16[896,384]{1,0:T(8,128)(2,1)}, bf16[896,384]{1,0:T(8,128)(2,1)S(1)}, u32[]{:S(2)}) copy-start(bf16[896,384]{1,0:T(8,128)(2,1)S(1)} %get-tuple-element.7.refs_0_) | copy-start | bytes 2064388
  19.5 8.1 %copy-start = (bf16[1,192,1536]{2,1,0:T(8,128)(2,1)S(1)}, bf16[1,192,1536]{2,1,0:T(8,128)(2,1)}, u32[]{:S(2)}) copy-start(bf16[1,192,1536]{2,1,0:T(8,128)(2,1)} %param.25) | copy-start | bytes 1769476
  19.5 8.1 %copy-start.1 = (bf16[1,192,1536]{2,1,0:T(8,128)(2,1)S(1)}, bf16[1,192,1536]{2,1,0:T(8,128)(2,1)}, u32[]{:S(2)}) copy-start(bf16[1,192,1536]{2,1,0:T(8,128)(2,1)} %param.26) | copy-start | bytes 1769476
  19.5 8.1 %copy-start.2 = (bf16[1,192,1536]{2,1,0:T(8,128)(2,1)S(1)}, bf16[1,192,1536]{2,1,0:T(8,128)(2,1)}, u32[]{:S(2)}) copy-start(bf16[1,192,1536]{2,1,0:T(8,128)(2,1)} %param.24) | copy-start | bytes 1769476
  23.3 13.2 %all-to-all-start.1 = ((bf16[16,72,128]{2,1,0:T(8,128)(2,1)}), bf16[16,72,128]{2,1,0:T(8,128)(2,1)S(1)}, u32[]{:S(2)}, u32[]{:S(2)}) async-start(bf16[16,72,128]{2,1,0:T(8,128)(2,1)} %shard_map.138), calls=%async_computation.1 | async-start | bytes 589824 | tf_op jit(solution)/shard_map/all_to_all | solution.py:560
  27.6 9.0 %copy-start.3 = (bf16[1,192,1536]{2,1,0:T(8,128)(2,1)S(1)}, bf16[1,192,1536]{2,1,0:T(8,128)(2,1)}, u32[]{:S(2)}) copy-start(bf16[1,192,1536]{2,1,0:T(8,128)(2,1)} %param.27) | copy-start | bytes 1769476
  27.6 9.0 %copy-start.5 = (f32[3072]{0:T(1024)S(1)}, f32[3072]{0:T(1024)}, u32[]{:S(2)}) copy-start(f32[3072]{0:T(1024)} %param.22) | copy-start | bytes 36868
  27.6 8.9 %copy-start.6 = (f32[128]{0:T(128)S(1)}, f32[128]{0:T(128)}, u32[]{:S(2)}) copy-start(f32[128]{0:T(128)} %param.23) | copy-start | bytes 1540
  36.6 13.5 %copy-start.8 = (s32[256]{0:T(256)S(1)}, s32[256]{0:T(256)}, u32[]{:S(2)}) copy-start(s32[256]{0:T(256)} %param.19) | copy-start | bytes 3076
  50.0 1.3 %collective-permute-start.2 = (bf16[16,32,128]{2,1,0:T(8,128)(2,1)S(1)}, bf16[16,32,128]{2,1,0:T(8,128)(2,1)S(1)}, u32[]{:S(2)}, u32[]{:S(2)}) collective-permute-start(bf16[16,32,128]{2,1,0:T(8,128)(2,1)S(1)} %all_to_all.15.refs_3_), channel_id=1, source_target_pairs={{0,1},{1,0},{2,3},{3,2},{4,5},{5,4},{6,7},{7,6},{8,9},{9,8},{10,11... | collective-permute-start | bytes 393224 | tf_op jit(solution)/shard_map/ppermute | solution.py:588

commit v6 on v5

--- a/solution.py
+++ b/solution.py
@@ -158,21 +158,43 @@
     return d * rstd, rstd
 
 
-def tokens_per_dp(sizes, tok_len):
-    return -(-tok_len // sizes[0])
-
-
-def packet_rows(per, n_core, width):
-    need = -(-per * n_core * width // LANES) + 1
-    return need, -(-need // 16) * 16
-
-
-def pack_body(sizes, width, per, ins, outs, scratch):
+SPECIAL = (2, 1, 1)
+
+
+def slots_of(sizes, tok_len):
+    return max(-(-(tok_len + sum(SPECIAL)) // sizes[0]), max(SPECIAL))
+
+
+def special_at(step):
+    return SPECIAL[step] if step < len(SPECIAL) else 0
+
+
+def first_token(step, slots):
+    passed = [slots * i - sum(SPECIAL[:i]) for i in range(len(SPECIAL) + 1)]
+    far = passed[-1] + (step - len(SPECIAL)) * slots
+    for i in range(len(SPECIAL)):
+        far = jnp.where(step == i, passed[i], far)
+    return far
+
+
+def owner_of(concept, n_dp, conc_dev):
+    owner = jnp.int32(0)
+    for d in range(1, n_dp):
+        owner += (concept >= d * conc_dev).astype(I32)
+    return owner
+
+
+def packet_rows(slots, n_core, width):
+    need = -(-slots * n_core * width // LANES) + 1
+    return need, -(-need // 8) * 8
+
+
+def pack_body(sizes, width, slots, conc_dev, ins, outs, scratch):
     n_dp, n_chip, n_core = sizes
     ids, times, tokens = ins
-    (out,), (held, flat) = outs, scratch
+    (out,), (held, chosen, flat) = outs, scratch
     tok_len = tokens.shape[0]
-    need, rows = packet_rows(per, n_core, width)
+    need, rows = packet_rows(slots, n_core, width)
     pieces = width // LANES
     held[...] = normalise(tokens[...].astype(F32))[0]
     flat[...] = jnp.zeros(flat.shape, F32)
@@ -182,42 +204,51 @@
     for i, x in enumerate(values):
         label = jnp.where(lane == i, x.astype(F32), label)
     core = lax.axis_index("core")
+    owner = owner_of(ids[0], n_dp, conc_dev)
     for d in range(n_dp):
+        token = first_token(lax.rem(d + n_dp - owner, n_dp), slots)
+        for i in range(slots):
+            chosen[i : i + 1, :] = held[pl.ds(jnp.minimum(token + i, tok_len - 1), 1), :]
         for chip in range(n_chip):
             base = (d * n_chip + chip) * rows
             flat[base + need - 1 : base + need, :] = label
-            for i in range(per):
-                t = d * per + i
-                for p in range(n_core if t < tok_len else 0):
+            for i in range(slots):
+                for p in range(n_core):
                     at = (chip * n_core + (core ^ p)) * width
                     for k in range(pieces):
                         r = base + (i * n_core + p) * pieces + k
                         lanes = pl.ds(pl.multiple_of(at + k * LANES, LANES), LANES)
-                        flat[r : r + 1, :] = held[t : t + 1, lanes]
-    out[...] = flat[...].reshape(out.shape).astype(BF16)
+                        flat[r : r + 1, :] = chosen[i : i + 1, lanes]
+    out[...] = flat[...].astype(BF16)
 
 
 def hat_body(ins, outs, scratch):
     outs[0][...] = normalise(ins[0][...].astype(F32))[0].astype(BF16)
 
 
-def pack(ids, times, tokens, sizes, width):
+def pack(ids, times, tokens, sizes, width, conc_dev):
     n_dp, n_chip, n_core = sizes
     n_all = n_dp * n_chip
     tok_len, model_width = tokens.shape
-    per = tokens_per_dp(sizes, tok_len)
-    need, rows = packet_rows(per, n_core, width)
+    slots = slots_of(sizes, tok_len)
+    need, rows = packet_rows(slots, n_core, width)
     if width % LANES == 0:
         (out,) = call(
-            functools.partial(pack_body, sizes, width, per),
-            [scalar(ids), scalar(times), hold(tokens)],
-            [((n_all, rows, LANES), BF16)],
-            [pltpu.VMEM(tokens.shape, F32), pltpu.VMEM((n_all * rows, LANES), F32)],
+            functools.partial(pack_body, sizes, width, slots, conc_dev),
+            [scalar(ids), scalar(times), direct(tokens)],
+            [((n_all * rows, LANES), BF16)],
+            [
+                pltpu.VMEM(tokens.shape, F32),
+                pltpu.VMEM((-(-slots // 8) * 8, model_width), F32),
+                pltpu.VMEM((n_all * rows, LANES), F32),
+            ],
         )
-        return out
-    (hat,) = call(hat_body, [hold(tokens)], [(tokens.shape, BF16)])
-    hat = jnp.pad(hat, ((0, n_dp * per - tok_len), (0, 0)))
-    hat = hat.reshape(n_dp, per, n_chip, n_core, width)
+        return out.reshape(n_all, rows, LANES)
+    (hat,) = call(hat_body, [direct(tokens)], [(tokens.shape, BF16)])
+    steps = (jnp.arange(n_dp, dtype=I32) + n_dp - owner_of(ids[0], n_dp, conc_dev)) % n_dp
+    token = first_token(steps, slots)[:, None] + jnp.arange(slots, dtype=I32)[None, :]
+    hat = jnp.take(hat, jnp.minimum(token, tok_len - 1).reshape(-1), axis=0)
+    hat = hat.reshape(n_dp, slots, n_chip, n_core, width)
     core = lax.axis_index("core")
     own = [lax.dynamic_index_in_dim(hat, core ^ p, 3, keepdims=False) for p in range(n_core)]
     body = jnp.stack(own, 3).transpose(0, 2, 1, 3, 4).reshape(n_all, -1)
@@ -273,7 +304,7 @@
     used = n_core * bank_rows(rows, buckets)
     return call(
         functools.partial(table_body, width, n_core),
-        [late(table, 2, 0)] + [hold(m) for m in mods] + parts,
+        [late(table, 2, 0)] + [direct(m) for m in mods] + parts,
         [((used + SPARE_ROWS, width), BF16, ((0, used),)), ((rows, 1), F32)],
         vmem=GRANT["table"],
     )
@@ -311,7 +342,7 @@
     return out
 
 
-def project_body(sizes, conc_dev, head_dim, per, chunks, ins, outs, scratch):
+def project_body(sizes, conc_dev, head_dim, slots, chunks, ins, outs, scratch):
     n_dp, n_chip, n_core = sizes
     n_all = n_dp * n_chip
     bank, weights, given = ins[0], ins[1 : 1 + n_core], ins[1 + n_core :]
@@ -321,7 +352,7 @@
     buckets = (each - conc_dev) // 2
     my_dp = lax.axis_index("dp")
     if len(given) == 1:
-        need, rows = packet_rows(per, n_core, width)
+        need, rows = packet_rows(slots, n_core, width)
         pieces = width // LANES
         flat_in[...] = given[0][...].reshape(n_all * rows, LANES).astype(F32)
         row = lambda r: flat_in[pl.ds(r, n_all, stride=rows), :]
@@ -346,14 +377,14 @@
         shift = dot(pick_time, bank[at : at + buckets, :])
         scale = 1.0 + dot(pick_time, bank[at + buckets : at + 2 * buckets, :])
         conc = scale * dot(pick_row, bank[p * each : p * each + conc_dev, :]) + shift
-        first = jnp.where(
-            owned_by(0), conc, jnp.where(owned_by(1), scale, jnp.where(owned_by(2), shift, 0.0))
-        )
-        lhs[p, 0:n_all] = first.astype(BF16)
-        for i in range(per):
-            rows_i = slice((1 + i) * n_all, (2 + i) * n_all)
-            lhs[p, rows_i] = (scale * token(i, p) + shift).astype(BF16)
-    slots = 1 + per
+        tokens = [scale * token(i, p) + shift for i in range(slots)]
+        special = ([conc, jnp.zeros_like(conc)], [scale], [shift])
+        for i in range(slots):
+            value = tokens[i]
+            for step, given_rows in enumerate(special):
+                value = jnp.where(owned_by(step), (given_rows + tokens)[i], value)
+            lhs[p, i * n_all : (i + 1) * n_all] = value.astype(BF16)
+    owned = owned_by(0)
     kv_rows = kv_width // head_dim
     block = math.gcd(kv_width // chunks, 4 * head_dim)
     for at in range(0, kv_width, block):
@@ -364,30 +395,32 @@
         terms = dot(lhs[0], weights[0][0][:, cols])
         for p in range(1, n_core):
             terms += dot(lhs[p], weights[p][0][:, cols])
-        for s in range(slots):
+        term = [terms[i * n_all : (i + 1) * n_all] for i in range(slots)]
+        term[1] = jnp.where(owned, term[0] - term[0].astype(BF16).astype(F32), term[1])
+        for i in range(slots):
             for r in range(block // head_dim):
-                to = pl.ds(s * kv_rows + at // head_dim + r, n_all, stride=slots * kv_rows)
-                flat[to, :] = terms[s * n_all : (s + 1) * n_all, r * head_dim : (r + 1) * head_dim]
-    out[...] = flat[...].reshape(out.shape).astype(BF16)
+                to = pl.ds(i * kv_rows + at // head_dim + r, n_all, stride=slots * kv_rows)
+                flat[to, :] = term[i][:, r * head_dim : (r + 1) * head_dim]
+    out[...] = flat[...].astype(BF16)
 
 
 def project(packets, bank, conc_dev, weights, sizes, head_dim, tok_len):
     n_dp, n_chip, n_core = sizes
     width, kv_width = weights[0].shape
-    per = tokens_per_dp(sizes, tok_len)
-    need, rows = packet_rows(per, n_core, width)
+    slots = slots_of(sizes, tok_len)
+    need, rows = packet_rows(slots, n_core, width)
     n_all = n_dp * n_chip
-    slots, kv_rows = 1 + per, kv_width // head_dim
+    kv_rows = kv_width // head_dim
     chunks = 3
     given = [direct(packets)]
     if width % LANES:
-        body = packets[:, : need - 1].reshape(n_all, -1)[:, : per * n_core * width]
-        body = body.reshape(n_all, per, n_core, width).transpose(1, 2, 0, 3)
+        body = packets[:, : need - 1].reshape(n_all, -1)[:, : slots * n_core * width]
+        body = body.reshape(n_all, slots, n_core, width).transpose(1, 2, 0, 3)
         given = [hold(body), hold(packets[:, need - 1])]
     (out,) = call(
-        functools.partial(project_body, sizes, conc_dev, head_dim, per, chunks),
+        functools.partial(project_body, sizes, conc_dev, head_dim, slots, chunks),
         [direct(bank)] + [late(w, chunks) for w in weights] + given,
-        [((n_all, slots * kv_rows, head_dim), BF16)],
+        [((n_all * slots * kv_rows, head_dim), BF16)],
         [
             pltpu.VMEM((n_core, slots * n_all, width), BF16),
             pltpu.VMEM((n_all * slots * kv_rows, head_dim), F32),
@@ -395,36 +428,32 @@
         ],
         vmem=GRANT["project"],
     )
-    return out
+    return out.reshape(n_all, slots * kv_rows, head_dim)
 
 
 def sample_body(sizes, tok_len, conc_dev, model_width, ins, outs, scratch):
     ids_ref, place_ref, time_ref, terms, bias, gain_ref, (stat_ref, stat_wait) = ins[:7]
     q, g = ins[7:]
-    (out,), (firsts, toks) = outs, scratch
+    (out,), (toks,) = outs, scratch
     n_dp, n_chip, _ = sizes
     heads, _, img_len = stat_ref.shape
     kv_rows, head_dim = bias.shape
-    per = tokens_per_dp(sizes, tok_len)
     scale = 1.0 / math.sqrt(head_dim)
-    owner = jnp.int32(0)
-    for d in range(1, n_dp):
-        owner += (ids_ref[0] >= d * conc_dev).astype(I32)
-    for d in range(n_dp):
-        total = terms[d * n_chip].astype(F32)
+    owner = owner_of(ids_ref[0], n_dp, conc_dev)
+    slots = slots_of(sizes, tok_len)
+    sums, t = [], 0
+    for step in range(n_dp):
+        first = lax.rem(owner + step, n_dp) * n_chip
+        total = terms[first].astype(F32)
         for s in range(1, n_chip):
-            total += terms[d * n_chip + s].astype(F32)
-        firsts[d * kv_rows : (d + 1) * kv_rows, :] = total[:kv_rows]
-        for i in range(per):
-            t = d * per + i
+            total += terms[first + s].astype(F32)
+        slot = lambda i: total[i * kv_rows : (i + 1) * kv_rows]
+        sums += [slot(i) for i in range(special_at(step))]
+        for i in range(special_at(step), slots):
             if t < tok_len:
-                toks[t * kv_rows : (t + 1) * kv_rows, :] = total[(1 + i) * kv_rows : (2 + i) * kv_rows]
-
-    def gathered(step):
-        at = lax.rem(owner + step, n_dp) * kv_rows
-        return firsts[pl.ds(pl.multiple_of(at, 8), kv_rows), :]
-
-    conc, scale_sum, shift_sum = gathered(0), gathered(1), gathered(2)
+                toks[t * kv_rows : (t + 1) * kv_rows, :] = slot(i)
+                t += 1
+    conc, scale_sum, shift_sum = sums[0] + sums[1], sums[2], sums[3]
     full = conc + bias[...]
     raw_pos = full[:heads]
     inv_pos = lax.rsqrt(jnp.mean(raw_pos * raw_pos, -1, keepdims=True) + EPSILON)
@@ -486,7 +515,6 @@
 
 def sample_part(ids, places, times, terms, bias, gain, stats, q, g, sizes, tok_len, conc_dev, model_width):
     kv_rows, head_dim = bias.shape
-    per = tokens_per_dp(sizes, tok_len)
     (out,) = call(
         functools.partial(sample_body, sizes, tok_len, conc_dev, model_width),
         [scalar(ids), scalar(places), scalar(times), direct(terms), direct(bias), direct(gain)]
@@ -494,7 +522,6 @@
         + [direct(q), direct(g)],
         [((sizes[0] * sizes[1], kv_rows + 8, head_dim), BF16)],
         [
-            pltpu.VMEM((sizes[0] * kv_rows, head_dim), F32),
             pltpu.VMEM((tok_len * kv_rows, head_dim), F32),
         ],
         vmem=GRANT["sample"],
@@ -588,7 +615,7 @@
             lax.ppermute(x, "core", [(i, i ^ s) for i in range(n_core)]) for s in range(1, n_core)
         ]
 
-    packets = pack(concept_ids, timesteps, txt_tokens[0], sizes, slice_width)
+    packets = pack(concept_ids, timesteps, txt_tokens[0], sizes, slice_width, conc_dev)
     packets = exchange(packets, CLASS)
     weights = by_core(kv_weight)
     bank, rstd = table_part(concept_table, by_core(mod_table), slice_width, n_core)

time: 55.4 us -> 55.6 us (level)
  transfers between devices with their start and end apart: 5 -> 5, of which waited for: 3 -> 3; matrix products, arithmetic and copies ran while one was open for 0% -> 0% of each run, Pallas kernels for 14% -> 13%
where the time goes in v6:
time: 55.6 us; the launch traced here: 55.2 us
  Pallas kernels  17.2 us (31%)
  starting transfers between devices  12.4 us (22%)
  waiting for transfers between devices  12.2 us (22%)
  blocking collectives  11 us (20%)
  between operations  2.13 us (4%)
    pallas_call x6, Pallas kernels, call(): pl.pallas_call(kernel, in_specs=[pl.BlockSpec(memory_space=spaces.get(o[0...  17.2 us
    all_to_all x2, starting transfers between devices, exchange(): return lax.all_to_all(x, axes, 0, 0, tiled=True)  11.9 us
    all_to_all x2, waiting for transfers between devices, exchange(): return lax.all_to_all(x, axes, 0, 0, tiled=True)  11.1 us
    all_to_all x1, blocking collectives, exchange(): return lax.all_to_all(x, axes, 0, 0, tiled=True)  11 us
    ppermute x3, waiting for transfers between devices, by_core(): lax.ppermute(x, 'core', [(i, i ^ s) for i in range(n_core)])  1.17 us
  transfers between devices with their start and end apart: 5, of which 3 were waited for; matrix products, arithmetic and copies ran while one was open for 0% of the time, Pallas kernels for 13%

profile of v6, /device:TPU:0, one launch (start us, length us, event | category | flops | bytes accessed | tf_op | source)
XLA Modules:
  0.0 55.2 jit_solution(15266124699785152817)
XLA Ops:
  0.0 0.5 collective-permute-start.1
  0.5 0.1 collective-permute-start
  1.8 0.0 copy-start.4
  1.8 1.9 %shard_map.137 = bf16[384,128]{1,0:T(8,128)(2,1)} custom-call(s32[1]{0:T(128)S(6)} %copy.16.refs_0_, s32[1]{0:T(128)S(6)} %copy.18.refs_1_.refs_2_, bf16[8,3072]{1,0:T(8,128)(2,1)} %bitcast.20), custom_call_target="tpu_custom_call" | custom-call | flops 2000000000 | bytes 1024 | tf_op jit(solution)/shard_map/pallas_call | solution.py:139
  3.7 8.3 %all-to-all-start = ((bf16[16,24,128]{2,1,0:T(8,128)(2,1)}), bf16[16,24,128]{2,1,0:T(8,128)(2,1)S(1)}, u32[]{:S(2)}, u32[]{:S(2)}) async-start(bf16[16,24,128]{2,1,0:T(8,128)(2,1)} %bitcast.18), calls=%async_computation | async-start | bytes 196608 | tf_op jit(solution)/shard_map/all_to_all | solution.py:587
  12.1 0.0 collective-permute-done.refs_2_
  12.1 0.0 copy-done.4
  12.1 2.3 %shard_map.136 = (bf16[896,384]{1,0:T(8,128)(2,1)S(1)}, f32[256,1]{1,0:T(8,128)S(1)}) custom-call(bf16[256,3072]{1,0:T(8,128)(2,1)} %refs_0_.3, bf16[64,2,384]{2,1,0:T(2,128)(2,1)S(1)} %copy-done.4, bf16[64,2,384]{2,1,0:T(2,128)(2,1)S(1)} %collective-permute-done.refs_2_), custom_call_target="tpu_custom_call" | custom-call | flops 2000000000 | bytes 1024 | tf_op jit(solution)/shard_map/pallas_call | solution.py:139
  14.4 0.0 copy-start.7
  14.4 5.3 %all-to-all-done.refs_3_ = bf16[16,24,128]{2,1,0:T(8,128)(2,1)S(1)} async-done(((bf16[16,24,128]{2,1,0:T(8,128)(2,1)}), bf16[16,24,128]{2,1,0:T(8,128)(2,1)S(1)}, u32[]{:S(2)}, u32[]{:S(2)}) %all-to-all-start) | async-done | bytes 98336 | tf_op jit(solution)/shard_map/all_to_all | solution.py:587
  19.7 0.0 collective-permute-done.1.refs_2_
  19.7 0.0 copy-start
  19.7 0.0 copy-start.1
  19.7 0.0 copy-start.2
  19.7 3.8 %shard_map.138 = bf16[1152,128]{1,0:T(8,128)(2,1)} custom-call(bf16[896,384]{1,0:T(8,128)(2,1)S(1)} %get-tuple-element.7.refs_0_, bf16[384,3072]{1,0:T(8,128)(2,1)} %refs_2_.2, bf16[384,3072]{1,0:T(8,128)(2,1)} %collective-permute-done.1.refs_2_, bf16[16,24,128]{2,1,0:T(8,128)(2,1)S(1)} %all-to-all-done.refs_3_), custom_call_target="tpu_custom_call" | custom-call | flops 2000000000 | bytes 1024 | tf_op jit(solution)/shard_map/pallas_call | solution.py:139
  23.6 0.0 copy-done.7
  23.6 3.5 %all-to-all-start.1 = ((bf16[16,72,128]{2,1,0:T(8,128)(2,1)}), bf16[16,72,128]{2,1,0:T(8,128)(2,1)S(1)}, u32[]{:S(2)}, u32[]{:S(2)}) async-start(bf16[16,72,128]{2,1,0:T(8,128)(2,1)} %bitcast.3), calls=%async_computation.1 | async-start | bytes 589824 | tf_op jit(solution)/shard_map/all_to_all | solution.py:587
  27.8 0.0 copy-done
  27.8 0.0 copy-done.1
  27.8 0.0 copy-done.2
  27.8 0.0 copy-start.3
  27.8 0.0 copy-start.5
  27.9 0.0 copy-start.6
  27.9 3.2 %shard_map.139.refs_6_ = f32[12,136,192]{2,1,0:T(8,128)} custom-call(bf16[192,1536]{1,0:T(8,128)(2,1)S(1)} %bitcast.12, bf16[192,1536]{1,0:T(8,128)(2,1)S(1)} %bitcast.10, bf16[192,1536]{1,0:T(8,128)(2,1)S(1)} %bitcast.11, bf16[192,1536]{1,0:T(8,128)(2,1)} %bitcast.14), custom_call_target="tpu_custom_call" | custom-call | flops 2000000000 | bytes 1024 | tf_op jit(solution)/shard_map/pallas_call | solution.py:139
  31.0 5.8 %all-to-all-done.1.refs_3_ = bf16[16,72,128]{2,1,0:T(8,128)(2,1)S(1)} async-done(((bf16[16,72,128]{2,1,0:T(8,128)(2,1)}), bf16[16,72,128]{2,1,0:T(8,128)(2,1)S(1)}, u32[]{:S(2)}, u32[]{:S(2)}) %all-to-all-start.1) | async-done | bytes 294944 | tf_op jit(solution)/shard_map/all_to_all | solution.py:587
  36.8 0.0 copy-done.3
  36.8 0.0 copy-done.5
  36.8 0.0 copy-done.6
  36.8 0.0 copy-start.8
  36.8 2.5 %shard_map.140 = bf16[16,32,128]{2,1,0:T(8,128)(2,1)S(1)} custom-call(s32[1]{0:T(128)S(6)} %copy.16.refs_0_, s32[1]{0:T(128)S(6)} %copy.17.refs_1_, s32[1]{0:T(128)S(6)} %copy.18.refs_1_.refs_2_, bf16[16,72,128]{2,1,0:T(8,128)(2,1)S(1)} %all-to-all-done.1.refs_3_, f32[24,128]{1,0:T(8,128)S(1)} %bitcast.16, f32[1,128]{1,0:T(1,128)S(1)} %bitcast.17, ...), custom_call_target="tpu_custom_call" | custom-call | flops 2000000000 | bytes 1024 | tf_op jit(solution)/shard_map/pallas_call | solution.py:139
  39.3 11.0 %all_to_all.15.refs_3_ = bf16[16,32,128]{2,1,0:T(8,128)(2,1)S(1)} all-to-all(bf16[16,32,128]{2,1,0:T(8,128)(2,1)S(1)} %shard_map.140), channel_id=1, replica_groups=mesh['dp'=4,'chip'=4,'core'=2] {'dp','chip'}, dimensions={0} | all-to-all | bytes 262144 | tf_op jit(solution)/shard_map/all_to_all | solution.py:587
  50.3 0.0 collective-permute-start.2
  50.3 0.0 copy-done.8
  50.3 0.1 copy.15
  50.5 1.2 %collective-permute-done.2.refs_4_ = bf16[16,32,128]{2,1,0:T(8,128)(2,1)S(1)} collective-permute-done((bf16[16,32,128]{2,1,0:T(8,128)(2,1)S(1)}, bf16[16,32,128]{2,1,0:T(8,128)(2,1)S(1)}, u32[]{:S(2)}, u32[]{:S(2)}) %collective-permute-start.2) | collective-permute-done | bytes 131104 | tf_op jit(solution)/shard_map/ppermute | solution.py:615
  51.6 3.5 %shard_map.141 = f32[256,384]{1,0:T(8,128)} custom-call(bf16[896,384]{1,0:T(8,128)(2,1)} %copy-done.7, f32[256,1]{1,0:T(8,128)S(1)} %div.3.refs_1_, bf16[384,3072]{1,0:T(8,128)(2,1)} %refs_2_.2, bf16[16,32,128]{2,1,0:T(8,128)(2,1)S(1)} %all_to_all.15.refs_3_, bf16[16,32,128]{2,1,0:T(8,128)(2,1)S(1)} %collective-permute-done.2.refs_4_), custom_call_target="tpu_custom_call" | custom-call | flops 2000000000 | bytes 1024 | tf_op jit(solution)/shard_map/pallas_call | solution.py:139
  (2 shorter events, 0.0 us)
Async XLA Ops:
  0.0 19.7 %collective-permute-start.1 = (bf16[384,3072]{1,0:T(8,128)(2,1)}, bf16[384,3072]{1,0:T(8,128)(2,1)}, u32[]{:S(2)}, u32[]{:S(2)}) collective-permute-start(bf16[384,3072]{1,0:T(8,128)(2,1)} %refs_2_.2), channel_id=1, source_target_pairs={{0,1},{1,0},{2,3},{3,2},{4,5},{5,4},{6,7},{7,6},{8,9},{9,8},{10,11... | collective-permute-start | bytes 7077896 | tf_op jit(solution)/shard_map/ppermute | solution.py:615
  0.5 11.6 %collective-permute-start = (bf16[64,2,384]{2,1,0:T(2,128)(2,1)}, bf16[64,2,384]{2,1,0:T(2,128)(2,1)S(1)}, u32[]{:S(2)}, u32[]{:S(2)}) collective-permute-start(bf16[64,2,384]{2,1,0:T(2,128)(2,1)} %refs_1_.4), channel_id=1, source_target_pairs={{0,1},{1,0},{2,3},{3,2},{4,5},{5,4},{6,7},{7,6},{8,9},{9,8},{10,11... | collective-permute-start | bytes 294920 | tf_op jit(solution)/shard_map/ppermute | solution.py:615
  1.8 10.3 %copy-start.4 = (bf16[64,2,384]{2,1,0:T(2,128)(2,1)S(1)}, bf16[64,2,384]{2,1,0:T(2,128)(2,1)}, u32[]{:S(2)}) copy-start(bf16[64,2,384]{2,1,0:T(2,128)(2,1)} %refs_1_.4) | copy-start | bytes 294916
  3.7 16.0 %all-to-all-start = ((bf16[16,24,128]{2,1,0:T(8,128)(2,1)}), bf16[16,24,128]{2,1,0:T(8,128)(2,1)S(1)}, u32[]{:S(2)}, u32[]{:S(2)}) async-start(bf16[16,24,128]{2,1,0:T(8,128)(2,1)} %bitcast.18), calls=%async_computation | async-start | bytes 196608 | tf_op jit(solution)/shard_map/all_to_all | solution.py:587
  14.4 9.2 %copy-start.7 = (bf16[896,384]{1,0:T(8,128)(2,1)}, bf16[896,384]{1,0:T(8,128)(2,1)S(1)}, u32[]{:S(2)}) copy-start(bf16[896,384]{1,0:T(8,128)(2,1)S(1)} %get-tuple-element.7.refs_0_) | copy-start | bytes 2064388
  19.7 8.1 %copy-start = (bf16[1,192,1536]{2,1,0:T(8,128)(2,1)S(1)}, bf16[1,192,1536]{2,1,0:T(8,128)(2,1)}, u32[]{:S(2)}) copy-start(bf16[1,192,1536]{2,1,0:T(8,128)(2,1)} %param.25) | copy-start | bytes 1769476
  19.7 8.1 %copy-start.1 = (bf16[1,192,1536]{2,1,0:T(8,128)(2,1)S(1)}, bf16[1,192,1536]{2,1,0:T(8,128)(2,1)}, u32[]{:S(2)}) copy-start(bf16[1,192,1536]{2,1,0:T(8,128)(2,1)} %param.26) | copy-start | bytes 1769476
  19.7 8.1 %copy-start.2 = (bf16[1,192,1536]{2,1,0:T(8,128)(2,1)S(1)}, bf16[1,192,1536]{2,1,0:T(8,128)(2,1)}, u32[]{:S(2)}) copy-start(bf16[1,192,1536]{2,1,0:T(8,128)(2,1)} %param.24) | copy-start | bytes 1769476
  23.6 13.2 %all-to-all-start.1 = ((bf16[16,72,128]{2,1,0:T(8,128)(2,1)}), bf16[16,72,128]{2,1,0:T(8,128)(2,1)S(1)}, u32[]{:S(2)}, u32[]{:S(2)}) async-start(bf16[16,72,128]{2,1,0:T(8,128)(2,1)} %bitcast.3), calls=%async_computation.1 | async-start | bytes 589824 | tf_op jit(solution)/shard_map/all_to_all | solution.py:587
  27.8 9.0 %copy-start.3 = (bf16[1,192,1536]{2,1,0:T(8,128)(2,1)S(1)}, bf16[1,192,1536]{2,1,0:T(8,128)(2,1)}, u32[]{:S(2)}) copy-start(bf16[1,192,1536]{2,1,0:T(8,128)(2,1)} %param.27) | copy-start | bytes 1769476
  27.8 9.0 %copy-start.5 = (f32[3072]{0:T(1024)S(1)}, f32[3072]{0:T(1024)}, u32[]{:S(2)}) copy-start(f32[3072]{0:T(1024)} %param.22) | copy-start | bytes 36868
  27.9 8.9 %copy-start.6 = (f32[128]{0:T(128)S(1)}, f32[128]{0:T(128)}, u32[]{:S(2)}) copy-start(f32[128]{0:T(128)} %param.23) | copy-start | bytes 1540
  36.8 13.5 %copy-start.8 = (s32[256]{0:T(256)S(1)}, s32[256]{0:T(256)}, u32[]{:S(2)}) copy-start(s32[256]{0:T(256)} %param.19) | copy-start | bytes 3076
  50.3 1.3 %collective-permute-start.2 = (bf16[16,32,128]{2,1,0:T(8,128)(2,1)S(1)}, bf16[16,32,128]{2,1,0:T(8,128)(2,1)S(1)}, u32[]{:S(2)}, u32[]{:S(2)}) collective-permute-start(bf16[16,32,128]{2,1,0:T(8,128)(2,1)S(1)} %all_to_all.15.refs_3_), channel_id=1, source_target_pairs={{0,1},{1,0},{2,3},{3,2},{4,5},{5,4},{6,7},{7,6},{8,9},{9,8},{10,11... | collective-permute-start | bytes 393224 | tf_op jit(solution)/shard_map/ppermute | solution.py:615

commit v7 on v6

--- a/solution.py
+++ b/solution.py
@@ -192,7 +192,7 @@
 def pack_body(sizes, width, slots, conc_dev, ins, outs, scratch):
     n_dp, n_chip, n_core = sizes
     ids, times, tokens = ins
-    (out,), (held, chosen, flat) = outs, scratch
+    (out,), (held, flat) = outs, scratch
     tok_len = tokens.shape[0]
     need, rows = packet_rows(slots, n_core, width)
     pieces = width // LANES
@@ -205,21 +205,22 @@
         label = jnp.where(lane == i, x.astype(F32), label)
     core = lax.axis_index("core")
     owner = owner_of(ids[0], n_dp, conc_dev)
-    for d in range(n_dp):
-        token = first_token(lax.rem(d + n_dp - owner, n_dp), slots)
-        for i in range(slots):
-            chosen[i : i + 1, :] = held[pl.ds(jnp.minimum(token + i, tok_len - 1), 1), :]
+    token = 0
+    for step in range(n_dp):
+        d = lax.rem(owner + step, n_dp)
+        count = min(slots - special_at(step), tok_len - token)
         for chip in range(n_chip):
-            base = (d * n_chip + chip) * rows
-            flat[base + need - 1 : base + need, :] = label
-            for i in range(slots):
+            to = d * n_chip + chip
+            flat[to, need - 1 : need, :] = label
+            for i in range(count):
                 for p in range(n_core):
                     at = (chip * n_core + (core ^ p)) * width
                     for k in range(pieces):
-                        r = base + (i * n_core + p) * pieces + k
+                        r = (i * n_core + p) * pieces + k
                         lanes = pl.ds(pl.multiple_of(at + k * LANES, LANES), LANES)
-                        flat[r : r + 1, :] = chosen[i : i + 1, lanes]
-    out[...] = flat[...].astype(BF16)
+                        flat[to, r : r + 1, :] = held[token + i : token + i + 1, lanes]
+        token += count
+    out[...] = flat[...].reshape(out.shape).astype(BF16)
 
 
 def hat_body(ins, outs, scratch):
@@ -239,8 +240,7 @@
             [((n_all * rows, LANES), BF16)],
             [
                 pltpu.VMEM(tokens.shape, F32),
-                pltpu.VMEM((-(-slots // 8) * 8, model_width), F32),
-                pltpu.VMEM((n_all * rows, LANES), F32),
+                pltpu.VMEM((n_all, rows, LANES), F32),
             ],
         )
         return out.reshape(n_all, rows, LANES)

time: 55.6 us -> 55.5 us (level)
  no operation moved by 1% of the time
where the time goes in v7:
time: 55.5 us; the launch traced here: 55.1 us
  Pallas kernels  17.1 us (31%)
  starting transfers between devices  12.4 us (22%)
  waiting for transfers between devices  12.2 us (22%)
  blocking collectives  11 us (20%)
  between operations  2.13 us (4%)
    pallas_call x6, Pallas kernels, call(): pl.pallas_call(kernel, in_specs=[pl.BlockSpec(memory_space=spaces.get(o[0...  17.1 us
    all_to_all x2, starting transfers between devices, exchange(): return lax.all_to_all(x, axes, 0, 0, tiled=True)  11.9 us
    all_to_all x2, waiting for transfers between devices, exchange(): return lax.all_to_all(x, axes, 0, 0, tiled=True)  11.1 us
    all_to_all x1, blocking collectives, exchange(): return lax.all_to_all(x, axes, 0, 0, tiled=True)  11 us
    ppermute x3, waiting for transfers between devices, by_core(): lax.ppermute(x, 'core', [(i, i ^ s) for i in range(n_core)])  1.17 us
  transfers between devices with their start and end apart: 5, of which 3 were waited for; matrix products, arithmetic and copies ran while one was open for 0% of the time, Pallas kernels for 13%

profile of v7, /device:TPU:0, one launch (start us, length us, event | category | flops | bytes accessed | tf_op | source)
XLA Modules:
  0.0 55.1 jit_solution(17278166142926954979)
XLA Ops:
  0.0 0.5 collective-permute-start.1
  0.5 0.1 collective-permute-start
  1.8 0.0 copy-start.4
  1.8 1.8 %shard_map.137 = bf16[384,128]{1,0:T(8,128)(2,1)} custom-call(s32[1]{0:T(128)S(6)} %copy.16.refs_0_, s32[1]{0:T(128)S(6)} %copy.18.refs_1_.refs_2_, bf16[8,3072]{1,0:T(8,128)(2,1)} %bitcast.20), custom_call_target="tpu_custom_call" | custom-call | flops 2000000000 | bytes 1024 | tf_op jit(solution)/shard_map/pallas_call | solution.py:139
  3.6 8.3 %all-to-all-start = ((bf16[16,24,128]{2,1,0:T(8,128)(2,1)}), bf16[16,24,128]{2,1,0:T(8,128)(2,1)S(1)}, u32[]{:S(2)}, u32[]{:S(2)}) async-start(bf16[16,24,128]{2,1,0:T(8,128)(2,1)} %bitcast.18), calls=%async_computation | async-start | bytes 196608 | tf_op jit(solution)/shard_map/all_to_all | solution.py:587
  12.0 0.0 collective-permute-done.refs_2_
  12.0 0.0 copy-done.4
  12.0 2.3 %shard_map.136 = (bf16[896,384]{1,0:T(8,128)(2,1)S(1)}, f32[256,1]{1,0:T(8,128)S(1)}) custom-call(bf16[256,3072]{1,0:T(8,128)(2,1)} %refs_0_.3, bf16[64,2,384]{2,1,0:T(2,128)(2,1)S(1)} %copy-done.4, bf16[64,2,384]{2,1,0:T(2,128)(2,1)S(1)} %collective-permute-done.refs_2_), custom_call_target="tpu_custom_call" | custom-call | flops 2000000000 | bytes 1024 | tf_op jit(solution)/shard_map/pallas_call | solution.py:139
  14.3 0.0 copy-start.7
  14.3 5.3 %all-to-all-done.refs_3_ = bf16[16,24,128]{2,1,0:T(8,128)(2,1)S(1)} async-done(((bf16[16,24,128]{2,1,0:T(8,128)(2,1)}), bf16[16,24,128]{2,1,0:T(8,128)(2,1)S(1)}, u32[]{:S(2)}, u32[]{:S(2)}) %all-to-all-start) | async-done | bytes 98336 | tf_op jit(solution)/shard_map/all_to_all | solution.py:587
  19.6 0.0 collective-permute-done.1.refs_2_
  19.6 0.0 copy-start
  19.6 0.0 copy-start.1
  19.6 0.0 copy-start.2
  19.6 3.8 %shard_map.138 = bf16[1152,128]{1,0:T(8,128)(2,1)} custom-call(bf16[896,384]{1,0:T(8,128)(2,1)S(1)} %get-tuple-element.7.refs_0_, bf16[384,3072]{1,0:T(8,128)(2,1)} %refs_2_.2, bf16[384,3072]{1,0:T(8,128)(2,1)} %collective-permute-done.1.refs_2_, bf16[16,24,128]{2,1,0:T(8,128)(2,1)S(1)} %all-to-all-done.refs_3_), custom_call_target="tpu_custom_call" | custom-call | flops 2000000000 | bytes 1024 | tf_op jit(solution)/shard_map/pallas_call | solution.py:139
  23.5 0.0 copy-done.7
  23.5 3.5 %all-to-all-start.1 = ((bf16[16,72,128]{2,1,0:T(8,128)(2,1)}), bf16[16,72,128]{2,1,0:T(8,128)(2,1)S(1)}, u32[]{:S(2)}, u32[]{:S(2)}) async-start(bf16[16,72,128]{2,1,0:T(8,128)(2,1)} %bitcast.3), calls=%async_computation.1 | async-start | bytes 589824 | tf_op jit(solution)/shard_map/all_to_all | solution.py:587
  27.7 0.0 copy-done
  27.7 0.0 copy-done.1
  27.7 0.0 copy-done.2
  27.7 0.0 copy-start.3
  27.7 0.0 copy-start.5
  27.8 0.0 copy-start.6
  27.8 3.2 %shard_map.139.refs_6_ = f32[12,136,192]{2,1,0:T(8,128)} custom-call(bf16[192,1536]{1,0:T(8,128)(2,1)S(1)} %bitcast.12, bf16[192,1536]{1,0:T(8,128)(2,1)S(1)} %bitcast.10, bf16[192,1536]{1,0:T(8,128)(2,1)S(1)} %bitcast.11, bf16[192,1536]{1,0:T(8,128)(2,1)} %bitcast.14), custom_call_target="tpu_custom_call" | custom-call | flops 2000000000 | bytes 1024 | tf_op jit(solution)/shard_map/pallas_call | solution.py:139
  30.9 5.7 %all-to-all-done.1.refs_3_ = bf16[16,72,128]{2,1,0:T(8,128)(2,1)S(1)} async-done(((bf16[16,72,128]{2,1,0:T(8,128)(2,1)}), bf16[16,72,128]{2,1,0:T(8,128)(2,1)S(1)}, u32[]{:S(2)}, u32[]{:S(2)}) %all-to-all-start.1) | async-done | bytes 294944 | tf_op jit(solution)/shard_map/all_to_all | solution.py:587
  36.7 0.0 copy-done.3
  36.7 0.0 copy-done.5
  36.7 0.0 copy-done.6
  36.7 0.0 copy-start.8
  36.7 2.5 %shard_map.140 = bf16[16,32,128]{2,1,0:T(8,128)(2,1)S(1)} custom-call(s32[1]{0:T(128)S(6)} %copy.16.refs_0_, s32[1]{0:T(128)S(6)} %copy.17.refs_1_, s32[1]{0:T(128)S(6)} %copy.18.refs_1_.refs_2_, bf16[16,72,128]{2,1,0:T(8,128)(2,1)S(1)} %all-to-all-done.1.refs_3_, f32[24,128]{1,0:T(8,128)S(1)} %bitcast.16, f32[1,128]{1,0:T(1,128)S(1)} %bitcast.17, ...), custom_call_target="tpu_custom_call" | custom-call | flops 2000000000 | bytes 1024 | tf_op jit(solution)/shard_map/pallas_call | solution.py:139
  39.2 11.0 %all_to_all.15.refs_3_ = bf16[16,32,128]{2,1,0:T(8,128)(2,1)S(1)} all-to-all(bf16[16,32,128]{2,1,0:T(8,128)(2,1)S(1)} %shard_map.140), channel_id=1, replica_groups=mesh['dp'=4,'chip'=4,'core'=2] {'dp','chip'}, dimensions={0} | all-to-all | bytes 262144 | tf_op jit(solution)/shard_map/all_to_all | solution.py:587
  50.2 0.0 collective-permute-start.2
  50.2 0.0 copy-done.8
  50.2 0.1 copy.15
  50.4 1.2 %collective-permute-done.2.refs_4_ = bf16[16,32,128]{2,1,0:T(8,128)(2,1)S(1)} collective-permute-done((bf16[16,32,128]{2,1,0:T(8,128)(2,1)S(1)}, bf16[16,32,128]{2,1,0:T(8,128)(2,1)S(1)}, u32[]{:S(2)}, u32[]{:S(2)}) %collective-permute-start.2) | collective-permute-done | bytes 131104 | tf_op jit(solution)/shard_map/ppermute | solution.py:615
  51.5 3.5 %shard_map.141 = f32[256,384]{1,0:T(8,128)} custom-call(bf16[896,384]{1,0:T(8,128)(2,1)} %copy-done.7, f32[256,1]{1,0:T(8,128)S(1)} %div.3.refs_1_, bf16[384,3072]{1,0:T(8,128)(2,1)} %refs_2_.2, bf16[16,32,128]{2,1,0:T(8,128)(2,1)S(1)} %all_to_all.15.refs_3_, bf16[16,32,128]{2,1,0:T(8,128)(2,1)S(1)} %collective-permute-done.2.refs_4_), custom_call_target="tpu_custom_call" | custom-call | flops 2000000000 | bytes 1024 | tf_op jit(solution)/shard_map/pallas_call | solution.py:139
  (2 shorter events, 0.0 us)
Async XLA Ops:
  0.0 19.6 %collective-permute-start.1 = (bf16[384,3072]{1,0:T(8,128)(2,1)}, bf16[384,3072]{1,0:T(8,128)(2,1)}, u32[]{:S(2)}, u32[]{:S(2)}) collective-permute-start(bf16[384,3072]{1,0:T(8,128)(2,1)} %refs_2_.2), channel_id=1, source_target_pairs={{0,1},{1,0},{2,3},{3,2},{4,5},{5,4},{6,7},{7,6},{8,9},{9,8},{10,11... | collective-permute-start | bytes 7077896 | tf_op jit(solution)/shard_map/ppermute | solution.py:615
  0.5 11.5 %collective-permute-start = (bf16[64,2,384]{2,1,0:T(2,128)(2,1)}, bf16[64,2,384]{2,1,0:T(2,128)(2,1)S(1)}, u32[]{:S(2)}, u32[]{:S(2)}) collective-permute-start(bf16[64,2,384]{2,1,0:T(2,128)(2,1)} %refs_1_.4), channel_id=1, source_target_pairs={{0,1},{1,0},{2,3},{3,2},{4,5},{5,4},{6,7},{7,6},{8,9},{9,8},{10,11... | collective-permute-start | bytes 294920 | tf_op jit(solution)/shard_map/ppermute | solution.py:615
  1.8 10.2 %copy-start.4 = (bf16[64,2,384]{2,1,0:T(2,128)(2,1)S(1)}, bf16[64,2,384]{2,1,0:T(2,128)(2,1)}, u32[]{:S(2)}) copy-start(bf16[64,2,384]{2,1,0:T(2,128)(2,1)} %refs_1_.4) | copy-start | bytes 294916
  3.6 16.0 %all-to-all-start = ((bf16[16,24,128]{2,1,0:T(8,128)(2,1)}), bf16[16,24,128]{2,1,0:T(8,128)(2,1)S(1)}, u32[]{:S(2)}, u32[]{:S(2)}) async-start(bf16[16,24,128]{2,1,0:T(8,128)(2,1)} %bitcast.18), calls=%async_computation | async-start | bytes 196608 | tf_op jit(solution)/shard_map/all_to_all | solution.py:587
  14.3 9.2 %copy-start.7 = (bf16[896,384]{1,0:T(8,128)(2,1)}, bf16[896,384]{1,0:T(8,128)(2,1)S(1)}, u32[]{:S(2)}) copy-start(bf16[896,384]{1,0:T(8,128)(2,1)S(1)} %get-tuple-element.7.refs_0_) | copy-start | bytes 2064388
  19.6 8.1 %copy-start = (bf16[1,192,1536]{2,1,0:T(8,128)(2,1)S(1)}, bf16[1,192,1536]{2,1,0:T(8,128)(2,1)}, u32[]{:S(2)}) copy-start(bf16[1,192,1536]{2,1,0:T(8,128)(2,1)} %param.25) | copy-start | bytes 1769476
  19.6 8.1 %copy-start.1 = (bf16[1,192,1536]{2,1,0:T(8,128)(2,1)S(1)}, bf16[1,192,1536]{2,1,0:T(8,128)(2,1)}, u32[]{:S(2)}) copy-start(bf16[1,192,1536]{2,1,0:T(8,128)(2,1)} %param.26) | copy-start | bytes 1769476
  19.6 8.1 %copy-start.2 = (bf16[1,192,1536]{2,1,0:T(8,128)(2,1)S(1)}, bf16[1,192,1536]{2,1,0:T(8,128)(2,1)}, u32[]{:S(2)}) copy-start(bf16[1,192,1536]{2,1,0:T(8,128)(2,1)} %param.24) | copy-start | bytes 1769476
  23.5 13.2 %all-to-all-start.1 = ((bf16[16,72,128]{2,1,0:T(8,128)(2,1)}), bf16[16,72,128]{2,1,0:T(8,128)(2,1)S(1)}, u32[]{:S(2)}, u32[]{:S(2)}) async-start(bf16[16,72,128]{2,1,0:T(8,128)(2,1)} %bitcast.3), calls=%async_computation.1 | async-start | bytes 589824 | tf_op jit(solution)/shard_map/all_to_all | solution.py:587
  27.7 9.0 %copy-start.3 = (bf16[1,192,1536]{2,1,0:T(8,128)(2,1)S(1)}, bf16[1,192,1536]{2,1,0:T(8,128)(2,1)}, u32[]{:S(2)}) copy-start(bf16[1,192,1536]{2,1,0:T(8,128)(2,1)} %param.27) | copy-start | bytes 1769476
  27.7 9.0 %copy-start.5 = (f32[3072]{0:T(1024)S(1)}, f32[3072]{0:T(1024)}, u32[]{:S(2)}) copy-start(f32[3072]{0:T(1024)} %param.22) | copy-start | bytes 36868
  27.8 8.9 %copy-start.6 = (f32[128]{0:T(128)S(1)}, f32[128]{0:T(128)}, u32[]{:S(2)}) copy-start(f32[128]{0:T(128)} %param.23) | copy-start | bytes 1540
  36.7 13.5 %copy-start.8 = (s32[256]{0:T(256)S(1)}, s32[256]{0:T(256)}, u32[]{:S(2)}) copy-start(s32[256]{0:T(256)} %param.19) | copy-start | bytes 3076
  50.2 1.3 %collective-permute-start.2 = (bf16[16,32,128]{2,1,0:T(8,128)(2,1)S(1)}, bf16[16,32,128]{2,1,0:T(8,128)(2,1)S(1)}, u32[]{:S(2)}, u32[]{:S(2)}) collective-permute-start(bf16[16,32,128]{2,1,0:T(8,128)(2,1)S(1)} %all_to_all.15.refs_3_), channel_id=1, source_target_pairs={{0,1},{1,0},{2,3},{3,2},{4,5},{5,4},{6,7},{7,6},{8,9},{9,8},{10,11... | collective-permute-start | bytes 393224 | tf_op jit(solution)/shard_map/ppermute | solution.py:615
